TPU v7x, 32 devices: a whole 2x2x4 slice. The times are simulated.
32 devices in a mesh: rep: 4 (over z), grp: 8 (over y, x, core).
Axes of the slice: x: 2, y: 2, z: 4, core: 2. Of those that a mesh axis runs over, the one named last changes fastest.
Arguments:
- tokens: bfloat16 [4, 192, 32, 1024], P(None, None, ('rep', 'grp')), may hold values from -6 to 6
- cotangent: bfloat16 [4, 192, 32, 1024], P(None, None, ('rep', 'grp')), may hold values from -6 to 6
- seq_lengths: int32 [4, 64], replicated, may hold values from 1 to 128, as said below
- w_qkv: bfloat16 [1024, 3072], P('grp'), may hold values from -0.1875 to 0.1875
- w_out: bfloat16 [1024, 1024], P('grp'), may hold values from -1.5 to 1.5
- w_in: bfloat16 [1024, 5248], P('grp'), may hold values from -0.1875 to 0.1875
- w_down: bfloat16 [2624, 1024], P('grp'), may hold values from -0.125 to 0.125
- attn_gain: bfloat16 [1024], P('grp'), may hold values from 0.099609375 to 1.8984375
- mlp_gain: bfloat16 [1024], P('grp'), may hold values from 0.099609375 to 1.8984375
Outputs:
- layer_out: bfloat16 [4, 192, 32, 1024], P(None, None, ('rep', 'grp'))
- grad_tokens: bfloat16 [4, 192, 32, 1024], P(None, None, ('rep', 'grp'))
- grad_attn_gain: float32 [1024], P('grp')
- grad_mlp_gain: float32 [1024], P('grp')
- grad_w_qkv: float32 [1024, 3072], P('grp')
- grad_w_out: float32 [1024, 1024], P('grp')
- grad_w_in: float32 [1024, 5248], P('grp')
- grad_w_down: float32 [2624, 1024], P('grp')
Inputs may be any that keep to these rules, and one draw needn't show every extreme that they name: `seq_lengths`: the lengths of one micro-batch sum to 192 times the number of devices; the 2 sequences s of one device (s div 2 the same), each padded to whole blocks of 128 tokens, fill exactly 2 blocks; in every micro-batch the longest sequence fills exactly 1 whole block. Hence the tokens of one micro-batch that go from one device to another number at most 256 / (number of devices), and in every micro-batch some device receives exactly that many from every device.
All inputs are finite; a program needn't handle non-finite values.
Results may differ from a plain program's by a relative error of at most 0.02.
Values may be sent and summed in bfloat16 or wider, within the bound.
A program may use at most 576 MiB of HBM per device.

v0:
```python
import math

import jax
import jax.numpy as jnp
from jax import lax
from jax.sharding import PartitionSpec as P

D = 1024
HEADS = 16
HD = 64
FF = 2624
BLK = 128
MICRO = 4
SEQ_DEV = 2
CAP = 256
TOK_DEV = 192


EPS = 1e-05
THETA = 160000.0
NEG = -1e30
ROOT_TWO = math.sqrt(2.0)
ROOT_TWO_PI = math.sqrt(2.0 * math.pi)


def feature_norm(values, gain):
    center = values - jnp.mean(values, axis=-1, keepdims=True)
    inverse = lax.rsqrt(jnp.mean(center * center, axis=-1, keepdims=True) + EPS)
    normal = center * inverse
    return (normal * gain, normal, inverse)


def norm_back(grad_normed, normal, inverse):
    centred = grad_normed - jnp.mean(grad_normed, axis=-1, keepdims=True)
    return inverse * (centred - normal * jnp.mean(grad_normed * normal, axis=-1, keepdims=True))


def rotary_tables(position):
    half_width = HD // 2
    frequency = THETA ** (-2.0 * jnp.arange(half_width, dtype=jnp.float32) / HD)
    angles = position.astype(jnp.float32)[:, None] * frequency[None, :]
    cosine = jnp.concatenate([jnp.cos(angles), jnp.cos(angles)], axis=1)
    sine = jnp.concatenate([jnp.sin(angles), jnp.sin(angles)], axis=1)
    return (cosine[:, None, :], sine[:, None, :])


def rotate(values, cosine, sine):
    half_width = HD // 2
    turned = jnp.concatenate([-values[..., half_width:], values[..., :half_width]], axis=-1)
    return values * cosine + turned * sine


def rotate_back(grad_rows, cosine, sine):
    half_width = HD // 2
    scaled = grad_rows * sine
    turned = jnp.concatenate([scaled[..., half_width:], -scaled[..., :half_width]], axis=-1)
    return grad_rows * cosine + turned


def source_plan(lengths_row, device, devices):
    seq_ends = jnp.cumsum(lengths_row)
    row_ids = jnp.arange(TOK_DEV, dtype=jnp.int32)
    given_pos = row_ids * devices + device
    sequence = jnp.sum((seq_ends[None, :] <= given_pos[:, None]).astype(jnp.int32), axis=1)
    target = sequence // SEQ_DEV
    earlier = (target[:, None] == target[None, :]) & (row_ids[None, :] < row_ids[:, None])
    return (target, jnp.sum(earlier.astype(jnp.int32), axis=1))


def dest_plan(lengths_row, device, devices):
    seq_starts = jnp.cumsum(lengths_row) - lengths_row
    row_ids = jnp.arange(CAP, dtype=jnp.int32)
    own_slots = device * SEQ_DEV + jnp.arange(SEQ_DEV, dtype=jnp.int32)
    own_blocks = (lengths_row[own_slots] + (BLK - 1)) // BLK
    own_first = (jnp.cumsum(own_blocks) - own_blocks) * BLK
    slot_rank = jnp.sum((own_first[None, :] <= row_ids[:, None]).astype(jnp.int32), axis=1) - 1
    in_sequence = row_ids - own_first[slot_rank]
    sequence = own_slots[slot_rank]
    is_valid = in_sequence < lengths_row[sequence]
    given_pos = seq_starts[sequence] + in_sequence
    source = given_pos % devices
    before = (
        (source[:, None] == source[None, :])
        & is_valid[None, :]
        & (given_pos[None, :] < given_pos[:, None])
    )
    pair_rank = jnp.sum(before.astype(jnp.int32), axis=1)
    segment = jnp.where(is_valid, slot_rank, -1)
    position = jnp.where(is_valid, in_sequence, 0)
    return (is_valid, source, pair_rank, segment, position)


def contract_rows(left, right):
    return lax.dot_general(
        left, right, (((0,), (0,)), ((), ())), preferred_element_type=jnp.float32
    )


def head_blocks(values, groups):
    return jnp.moveaxis(values.reshape(values.shape[0], groups, -1, HD), 1, 0)


def head_join(values):
    return jnp.moveaxis(values, 0, 1).reshape(values.shape[1], -1)


def layer_pass(
    hidden, grad_top, segment, position, full_qkv, full_out, full_in, full_down, gain_one, gain_two
):
    row_total = hidden.shape[0]
    groups = HEADS // 2
    score_scale = HD ** (-0.5)
    same_seq = segment[:, None] == segment[None, :]
    cosine, sine = rotary_tables(position)
    normed_one, normal_one, inverse_one = feature_norm(hidden, gain_one)
    act_a = normed_one.astype(jnp.bfloat16)
    packed = jnp.dot(act_a, full_qkv, preferred_element_type=jnp.float32)
    queries = rotate(packed[:, :D].reshape(row_total, HEADS, HD), cosine, sine).astype(jnp.bfloat16)
    keys_rot = rotate(packed[:, D : 2 * D].reshape(row_total, HEADS, HD), cosine, sine).astype(
        jnp.bfloat16
    )
    values_low = packed[:, 2 * D :].reshape(row_total, HEADS, HD).astype(jnp.bfloat16)
    query_blocks = head_blocks(queries, groups)
    key_blocks = head_blocks(keys_rot, groups)
    value_blocks = head_blocks(values_low, groups)

    def block_scores(query_part, key_part):
        scores = (
            jnp.einsum("qhd,khd->hqk", query_part, key_part, preferred_element_type=jnp.float32)
            * score_scale
        )
        return jnp.where(same_seq[None], scores, NEG)

    def attend(operands):
        query_part, key_part, value_part = operands
        scores = block_scores(query_part, key_part)
        top_score = jnp.max(scores, axis=-1, keepdims=True)
        expo = jnp.exp(scores - top_score)
        summed = jnp.sum(expo, axis=-1, keepdims=True)
        weights_low = (expo / summed).astype(jnp.bfloat16)
        context = jnp.einsum(
            "hqk,khd->qhd", weights_low, value_part, preferred_element_type=jnp.float32
        )
        return (context, (top_score + jnp.log(summed))[..., 0])

    contexts, log_total = lax.map(attend, (query_blocks, key_blocks, value_blocks))
    attn_o = head_join(contexts).astype(jnp.bfloat16)
    middle = hidden + jnp.dot(attn_o, full_out, preferred_element_type=jnp.float32)
    normed_two, normal_two, inverse_two = feature_norm(middle, gain_two)
    act_b = normed_two.astype(jnp.bfloat16)
    gate_up = jnp.dot(act_b, full_in, preferred_element_type=jnp.float32)
    gelu_in = gate_up[:, :FF]
    linear_in = gate_up[:, FF:]
    gelu_out = jax.nn.gelu(gelu_in, approximate=False)
    act_c = (gelu_out * linear_in).astype(jnp.bfloat16)
    layer_rows = (middle + jnp.dot(act_c, full_down, preferred_element_type=jnp.float32)).astype(
        jnp.bfloat16
    )
    grad_m = grad_top.astype(jnp.bfloat16)
    grad_c = jnp.dot(grad_m, full_down.T, preferred_element_type=jnp.float32)
    slope = (
        0.5 * (1.0 + jax.scipy.special.erf(gelu_in / ROOT_TWO))
        + gelu_in * jnp.exp(-0.5 * gelu_in * gelu_in) / ROOT_TWO_PI
    )
    grad_gu = jnp.concatenate([grad_c * linear_in * slope, grad_c * gelu_out], axis=1).astype(
        jnp.bfloat16
    )
    grad_b = jnp.dot(grad_gu, full_in.T, preferred_element_type=jnp.float32)
    gain_two_grad = jnp.sum(grad_b * normal_two, axis=0)
    grad_mid = grad_top + norm_back(grad_b * gain_two, normal_two, inverse_two)
    grad_branch = grad_mid.astype(jnp.bfloat16)
    grad_o = jnp.dot(grad_branch, full_out.T, preferred_element_type=jnp.float32).astype(
        jnp.bfloat16
    )

    def attend_back(operands):
        query_part, key_part, value_part, grad_part, log_part = operands
        softmax_w = jnp.exp(block_scores(query_part, key_part) - log_part[..., None])
        grad_v = jnp.einsum(
            "hqk,qhd->khd",
            softmax_w.astype(jnp.bfloat16),
            grad_part,
            preferred_element_type=jnp.float32,
        )
        grad_p = jnp.einsum(
            "qhd,khd->hqk", grad_part, value_part, preferred_element_type=jnp.float32
        )
        grad_s = (
            softmax_w * (grad_p - jnp.sum(softmax_w * grad_p, axis=-1, keepdims=True))
        ).astype(jnp.bfloat16)
        grad_q = (
            jnp.einsum("hqk,khd->qhd", grad_s, key_part, preferred_element_type=jnp.float32)
            * score_scale
        )
        grad_k = (
            jnp.einsum("hqk,qhd->khd", grad_s, query_part, preferred_element_type=jnp.float32)
            * score_scale
        )
        return (grad_q, grad_k, grad_v)

    grad_o_blocks = head_blocks(grad_o.reshape(row_total, HEADS, HD), groups)
    grad_qs, grad_ks, grad_vs = lax.map(
        attend_back, (query_blocks, key_blocks, value_blocks, grad_o_blocks, log_total)
    )
    grad_q_rows = rotate_back(
        head_join(grad_qs).reshape(row_total, HEADS, HD), cosine, sine
    ).reshape(row_total, D)
    grad_k_rows = rotate_back(
        head_join(grad_ks).reshape(row_total, HEADS, HD), cosine, sine
    ).reshape(row_total, D)
    grad_qkv = jnp.concatenate([grad_q_rows, grad_k_rows, head_join(grad_vs)], axis=1).astype(
        jnp.bfloat16
    )
    grad_a = jnp.dot(grad_qkv, full_qkv.T, preferred_element_type=jnp.float32)
    gain_one_grad = jnp.sum(grad_a * normal_one, axis=0)
    grad_in = grad_mid + norm_back(grad_a * gain_one, normal_one, inverse_one)
    kept_items = (
        act_a,
        grad_qkv,
        attn_o,
        grad_branch,
        act_b,
        grad_gu,
        act_c,
        grad_m,
        gain_one_grad,
        gain_two_grad,
    )
    return (layer_rows, grad_in.astype(jnp.bfloat16), kept_items)


def reduce_grads(kept_list):
    summed = None
    for row_kept_items in kept_list:
        act_a, grad_qkv, attn_o, grad_branch, act_b, grad_gu = row_kept_items[:6]
        pieces = [
            contract_rows(act_a, grad_qkv),
            contract_rows(attn_o, grad_branch),
            contract_rows(act_b, grad_gu),
        ]
        joined = jnp.concatenate(pieces, axis=1)
        summed = joined if summed is None else summed + joined
    row_owned = lax.psum_scatter(
        summed.astype(jnp.bfloat16), "grp", scatter_dimension=0, tiled=True
    ).astype(jnp.float32)
    down_term = None
    gain_one_sum = None
    gain_two_sum = None
    for kept_items in kept_list:
        piece_down = contract_rows(kept_items[6], kept_items[7])
        down_term = piece_down if down_term is None else down_term + piece_down
        gain_one_sum = kept_items[8] if gain_one_sum is None else gain_one_sum + kept_items[8]
        gain_two_sum = kept_items[9] if gain_two_sum is None else gain_two_sum + kept_items[9]
    tail_owned = (
        lax.psum_scatter(
            down_term.astype(jnp.bfloat16), "grp", scatter_dimension=0, tiled=True
        ).astype(jnp.float32),
        lax.psum_scatter(
            gain_one_sum.astype(jnp.bfloat16), "grp", scatter_dimension=0, tiled=True
        ).astype(jnp.float32),
        lax.psum_scatter(
            gain_two_sum.astype(jnp.bfloat16), "grp", scatter_dimension=0, tiled=True
        ).astype(jnp.float32),
    )
    return (row_owned, tail_owned[0], tail_owned[1], tail_owned[2])


def body(tokens, cotangent, seq_lengths, w_qkv, w_out, w_in, w_down, attn_gain, mlp_gain):
    group_size = lax.axis_size("grp")
    replica_count = lax.axis_size("rep")
    devices = replica_count * group_size
    device = lax.axis_index("rep") * group_size + lax.axis_index("grp")
    pair_cap = CAP // devices
    gathered = (
        lax.all_gather(w_qkv, "grp", axis=0, tiled=True),
        lax.all_gather(w_out, "grp", axis=0, tiled=True),
        lax.all_gather(w_in, "grp", axis=0, tiled=True),
        lax.all_gather(w_down, "grp", axis=0, tiled=True),
        lax.all_gather(attn_gain, "grp", axis=0, tiled=True),
        lax.all_gather(mlp_gain, "grp", axis=0, tiled=True),
    )
    full_qkv, full_out, full_in, full_down = (gathered[0], gathered[1], gathered[2], gathered[3])
    gain_one = gathered[4].astype(jnp.float32)
    gain_two = gathered[5].astype(jnp.float32)
    kept_list = []
    owned = None
    layer_parts = []
    grad_parts = []
    for micro_step in range(MICRO):
        target, send_rank = source_plan(seq_lengths[micro_step], device, devices)
        is_valid, source, pair_rank, segment, position = dest_plan(
            seq_lengths[micro_step], device, devices
        )
        outgoing = jnp.zeros((2, devices, pair_cap, D), jnp.bfloat16)
        outgoing = outgoing.at[0, target, send_rank].set(tokens[micro_step, :, 0])
        outgoing = outgoing.at[1, target, send_rank].set(cotangent[micro_step, :, 0])
        arrived = lax.all_to_all(outgoing, ("rep", "grp"), split_axis=1, concat_axis=1, tiled=True)
        safe_source = jnp.where(is_valid, source, 0)
        safe_rank = jnp.where(is_valid, pair_rank, 0)
        picked = jnp.where(is_valid[None, :, None], arrived[:, safe_source, safe_rank], 0).astype(
            jnp.float32
        )
        layer_rows, grad_rows, kept_items = layer_pass(
            picked[0],
            picked[1],
            segment,
            position,
            full_qkv,
            full_out,
            full_in,
            full_down,
            gain_one,
            gain_two,
        )
        drop_source = jnp.where(is_valid, source, devices)
        back_rows = jnp.zeros((2, devices, pair_cap, D), jnp.bfloat16)
        back_rows = back_rows.at[0, drop_source, safe_rank].set(layer_rows, mode="drop")
        back_rows = back_rows.at[1, drop_source, safe_rank].set(grad_rows, mode="drop")
        returned = lax.all_to_all(
            back_rows, ("rep", "grp"), split_axis=1, concat_axis=1, tiled=True
        )
        layer_parts.append(returned[0, target, send_rank])
        grad_parts.append(returned[1, target, send_rank])
        kept_list.append(kept_items)
    owned = reduce_grads(kept_list)
    totals = (
        lax.psum(owned[0].astype(jnp.bfloat16), "rep").astype(jnp.float32),
        lax.psum(owned[1].astype(jnp.bfloat16), "rep").astype(jnp.float32),
        lax.psum(owned[2].astype(jnp.bfloat16), "rep").astype(jnp.float32),
        lax.psum(owned[3].astype(jnp.bfloat16), "rep").astype(jnp.float32),
    )
    row_sums = totals[0]
    grad_w_qkv = row_sums[:, : 3 * D]
    grad_w_out = row_sums[:, 3 * D : 4 * D]
    grad_w_in = row_sums[:, 4 * D :]
    layer_out = jnp.stack(layer_parts)[:, :, None, :]
    grad_tokens = jnp.stack(grad_parts)[:, :, None, :]
    return (
        layer_out,
        grad_tokens,
        totals[2],
        totals[3],
        grad_w_qkv,
        grad_w_out,
        grad_w_in,
        totals[1],
    )


def solution(mesh):
    return jax.shard_map(
        body,
        mesh=mesh,
        in_specs=(
            P(None, None, ("rep", "grp"), None),
            P(None, None, ("rep", "grp"), None),
            P(),
            P("grp", None),
            P("grp", None),
            P("grp", None),
            P("grp", None),
            P("grp"),
            P("grp"),
        ),
        out_specs=(
            P(None, None, ("rep", "grp"), None),
            P(None, None, ("rep", "grp"), None),
            P("grp"),
            P("grp"),
            P("grp", None),
            P("grp", None),
            P("grp", None),
            P("grp", None),
        ),
        check_vma=False,
    )
```

profile of v0, /device:TPU:0, one launch (start us, length us, event | category | flops | bytes accessed | tf_op | source)
XLA Modules:
  0.0 1394.6 jit_solution(13109579183545620754)
XLA Ops:
  85.8 21.0 %scatter_fusion.8 = bf16[2,32,8,1024]{3,2,1,0:T(8,128)(2,1)S(1)} fusion(bf16[2,32,8,1024]{3,2,1,0:T(8,128)(2,1)S(1)} %broadcast.2252.clone.2, s32[192]{0:T(256)S(1)} %bitcast.1024, bf16[192,1024]{1,0:T(8,128)(2,1)} %get-tuple-element.857), kind=kCustom, calls=%fused_computation.32 | custom fusion | bytes 1181952 | tf_op jit(solution)/shard_map/scatter | solution.py:295
  106.8 21.0 %scatter_fusion.9 = bf16[2,32,8,1024]{3,2,1,0:T(8,128)(2,1)S(1)} fusion(bf16[2,32,8,1024]{3,2,1,0:T(8,128)(2,1)S(1)} %scatter_fusion.8, s32[192]{0:T(256)S(1)} %bitcast.1032, bf16[192,1024]{1,0:T(8,128)(2,1)} %get-tuple-element.853), kind=kCustom, calls=%fused_computation.33 | custom fusion | bytes 1181952 | tf_op jit(solution)/shard_map/scatter | solution.py:296
  144.2 21.0 %scatter_fusion.5 = bf16[2,32,8,1024]{3,2,1,0:T(8,128)(2,1)S(1)} fusion(bf16[2,32,8,1024]{3,2,1,0:T(8,128)(2,1)S(1)} %scatter_fusion.4, s32[192]{0:T(256)S(1)} %bitcast.1033, bf16[192,1024]{1,0:T(8,128)(2,1)} %get-tuple-element.851), kind=kCustom, calls=%fused_computation.29 | custom fusion | bytes 1181952 | tf_op jit(solution)/shard_map/scatter | solution.py:296
  185.0 18.3 %all-to-all-done.4 = bf16[2,32,8,1024]{3,2,0,1:T(8,128)(2,1)S(1)} async-done(((bf16[2,32,8,1024]{3,2,0,1:T(8,128)(2,1)}), bf16[2,32,8,1024]{3,2,0,1:T(8,128)(2,1)S(1)}, u32[]{:S(2)}, u32[]{:S(2)}) %all-to-all-start.4) | async-done | bytes 1048608 | tf_op jit(solution)/shard_map/all_to_all | solution.py:297
  343.6 19.9 %while.112 = (s32[]{:T(128)}, bf16[8,256,2,64]{1,3,2,0:T(8,128)(2,1)S(1)}, f32[8,2,256]{2,1,0:T(2,128)S(1)}, bf16[8,256,2,64]{1,3,2,0:T(8,128)(2,1)}, bf16[8,256...) while((s32[]{:T(128)}, ...), condition=%wide.region_13.14_spmd.clone, body=%wide.region_10.13_spmd.clone.sunk | while | flops 34668032 | bytes 2051169 | solution.py:146
  373.0 19.9 %while.114 = (s32[]{:T(128)}, bf16[8,256,2,64]{1,3,2,0:T(8,128)(2,1)S(1)}, f32[8,2,256]{2,1,0:T(2,128)S(1)}, bf16[8,256,2,64]{1,3,2,0:T(8,128)(2,1)}, bf16[8,256...) while((s32[]{:T(128)}, ...), condition=%wide.region_38.39_spmd.clone, body=%wide.region_35.38_spmd.clone.sunk | while | flops 34668032 | bytes 2051169 | solution.py:146
  405.8 19.8 %while.118 = (s32[]{:T(128)}, bf16[8,256,2,64]{1,3,2,0:T(8,128)(2,1)S(1)}, f32[8,2,256]{2,1,0:T(2,128)S(1)}, bf16[8,256,2,64]{1,3,2,0:T(8,128)(2,1)}, bf16[8,256...) while((s32[]{:T(128)}, ...), condition=%wide.region_88.89_spmd.clone, body=%wide.region_85.88_spmd.clone.sunk | while | flops 34668032 | bytes 2051169 | solution.py:146
  440.1 24.7 %while.116 = (s32[]{:T(128)}, bf16[8,256,2,64]{1,3,2,0:T(8,128)(2,1)}, f32[8,2,256]{2,1,0:T(2,128)S(1)}, bf16[8,256,2,64]{1,3,2,0:T(8,128)(2,1)}, bf16[8,256,2,6...) while((s32[]{:T(128)}, ...), condition=%wide.region_63.64_spmd.clone, body=%wide.region_60.63_spmd.clone.sunk | while | flops 34668032 | bytes 2051169 | solution.py:146
  604.4 66.4 %while.117 = (s32[]{:T(128)}, f32[8,256,2,64]{1,3,2,0:T(8,128)}, f32[8,256,2,64]{1,3,2,0:T(8,128)}, bf16[8,256,2,64]{1,3,2,0:T(8,128)(2,1)}, bf16[8,256,2,64]{1,...) while((s32[]{:T(128)}, f32[8,256,2,64]{1,3,2,0:T(8,128)}, ...), condition=%wide.region_71.72_spmd.clone, body=%wide.region_69.71_spmd.clone.sunk | while | flops 85196288 | bytes 4931705 | solution.py:202
  678.9 66.6 %while.119 = (s32[]{:T(128)}, f32[8,256,2,64]{1,3,2,0:T(8,128)}, f32[8,256,2,64]{1,3,2,0:T(8,128)}, bf16[8,256,2,64]{1,3,2,0:T(8,128)(2,1)}, bf16[8,256,2,64]{1,...) while((s32[]{:T(128)}, f32[8,256,2,64]{1,3,2,0:T(8,128)}, ...), condition=%wide.region_96.97_spmd.clone, body=%wide.region_94.96_spmd.clone.sunk | while | flops 85196288 | bytes 4931705 | solution.py:202
  756.5 49.0 %while.113 = (s32[]{:T(128)}, f32[8,256,2,64]{1,3,2,0:T(8,128)S(1)}, f32[8,256,2,64]{1,3,2,0:T(8,128)S(1)}, bf16[8,256,2,64]{1,3,2,0:T(8,128)(2,1)}, bf16[8,256,...) while((s32[]{:T(128)}, f32[8,256,2,64]{1,3,2,0:T(8,128)S(1)}, ...), condition=%wide.region_21.22_spmd.clone, body=%wide.region_19.21_spmd.clone.sunk | while | flops 85196288 | bytes 4931705 | solution.py:202
  806.7 55.9 %while.115 = (s32[]{:T(128)}, f32[8,256,2,64]{1,3,2,0:T(8,128)S(1)}, f32[8,256,2,64]{1,3,2,0:T(8,128)S(1)}, bf16[8,256,2,64]{1,3,2,0:T(8,128)(2,1)}, bf16[8,256,...) while((s32[]{:T(128)}, f32[8,256,2,64]{1,3,2,0:T(8,128)S(1)}, ...), condition=%wide.region_46.47_spmd.clone, body=%wide.region_44.46_spmd.clone.sunk | while | flops 85196288 | bytes 4931705 | solution.py:202
  963.4 53.1 %fusion.190 = bf16[1024,9344]{1,0:T(8,128)(2,1)} fusion(f32[1024,5248]{1,0:T(8,128)} %fusion.257, f32[1024,1024]{1,0:T(8,128)} %fusion.328, f32[1024,3072]{1,0:T(8,128)} %fusion.309, f32[1024,5248]{1,0:T(8,128)} %fusion.255, f32[1024,1024]{1,0:T(8,128)} %fusion.325, f32[1024,3072]{1,0:T(8,128)} %fusion.307, f32[1024,5248]{1,0:T(8,128)} %fusion.253, ...), kind=kLoop, calls=%fused_computation.279 | loop fusion | flops 114819072 | bytes 172228608 | tf_op jit(solution)/shard_map/convert_element_type | solution.py:244
  1023.3 27.8 %scatter_fusion.10 = bf16[2,32,8,1024]{3,2,1,0:T(8,128)(2,1)S(1)} fusion(bf16[2,32,8,1024]{3,2,1,0:T(8,128)(2,1)S(1)} %broadcast.2252.clone.5, s32[256]{0:T(256)S(1)} %bitcast.1002, bf16[256,1024]{1,0:T(8,128)(2,1)} %fusion.261), kind=kCustom, calls=%fused_computation.34 | custom fusion | bytes 1575936 | tf_op jit(solution)/shard_map/scatter | solution.py:317
  1078.0 27.3 %scatter_fusion.11 = bf16[2,32,8,1024]{3,2,1,0:T(8,128)(2,1)S(1)} fusion(bf16[2,32,8,1024]{3,2,1,0:T(8,128)(2,1)S(1)} %scatter_fusion.10, s32[256]{0:T(256)S(1)} %bitcast.1001, bf16[256,1024]{1,0:T(8,128)(2,1)} %get-tuple-element.942), kind=kCustom, calls=%fused_computation.35 | custom fusion | bytes 1575936 | tf_op jit(solution)/shard_map/scatter | solution.py:318
  1115.3 27.3 %scatter_fusion.2 = bf16[2,32,8,1024]{3,2,1,0:T(8,128)(2,1)S(1)} fusion(bf16[2,32,8,1024]{3,2,1,0:T(8,128)(2,1)S(1)} %broadcast.2252.clone.7, s32[256]{0:T(256)S(1)} %bitcast.998, bf16[256,1024]{1,0:T(8,128)(2,1)} %fusion.259), kind=kCustom, calls=%fused_computation.26 | custom fusion | bytes 1575936 | tf_op jit(solution)/shard_map/scatter | solution.py:317
  1142.7 17.3 %scatter_fusion.3 = bf16[2,32,8,1024]{3,2,1,0:T(8,128)(2,1)S(1)} fusion(bf16[2,32,8,1024]{3,2,1,0:T(8,128)(2,1)S(1)} %scatter_fusion.2, s32[256]{0:T(256)S(1)} %bitcast.997, bf16[256,1024]{1,0:T(8,128)(2,1)S(1)} %copy-done.174), kind=kCustom, calls=%fused_computation.27 | custom fusion | bytes 1575936 | tf_op jit(solution)/shard_map/scatter | solution.py:318
  1172.4 27.3 %scatter_fusion.6 = bf16[2,32,8,1024]{3,2,1,0:T(8,128)(2,1)S(1)} fusion(bf16[2,32,8,1024]{3,2,1,0:T(8,128)(2,1)S(1)} %broadcast.2252.clone.6, s32[256]{0:T(256)S(1)} %bitcast.1000, bf16[256,1024]{1,0:T(8,128)(2,1)} %fusion.260), kind=kCustom, calls=%fused_computation.30 | custom fusion | bytes 1575936 | tf_op jit(solution)/shard_map/scatter | solution.py:317
  1199.7 17.2 %scatter_fusion.7 = bf16[2,32,8,1024]{3,2,1,0:T(8,128)(2,1)S(1)} fusion(bf16[2,32,8,1024]{3,2,1,0:T(8,128)(2,1)S(1)} %scatter_fusion.6, s32[256]{0:T(256)S(1)} %bitcast.999, bf16[256,1024]{1,0:T(8,128)(2,1)S(1)} %copy-done.173), kind=kCustom, calls=%fused_computation.31 | custom fusion | bytes 1575936 | tf_op jit(solution)/shard_map/scatter | solution.py:318
  1229.7 27.3 %scatter_fusion.14 = bf16[2,32,8,1024]{3,2,1,0:T(8,128)(2,1)S(1)} fusion(bf16[2,32,8,1024]{3,2,1,0:T(8,128)(2,1)S(1)} %broadcast.2252.clone, s32[256]{0:T(256)S(1)} %bitcast.996, bf16[256,1024]{1,0:T(8,128)(2,1)} %fusion.262), kind=kCustom, calls=%fused_computation.38 | custom fusion | bytes 1575936 | tf_op jit(solution)/shard_map/scatter | solution.py:317
  1257.0 17.2 %scatter_fusion.15 = bf16[2,32,8,1024]{3,2,1,0:T(8,128)(2,1)S(1)} fusion(bf16[2,32,8,1024]{3,2,1,0:T(8,128)(2,1)S(1)} %scatter_fusion.14, s32[256]{0:T(256)S(1)} %bitcast.995, bf16[256,1024]{1,0:T(8,128)(2,1)S(1)} %copy-done.124), kind=kCustom, calls=%fused_computation.39 | custom fusion | bytes 1575936 | tf_op jit(solution)/shard_map/scatter | solution.py:318
  1282.5 15.2 %all-reduce.2 = (bf16[1024]{0:T(1024)(128)(2,1)S(1)}, bf16[1024]{0:T(1024)(128)(2,1)S(1)}) all-reduce(bf16[1024]{0:T(1024)(128)(2,1)S(1)} %add_convert_fusion.6, bf16[1024]{0:T(1024)(128)(2,1)S(1)} %add_convert_fusion.5), channel_id=2, replica_groups=mesh['rep'=4,'grp'=8] {'grp'}, use_global_device_ids=true, to_apply=%region_104.105.clone | all-reduce | flops 2048 | bytes 8192
  1297.9 19.6 %all-reduce.3 = (bf16[128]{0:T(256)(128)(2,1)S(1)}, bf16[128]{0:T(256)(128)(2,1)S(1)}) all-reduce(bf16[128]{0:T(256)(128)(2,1)S(1)} %dynamic-slice.1, bf16[128]{0:T(256)(128)(2,1)S(1)} %dynamic-slice.3), channel_id=1, replica_groups=mesh['rep'=4,'grp'=8] {'rep'}, use_global_device_ids=true, to_apply=%region_105.106 | all-reduce | flops 256 | bytes 1024 | tf_op jit(solution)/shard_map/psum | solution.py:329
  1361.5 18.8 %all-reduce.7.cloned.1.call-done = (bf16[128,9344]{1,0:T(8,128)(2,1)}, bf16[328,1024]{1,0:T(8,128)(2,1)}) async-done(((bf16[128,9344]{1,0:T(8,128)(2,1)}, bf16[328,1024]{1,0:T(8,128)(2,1)}), (bf16[128,9344]{1,0:T(8,128)(2,1)}, bf16[328,1024]{1,0:T(8,128)(2,1)})) %all-reduce.7.cloned.1.call-update) | async-done | bytes 3063824 | tf_op jit(solution)/shard_map/psum | solution.py:327
  (1277 shorter events, 997.1 us)
Async XLA Ops:
  7.2 311.2 %all-gather.7.cloned.1.call-start = ((), (), s32[]{:S(2)}) async-start(), calls=%async_computation.10 | async-start | bytes 7077888 | tf_op jit(solution)/shard_map/all_gather | solution.py:275
  7.9 355.7 %all-gather.9.cloned.1.call-start = ((), (), s32[]{:S(2)}) async-start(), calls=%async_computation.11 | async-start | bytes 2359296 | tf_op jit(solution)/shard_map/all_gather | solution.py:276
  8.6 459.7 %all-gather.11.cloned.1.call-start = ((), (), s32[]{:S(2)}) async-start(), calls=%async_computation.12 | async-start | bytes 12091392 | tf_op jit(solution)/shard_map/all_gather | solution.py:277
  11.6 72.6 %copy-start.208 = (s32[192]{0:T(256)}, s32[192]{0:T(256)S(1)}, u32[]{:S(2)}) copy-start(s32[192]{0:T(256)S(1)} %get-tuple-element.620) | copy-start | bytes 2308
  46.7 124.4 %all-to-all-start.6 = ((bf16[2,32,8,1024]{3,2,0,1:T(8,128)(2,1)}), bf16[2,32,8,1024]{3,2,0,1:T(8,128)(2,1)S(1)}, u32[]{:S(2)}, u32[]{:S(2)}) async-start(bf16[2,32,8,1024]{3,2,0,1:T(8,128)(2,1)} %copy.360), calls=%async_computation.6 | async-start | bytes 2097152 | tf_op jit(solution)/shard_map/all_to_all | solution.py:297
  54.1 424.4 %all-gather.13.cloned.1.call-start = ((), (), s32[]{:S(2)}) async-start(), calls=%async_computation.13 | async-start | bytes 6045696 | tf_op jit(solution)/shard_map/all_gather | solution.py:278
  67.1 114.1 %copy-start.203 = (s32[256]{0:T(256)}, s32[256]{0:T(256)S(1)}, u32[]{:S(2)}) copy-start(s32[256]{0:T(256)S(1)} %gather_fusion.1) | copy-start | bytes 3076
  74.7 91.6 %copy-start.199 = (s32[256]{0:T(256)}, s32[256]{0:T(256)S(1)}, u32[]{:S(2)}) copy-start(s32[256]{0:T(256)S(1)} %gather_fusion.11) | copy-start | bytes 3076
  76.6 107.1 %copy-start.201 = (s32[256]{0:T(256)}, s32[256]{0:T(256)S(1)}, u32[]{:S(2)}) copy-start(s32[256]{0:T(256)S(1)} %gather_fusion.16) | copy-start | bytes 3076
  78.5 89.0 %copy-start.212 = (s32[256]{0:T(256)}, s32[256]{0:T(256)S(1)}, u32[]{:S(2)}) copy-start(s32[256]{0:T(256)S(1)} %gather_fusion.7) | copy-start | bytes 3076
  80.4 87.1 %copy-start.214 = (s32[256]{0:T(256)}, s32[256]{0:T(256)S(1)}, u32[]{:S(2)}) copy-start(s32[256]{0:T(256)S(1)} %gather_fusion.12) | copy-start | bytes 3076
  82.3 85.2 %copy-start.216 = (s32[256]{0:T(256)}, s32[256]{0:T(256)S(1)}, u32[]{:S(2)}) copy-start(s32[256]{0:T(256)S(1)} %gather_fusion.17) | copy-start | bytes 3076
  84.2 83.3 %copy-start.217 = (s32[256]{0:T(256)}, s32[256]{0:T(256)S(1)}, u32[]{:S(2)}) copy-start(s32[256]{0:T(256)S(1)} %gather_fusion.2) | copy-start | bytes 3076
  171.2 32.1 %all-to-all-start.4 = ((bf16[2,32,8,1024]{3,2,0,1:T(8,128)(2,1)}), bf16[2,32,8,1024]{3,2,0,1:T(8,128)(2,1)S(1)}, u32[]{:S(2)}, u32[]{:S(2)}) async-start(bf16[2,32,8,1024]{3,2,0,1:T(8,128)(2,1)} %copy.346), calls=%async_computation.4 | async-start | bytes 2097152 | tf_op jit(solution)/shard_map/all_to_all | solution.py:297
  203.3 72.5 %all-to-all-start.2 = ((bf16[2,32,8,1024]{3,2,0,1:T(8,128)(2,1)}), bf16[2,32,8,1024]{3,2,0,1:T(8,128)(2,1)}, u32[]{:S(2)}, u32[]{:S(2)}) async-start(bf16[2,32,8,1024]{3,2,0,1:T(8,128)(2,1)} %copy.332), calls=%async_computation.2 | async-start | bytes 2097152 | tf_op jit(solution)/shard_map/all_to_all | solution.py:297
  220.6 113.9 %copy-start.108 = (f32[8,1,128]{2,1,0:T(1,128)}, f32[8,1,128]{2,1,0:T(1,128)S(1)}, u32[]{:S(2)}) copy-start(f32[8,1,128]{2,1,0:T(1,128)S(1)} %convert_element_type.453) | copy-start | bytes 12292
  275.8 31.0 %all-to-all-start = ((bf16[2,32,8,1024]{3,2,0,1:T(8,128)(2,1)}), bf16[2,32,8,1024]{3,2,0,1:T(8,128)(2,1)}, u32[]{:S(2)}, u32[]{:S(2)}) async-start(bf16[2,32,8,1024]{3,2,0,1:T(8,128)(2,1)} %copy.318), calls=%async_computation | async-start | bytes 2097152 | tf_op jit(solution)/shard_map/all_to_all | solution.py:297
  280.6 943.2 %reduce-scatter.5.cloned.1.call-start = ((), (), s32[]{:S(2)}) async-start(), calls=%async_computation.15 | async-start | bytes 6045696 | tf_op jit(solution)/shard_map/reduce_scatter | solution.py:255
  903.8 320.0 %reduce-scatter.3.cloned.1.call-start = ((), (), s32[]{:S(2)}) async-start(), calls=%async_computation.14 | async-start | bytes 21528576 | tf_op jit(solution)/shard_map/reduce_scatter | solution.py:243
  1106.4 54.7 %all-to-all-start.5 = ((bf16[2,32,8,1024]{3,2,0,1:T(8,128)(2,1)}), bf16[2,32,8,1024]{3,2,0,1:T(8,128)(2,1)}, u32[]{:S(2)}, u32[]{:S(2)}) async-start(bf16[2,32,8,1024]{3,2,0,1:T(8,128)(2,1)} %copy.357), calls=%async_computation.5 | async-start | bytes 2097152 | tf_op jit(solution)/shard_map/all_to_all | solution.py:319
  1161.1 57.0 %all-to-all-start.1 = ((bf16[2,32,8,1024]{3,2,0,1:T(8,128)(2,1)}), bf16[2,32,8,1024]{3,2,0,1:T(8,128)(2,1)}, u32[]{:S(2)}, u32[]{:S(2)}) async-start(bf16[2,32,8,1024]{3,2,0,1:T(8,128)(2,1)} %copy.329), calls=%async_computation.1 | async-start | bytes 2097152 | tf_op jit(solution)/shard_map/all_to_all | solution.py:319
  1218.0 57.4 %all-to-all-start.3 = ((bf16[2,32,8,1024]{3,2,0,1:T(8,128)(2,1)}), bf16[2,32,8,1024]{3,2,0,1:T(8,128)(2,1)S(1)}, u32[]{:S(2)}, u32[]{:S(2)}) async-start(bf16[2,32,8,1024]{3,2,0,1:T(8,128)(2,1)} %copy.343), calls=%async_computation.3 | async-start | bytes 2097152 | tf_op jit(solution)/shard_map/all_to_all | solution.py:319
  1223.7 156.6 %all-reduce.7.cloned.1.call-start = ((), (), s32[]{:S(2)}) async-start(), calls=%async_computation.16 | async-start | bytes 6127616 | tf_op jit(solution)/shard_map/psum | solution.py:327
  1275.4 72.3 %all-to-all-start.7 = ((bf16[2,32,8,1024]{3,2,0,1:T(8,128)(2,1)}), bf16[2,32,8,1024]{3,2,0,1:T(8,128)(2,1)S(1)}, u32[]{:S(2)}, u32[]{:S(2)}) async-start(bf16[2,32,8,1024]{3,2,0,1:T(8,128)(2,1)} %copy.371), calls=%async_computation.7 | async-start | bytes 2097152 | tf_op jit(solution)/shard_map/all_to_all | solution.py:319
  (230 other events, 2111.8 us)
Sparse Core Ops, SparseCore 0:
  9.9 48.2 all-gather.6
  60.1 29.2 all-gather.8
  91.3 64.3 all-gather.10
  157.4 49.8 all-gather.12
  903.9 56.2 reduce-scatter.4
  1016.7 134.4 reduce-scatter.2
  1227.0 153.2 all-reduce.6
where the time goes:
time: 1420 us; the launch traced here: 1390 us
  matrix products  565 us (40%)
  local copies, waits for them, and re-layouts  511 us (36%)
  other arithmetic  146 us (10%)
  waiting for transfers between devices  54.4 us (4%)
  blocking collectives  53 us (4%)
  starting transfers between devices  43.8 us (3%)
  between operations  18.5 us (1%)
    dot_general x16, matrix products, contract_rows(): lax.dot_general(left, right, (((0,), (0,)), ((), ())), preferred_element_...  111 us
    scatter x4, local copies, waits for them, and re-layouts, body(): back_rows.at[0, drop_source, safe_rank].set(layer_rows, mode='drop')  110 us
    scatter x8, local copies, waits for them, and re-layouts, body(): back_rows.at[1, drop_source, safe_rank].set(grad_rows, mode='drop')  83.3 us
    dot_general x64, matrix products, block_scores(): jnp.einsum('qhd,khd->hqk', query_part, key_part, preferred_element_type=j...  76.8 us
    scatter x8, local copies, waits for them, and re-layouts, body(): outgoing.at[1, target, send_rank].set(cotangent[micro_step, :, 0])  74.2 us
    scatter x4, local copies, waits for them, and re-layouts, body(): outgoing = outgoing.at[0, target, send_rank].set(tokens[micro_step, :, 0])  62.9 us
    convert_element_type x1, other arithmetic, reduce_grads(): summed.astype(jnp.bfloat16)  53.1 us
    dot_general x32, matrix products, attend_back(): jnp.einsum('hqk,qhd->khd', softmax_w.astype(jnp.bfloat16), grad_part, pre...  46.8 us
  transfers between devices with their start and end apart: 15, of which 3 were waited for; matrix products, arithmetic and copies ran while one was open for 56% of the time, Pallas kernels for 0%

commit v1 on v0

v1 whole, which is shorter than its diff:
```python
import functools
import math

import jax
import jax.numpy as jnp
import numpy as np
from jax import lax
from jax.experimental import pallas as pl
from jax.experimental.pallas import tpu as pltpu
from jax.sharding import PartitionSpec as P

D = 1024
HEADS = 16
HD = 64
FF = 2624
BLK = 128
MICRO = 4
SEQ_DEV = 2
CAP = 256
TOK_DEV = 192
ROWS = MICRO * CAP
BLOCKS = ROWS // BLK
PAIRS = HEADS // 2
LANES = 2 * HD

EPS = 1e-05
THETA = 160000.0
NEG = -1e30
ROOT_HALF = math.sqrt(0.5)
INV_ROOT_TWO_PI = 1.0 / math.sqrt(2.0 * math.pi)
SCALE = HD**-0.5

FF_TILE = 384
FF_STEPS = -(-FF // FF_TILE)
FF_PAD = FF_STEPS * FF_TILE
ROW_CHUNK = 256
CHUNK_ROWS = 16

F32 = jnp.float32
BF16 = jnp.bfloat16
MIB = 1 << 20


def dot(left, right, left_dim=1, right_dim=0):
    return lax.dot_general(
        left, right, (((left_dim,), (right_dim,)), ((), ())), preferred_element_type=F32
    )


def params(mib, steps=1):
    return pltpu.CompilerParams(
        vmem_limit_bytes=mib * MIB, dimension_semantics=("arbitrary",) * steps
    )


def cost(flops, moved, transcendentals=0):
    return pl.CostEstimate(
        flops=flops, bytes_accessed=moved, transcendentals=transcendentals
    )


def normed(values):
    center = values - jnp.mean(values, axis=-1, keepdims=True)
    inverse = lax.rsqrt(jnp.mean(center * center, axis=-1, keepdims=True) + EPS)
    return center * inverse, inverse


def norm_back(grad, normal, inverse):
    centred = grad - jnp.mean(grad, axis=-1, keepdims=True)
    return inverse * (centred - normal * jnp.mean(grad * normal, axis=-1, keepdims=True))


def rotary_tables(width):
    half = HD // 2
    frequency = THETA ** (-2.0 * jnp.arange(half, dtype=F32) / HD)
    angles = jnp.arange(BLK, dtype=F32)[:, None] * frequency[None, :]
    cosine, sine = jnp.cos(angles), jnp.sin(angles)
    cosine = jnp.concatenate([cosine, cosine], axis=1)
    sine = jnp.concatenate([-sine, sine], axis=1)
    return (jnp.tile(cosine, (1, width // HD)), jnp.tile(sine, (1, width // HD)))


def turned(values):
    axis = values.ndim - 1
    half = HD // 2
    width = values.shape[axis]
    lane = lax.broadcasted_iota(jnp.int32, values.shape, axis) % HD
    return jnp.where(
        lane < half,
        pltpu.roll(values, width - half, axis),
        pltpu.roll(values, half, axis),
    )


def pack_kernel(micros, rows_ref, want_ref, out_ref):
    total = None
    for step in range(micros):
        want = want_ref[step]
        mine = lax.broadcasted_iota(jnp.int32, (TOK_DEV, want.shape[1]), 0)
        pick = (mine == want).astype(F32).astype(BF16)
        term = dot(pick, rows_ref[step], 0, 0)
        total = term if total is None else total + term
    out_ref[...] = total.astype(BF16).reshape(out_ref.shape)


def pack_rows(rows, want, devices, micros):
    groups = MICRO // micros
    slots = want.shape[-1]
    return pl.pallas_call(
        functools.partial(pack_kernel, micros),
        grid=(groups,),
        in_specs=[
            pl.BlockSpec((micros, TOK_DEV, D), lambda g: (g, 0, 0)),
            pl.BlockSpec((micros, 1, slots), lambda g: (g, 0, 0)),
        ],
        out_specs=pl.BlockSpec((devices, 1, CHUNK_ROWS, D), lambda g: (0, g, 0, 0)),
        out_shape=jax.ShapeDtypeStruct((devices, groups, CHUNK_ROWS, D), BF16),
        compiler_params=params(40),
        cost_estimate=cost(2 * MICRO * TOK_DEV * slots * D, 4 * groups * slots * D),
    )(rows, want)


def spread_kernel(micros, back_ref, want_ref, out_ref):
    arrived = back_ref[...].reshape(-1, D)
    for step in range(micros):
        want = want_ref[step]
        mine = lax.broadcasted_iota(jnp.int32, (TOK_DEV, want.shape[1]), 0)
        pick = (mine == want).astype(F32).astype(BF16)
        out_ref[step] = dot(pick, arrived).astype(BF16)


def spread_rows(back, want, devices, micros):
    groups = MICRO // micros
    slots = want.shape[-1]
    return pl.pallas_call(
        functools.partial(spread_kernel, micros),
        grid=(groups,),
        in_specs=[
            pl.BlockSpec((devices, 1, CHUNK_ROWS, D), lambda g: (0, g, 0, 0)),
            pl.BlockSpec((micros, 1, slots), lambda g: (g, 0, 0)),
        ],
        out_specs=pl.BlockSpec((micros, TOK_DEV, D), lambda g: (g, 0, 0)),
        out_shape=jax.ShapeDtypeStruct((MICRO, TOK_DEV, D), BF16),
        compiler_params=params(40),
        cost_estimate=cost(2 * MICRO * TOK_DEV * slots * D, 4 * groups * slots * D),
    )(back, want)


def row_pick(start_ref, length_ref, slot_ref, group, micros):
    parts = []
    for step in range(micros):
        slots = slot_ref[step]
        for block in range(CAP // BLK):
            micro = group * micros + step
            place = lax.broadcasted_iota(jnp.int32, (BLK, slots.shape[1]), 0)
            given = jnp.where(
                place < length_ref[micro, block], place + start_ref[micro, block], -1
            )
            parts.append((given == slots).astype(F32).astype(BF16))
    return jnp.concatenate(parts, axis=0)


def unpack_kernel(
    micros, with_norm, start_ref, length_ref, slot_ref, arrived_ref, gain_ref, *outs
):
    pick = row_pick(start_ref, length_ref, slot_ref, pl.program_id(0), micros)
    rows = dot(pick, arrived_ref[...].reshape(-1, D))
    outs[0][...] = rows.astype(BF16)
    if with_norm:
        outs[1][...] = (normed(rows)[0] * gain_ref[...]).astype(BF16)


def unpack_rows(arrived, starts, lengths, slots, gain, devices, micros, with_norm):
    groups = MICRO // micros
    width = slots.shape[-1]
    out_spec = pl.BlockSpec((micros * CAP, D), lambda g: (g, 0))
    out_type = jax.ShapeDtypeStruct((ROWS, D), BF16)
    count = 2 if with_norm else 1
    return pl.pallas_call(
        functools.partial(unpack_kernel, micros, with_norm),
        grid=(groups,),
        in_specs=[
            pl.BlockSpec(memory_space=pltpu.SMEM),
            pl.BlockSpec(memory_space=pltpu.SMEM),
            pl.BlockSpec((micros, 1, width), lambda g: (g, 0, 0)),
            pl.BlockSpec((devices, 1, CHUNK_ROWS, D), lambda g: (0, g, 0, 0)),
            pl.BlockSpec((1, D), lambda g: (0, 0)),
        ],
        out_specs=[out_spec] * count,
        out_shape=[out_type] * count,
        compiler_params=params(40),
        cost_estimate=cost(2 * ROWS * width * D, 4 * groups * width * D),
    )(starts, lengths, slots, arrived, gain)


def repack_kernel(micros, start_ref, length_ref, slot_ref, rows_ref, out_ref):
    pick = row_pick(start_ref, length_ref, slot_ref, pl.program_id(0), micros)
    out_ref[...] = dot(pick, rows_ref[...], 0, 0).astype(BF16).reshape(out_ref.shape)


def repack_rows(rows, starts, lengths, slots, devices, micros):
    groups = MICRO // micros
    width = slots.shape[-1]
    return pl.pallas_call(
        functools.partial(repack_kernel, micros),
        grid=(groups,),
        in_specs=[
            pl.BlockSpec(memory_space=pltpu.SMEM),
            pl.BlockSpec(memory_space=pltpu.SMEM),
            pl.BlockSpec((micros, 1, width), lambda g: (g, 0, 0)),
            pl.BlockSpec((micros * CAP, D), lambda g: (g, 0)),
        ],
        out_specs=pl.BlockSpec((devices, 1, CHUNK_ROWS, D), lambda g: (0, g, 0, 0)),
        out_shape=jax.ShapeDtypeStruct((devices, groups, CHUNK_ROWS, D), BF16),
        compiler_params=params(40),
        cost_estimate=cost(2 * ROWS * width * D, 4 * groups * width * D),
    )(starts, lengths, slots, rows)


QKV_TILE = 512


def qkv_kernel(act_ref, weight_ref, cos_ref, sin_ref, out_ref):
    packed = dot(act_ref[...], weight_ref[...])
    is_value = pl.program_id(0) >= 2 * D // QKV_TILE

    @pl.when(is_value)
    def _():
        out_ref[...] = packed.astype(BF16)

    @pl.when(jnp.logical_not(is_value))
    def _():
        split = packed.reshape(BLOCKS, BLK, QKV_TILE)
        spun = split * cos_ref[...][None] + turned(split) * sin_ref[...][None]
        out_ref[...] = spun.reshape(ROWS, QKV_TILE).astype(BF16)


def qkv_rows(act, weight, cosine, sine):
    return pl.pallas_call(
        qkv_kernel,
        grid=(3 * D // QKV_TILE,),
        in_specs=[
            pl.BlockSpec((ROWS, D), lambda j: (0, 0)),
            pl.BlockSpec((D, QKV_TILE), lambda j: (0, j)),
            pl.BlockSpec((BLK, QKV_TILE), lambda j: (0, 0)),
            pl.BlockSpec((BLK, QKV_TILE), lambda j: (0, 0)),
        ],
        out_specs=pl.BlockSpec((ROWS, QKV_TILE), lambda j: (0, j)),
        out_shape=jax.ShapeDtypeStruct((ROWS, 3 * D), BF16),
        compiler_params=params(40),
        cost_estimate=cost(2 * ROWS * D * 3 * D, 2 * (3 * D * D + ROWS * 4 * D)),
    )(act, weight, cosine, sine)


def head_masks(dtype):
    lane = lax.broadcasted_iota(jnp.int32, (BLK, LANES), 1)
    low = (lane < HD).astype(F32).astype(dtype)
    high = (lane >= HD).astype(F32).astype(dtype)
    return low, high


def attend_kernel(length_ref, q_ref, k_ref, v_ref, out_ref, prob_ref):
    block = pl.program_id(0)
    length = length_ref[block // 2, block % 2]
    low, high = head_masks(BF16)
    valid = lax.broadcasted_iota(jnp.int32, (BLK, BLK), 1) < length
    for pair in range(PAIRS):
        lanes = slice(pair * LANES, (pair + 1) * LANES)
        query, key, value = q_ref[:, lanes], k_ref[:, lanes], v_ref[:, lanes]
        scores = dot(query, jnp.concatenate([key * low, key * high], axis=0), 1, 1)
        parts = []
        for head in range(2):
            score = scores[:, head * BLK : (head + 1) * BLK] * SCALE
            score = jnp.where(valid, score, NEG)
            expo = jnp.exp(score - jnp.max(score, axis=-1, keepdims=True))
            parts.append(expo / jnp.sum(expo, axis=-1, keepdims=True))
        prob = jnp.concatenate(parts, axis=1).astype(BF16)
        prob_ref[0, pair] = prob
        both = jnp.concatenate([value * low, value * high], axis=0)
        out_ref[:, lanes] = dot(prob, both).astype(BF16)


def attend(qkv, lengths):
    return pl.pallas_call(
        attend_kernel,
        grid=(BLOCKS,),
        in_specs=[
            pl.BlockSpec(memory_space=pltpu.SMEM),
            pl.BlockSpec((BLK, D), lambda b: (b, 0)),
            pl.BlockSpec((BLK, D), lambda b: (b, 1)),
            pl.BlockSpec((BLK, D), lambda b: (b, 2)),
        ],
        out_specs=[
            pl.BlockSpec((BLK, D), lambda b: (b, 0)),
            pl.BlockSpec((1, PAIRS, BLK, 2 * BLK), lambda b: (b, 0, 0, 0)),
        ],
        out_shape=[
            jax.ShapeDtypeStruct((ROWS, D), BF16),
            jax.ShapeDtypeStruct((BLOCKS, PAIRS, BLK, 2 * BLK), BF16),
        ],
        compiler_params=params(32),
        cost_estimate=cost(8 * ROWS * BLK * D, 2 * ROWS * 6 * D, ROWS * HEADS * BLK),
    )(lengths, qkv, qkv, qkv)


def attend_back_kernel(
    q_ref, k_ref, v_ref, grad_ref, prob_ref, cos_ref, sin_ref, out_ref
):
    low, high = head_masks(BF16)
    lane = lax.broadcasted_iota(jnp.int32, (BLK, LANES), 1)
    is_low = lane < HD
    cosine, sine = cos_ref[...], sin_ref[...]
    for pair in range(PAIRS):
        lanes = slice(pair * LANES, (pair + 1) * LANES)
        query, key, value = q_ref[:, lanes], k_ref[:, lanes], v_ref[:, lanes]
        grad, prob = grad_ref[:, lanes], prob_ref[0, pair]
        grad_v = dot(prob, grad, 0, 0)
        grad_v = jnp.where(is_low, grad_v[:BLK], grad_v[BLK:])
        grad_p = dot(grad, jnp.concatenate([value * low, value * high], axis=0), 1, 1)
        parts = []
        for head in range(2):
            keys = slice(head * BLK, (head + 1) * BLK)
            weight, slope = prob[:, keys].astype(F32), grad_p[:, keys]
            inner = jnp.sum(weight * slope, axis=-1, keepdims=True)
            parts.append(weight * (slope - inner))
        grad_s = jnp.concatenate(parts, axis=1).astype(BF16)
        both = jnp.concatenate([key * low, key * high], axis=0)
        grad_q = dot(grad_s, both) * SCALE
        grad_k = dot(grad_s, query, 0, 0)
        grad_k = jnp.where(is_low, grad_k[:BLK], grad_k[BLK:]) * SCALE
        start = pair * LANES
        out_ref[:, start : start + LANES] = (
            grad_q * cosine - turned(grad_q) * sine
        ).astype(BF16)
        out_ref[:, D + start : D + start + LANES] = (
            grad_k * cosine - turned(grad_k) * sine
        ).astype(BF16)
        out_ref[:, 2 * D + start : 2 * D + start + LANES] = grad_v.astype(BF16)


def attend_back(qkv, grad_o, prob, cosine, sine):
    return pl.pallas_call(
        attend_back_kernel,
        grid=(BLOCKS,),
        in_specs=[
            pl.BlockSpec((BLK, D), lambda b: (b, 0)),
            pl.BlockSpec((BLK, D), lambda b: (b, 1)),
            pl.BlockSpec((BLK, D), lambda b: (b, 2)),
            pl.BlockSpec((BLK, D), lambda b: (b, 0)),
            pl.BlockSpec((1, PAIRS, BLK, 2 * BLK), lambda b: (b, 0, 0, 0)),
            pl.BlockSpec((BLK, LANES), lambda b: (0, 0)),
            pl.BlockSpec((BLK, LANES), lambda b: (0, 0)),
        ],
        out_specs=pl.BlockSpec((BLK, 3 * D), lambda b: (b, 0)),
        out_shape=jax.ShapeDtypeStruct((ROWS, 3 * D), BF16),
        compiler_params=params(32),
        cost_estimate=cost(20 * ROWS * BLK * D, 2 * ROWS * 9 * D),
    )(qkv, qkv, qkv, grad_o, prob, cosine, sine)


def middle_kernel(attn_ref, hidden_ref, weight_ref, gain_ref, mid_ref, act_ref):
    middle = hidden_ref[...].astype(F32) + dot(attn_ref[...], weight_ref[...])
    mid_ref[...] = middle
    act_ref[...] = (normed(middle)[0] * gain_ref[...]).astype(BF16)


def middle_rows(attn_o, hidden, weight, gain):
    tile = pl.BlockSpec((ROW_CHUNK, D), lambda i: (i, 0))
    return pl.pallas_call(
        middle_kernel,
        grid=(ROWS // ROW_CHUNK,),
        in_specs=[
            tile,
            tile,
            pl.BlockSpec((D, D), lambda i: (0, 0)),
            pl.BlockSpec((1, D), lambda i: (0, 0)),
        ],
        out_specs=[tile, tile],
        out_shape=[
            jax.ShapeDtypeStruct((ROWS, D), F32),
            jax.ShapeDtypeStruct((ROWS, D), BF16),
        ],
        compiler_params=params(32),
        cost_estimate=cost(2 * ROWS * D * D, 2 * D * D + 10 * ROWS * D),
    )(attn_o, hidden, weight, gain)


def ffn_kernel(
    act_ref,
    top_ref,
    mid_ref,
    gelu_w_ref,
    line_w_ref,
    down_ref,
    layer_ref,
    grad_b_ref,
    grad_gelu_ref,
    grad_line_ref,
    grad_down_ref,
    total,
    act_t,
    down_clean,
    kept_c,
    kept_gelu,
    kept_line,
):
    step = pl.program_id(0)

    @pl.when(step == 0)
    def _():
        total[...] = mid_ref[...]
        grad_b_ref[...] = jnp.zeros_like(grad_b_ref)
        act_t[...] = act_ref[...].T

    row = lax.broadcasted_iota(jnp.int32, (FF_TILE, D), 0) + step * FF_TILE
    down_clean[...] = jnp.where(row < FF, down_ref[...].astype(F32), 0.0).astype(BF16)

    def rows_step(index, carry):
        rows = pl.ds(pl.multiple_of(index * ROW_CHUNK, ROW_CHUNK), ROW_CHUNK)
        act, top = act_ref[rows, :], top_ref[rows, :]
        gelu_in = dot(act, gelu_w_ref[...])
        linear = dot(act, line_w_ref[...])
        grad_c = dot(top, down_clean[...], 1, 1)
        phi = 0.5 * (1.0 + lax.erf(gelu_in * ROOT_HALF))
        gelu_out = gelu_in * phi
        slope = phi + gelu_in * (jnp.exp(-0.5 * gelu_in * gelu_in) * INV_ROOT_TWO_PI)
        act_c = (gelu_out * linear).astype(BF16)
        grad_gelu = (grad_c * linear * slope).astype(BF16)
        grad_line = (grad_c * gelu_out).astype(BF16)
        kept_c[rows, :] = act_c
        kept_gelu[rows, :] = grad_gelu
        kept_line[rows, :] = grad_line
        total[rows, :] += dot(act_c, down_clean[...])
        grad_b_ref[rows, :] += dot(grad_gelu, gelu_w_ref[...], 1, 1) + dot(
            grad_line, line_w_ref[...], 1, 1
        )
        return carry

    lax.fori_loop(0, ROWS // ROW_CHUNK, rows_step, 0)
    grad_gelu_ref[...] = dot(act_t[...], kept_gelu[...]).astype(BF16)
    grad_line_ref[...] = dot(act_t[...], kept_line[...]).astype(BF16)
    grad_down_ref[...] = dot(kept_c[...], top_ref[...], 0, 0).astype(BF16)

    @pl.when(step == FF_STEPS - 1)
    def _():
        layer_ref[...] = total[...].astype(BF16)


def ffn(act, top, middle, full_in, full_down):
    whole = pl.BlockSpec((ROWS, D), lambda j: (0, 0))
    tall = pl.BlockSpec((D, FF_TILE), lambda j: (0, j))
    wide = pl.BlockSpec((FF_TILE, D), lambda j: (j, 0))
    return pl.pallas_call(
        ffn_kernel,
        grid=(FF_STEPS,),
        in_specs=[
            whole,
            whole,
            whole,
            tall,
            pl.BlockSpec((D, FF_TILE), lambda j: (0, j + FF_STEPS)),
            wide,
        ],
        out_specs=[whole, whole, tall, tall, wide],
        out_shape=[
            jax.ShapeDtypeStruct((ROWS, D), BF16),
            jax.ShapeDtypeStruct((ROWS, D), F32),
            jax.ShapeDtypeStruct((D, FF_PAD), BF16),
            jax.ShapeDtypeStruct((D, FF_PAD), BF16),
            jax.ShapeDtypeStruct((FF, D), BF16),
        ],
        scratch_shapes=[
            pltpu.VMEM((ROWS, D), F32),
            pltpu.VMEM((D, ROWS), BF16),
            pltpu.VMEM((FF_TILE, D), BF16),
            pltpu.VMEM((ROWS, FF_TILE), BF16),
            pltpu.VMEM((ROWS, FF_TILE), BF16),
            pltpu.VMEM((ROWS, FF_TILE), BF16),
        ],
        compiler_params=params(60),
        cost_estimate=cost(18 * ROWS * D * FF, 12 * D * FF, 2 * ROWS * FF),
    )(act, top, middle, full_in, full_in, full_down)


def branch_kernel(
    grad_b_ref,
    mid_ref,
    top_ref,
    attn_ref,
    weight_ref,
    gain_ref,
    grad_mid_ref,
    grad_o_ref,
    grad_w_ref,
    grad_gain_ref,
    total,
):
    step = pl.program_id(0)

    @pl.when(step == 0)
    def _():
        total[...] = jnp.zeros_like(total)
        grad_gain_ref[...] = jnp.zeros_like(grad_gain_ref)

    grad_b = grad_b_ref[...]
    normal, inverse = normed(mid_ref[...])
    grad_gain_ref[...] += jnp.sum(grad_b * normal, axis=0, keepdims=True)
    grad_mid = top_ref[...].astype(F32) + norm_back(
        grad_b * gain_ref[...], normal, inverse
    )
    grad_mid_ref[...] = grad_mid
    grad_r = grad_mid.astype(BF16)
    grad_o_ref[...] = dot(grad_r, weight_ref[...], 1, 1).astype(BF16)
    total[...] += dot(attn_ref[...], grad_r, 0, 0)

    @pl.when(step == ROWS // ROW_CHUNK - 1)
    def _():
        grad_w_ref[...] = total[...].astype(BF16)


def branch_back(grad_b, middle, top, attn_o, weight, gain):
    tile = pl.BlockSpec((ROW_CHUNK, D), lambda i: (i, 0))
    square = pl.BlockSpec((D, D), lambda i: (0, 0))
    line = pl.BlockSpec((1, D), lambda i: (0, 0))
    return pl.pallas_call(
        branch_kernel,
        grid=(ROWS // ROW_CHUNK,),
        in_specs=[tile, tile, tile, tile, square, line],
        out_specs=[tile, tile, square, line],
        out_shape=[
            jax.ShapeDtypeStruct((ROWS, D), F32),
            jax.ShapeDtypeStruct((ROWS, D), BF16),
            jax.ShapeDtypeStruct((D, D), BF16),
            jax.ShapeDtypeStruct((1, D), F32),
        ],
        scratch_shapes=[pltpu.VMEM((D, D), F32)],
        compiler_params=params(40),
        cost_estimate=cost(4 * ROWS * D * D, 4 * D * D + 18 * ROWS * D),
    )(grad_b, middle, top, attn_o, weight, gain)


def input_kernel(
    grad_qkv_ref, weight_ref, hidden_ref, grad_mid_ref, gain_ref, out_ref, grad_gain_ref
):
    @pl.when(pl.program_id(0) == 0)
    def _():
        grad_gain_ref[...] = jnp.zeros_like(grad_gain_ref)

    grad_a = dot(grad_qkv_ref[...], weight_ref[...], 1, 1)
    normal, inverse = normed(hidden_ref[...].astype(F32))
    grad_gain_ref[...] += jnp.sum(grad_a * normal, axis=0, keepdims=True)
    out_ref[...] = (
        grad_mid_ref[...] + norm_back(grad_a * gain_ref[...], normal, inverse)
    ).astype(BF16)


def input_back(grad_qkv, weight, hidden, grad_mid, gain):
    tile = pl.BlockSpec((ROW_CHUNK, D), lambda i: (i, 0))
    line = pl.BlockSpec((1, D), lambda i: (0, 0))
    return pl.pallas_call(
        input_kernel,
        grid=(ROWS // ROW_CHUNK,),
        in_specs=[
            pl.BlockSpec((ROW_CHUNK, 3 * D), lambda i: (i, 0)),
            pl.BlockSpec((D, 3 * D), lambda i: (0, 0)),
            tile,
            tile,
            line,
        ],
        out_specs=[tile, line],
        out_shape=[
            jax.ShapeDtypeStruct((ROWS, D), BF16),
            jax.ShapeDtypeStruct((1, D), F32),
        ],
        compiler_params=params(40),
        cost_estimate=cost(6 * ROWS * D * D, 6 * D * D + 14 * ROWS * D),
    )(grad_qkv, weight, hidden, grad_mid, gain)


def qkv_grad_kernel(act_ref, grad_ref, out_ref, act_t):
    @pl.when(pl.program_id(0) == 0)
    def _():
        act_t[...] = act_ref[...].T

    out_ref[...] = dot(act_t[...], grad_ref[...]).astype(BF16)


def qkv_grad(act, grad_qkv):
    return pl.pallas_call(
        qkv_grad_kernel,
        grid=(3 * D // QKV_TILE,),
        in_specs=[
            pl.BlockSpec((ROWS, D), lambda j: (0, 0)),
            pl.BlockSpec((ROWS, QKV_TILE), lambda j: (0, j)),
        ],
        out_specs=pl.BlockSpec((D, QKV_TILE), lambda j: (0, j)),
        out_shape=jax.ShapeDtypeStruct((D, 3 * D), BF16),
        scratch_shapes=[pltpu.VMEM((D, ROWS), BF16)],
        compiler_params=params(32),
        cost_estimate=cost(6 * ROWS * D * D, 2 * (7 * D * D)),
    )(act, grad_qkv)


def plan(seq_lengths, device, devices, micros):
    pair_cap = CAP // devices
    slots = devices * CHUNK_ROWS
    slot = jnp.arange(slots, dtype=jnp.int32)
    peer, inner = slot // CHUNK_ROWS, slot % CHUNK_ROWS
    rank, part = inner % pair_cap, inner // pair_cap
    micro = jnp.arange(MICRO, dtype=jnp.int32)
    mine = (micro % micros)[:, None] == part[None, :]
    seq = jnp.arange(seq_lengths.shape[1], dtype=jnp.int32)
    ahead = seq[None, :] < SEQ_DEV * peer[:, None]
    peer_start = jnp.sum(
        jnp.where(ahead[None], seq_lengths[:, None, :], 0), axis=2, dtype=jnp.int32
    )
    want = jnp.where(
        mine, (peer_start - device + devices - 1) // devices + rank[None, :], -1
    )
    own_seq = device * SEQ_DEV + jnp.arange(SEQ_DEV, dtype=jnp.int32)
    starts = jnp.sum(
        jnp.where(seq[None, None, :] < own_seq[None, :, None], seq_lengths[:, None, :], 0),
        axis=2,
        dtype=jnp.int32,
    )
    lengths = jnp.sum(
        jnp.where(seq[None, None, :] == own_seq[None, :, None], seq_lengths[:, None, :], 0),
        axis=2,
        dtype=jnp.int32,
    )
    first = (starts[:, :1] - peer[None, :] + devices - 1) // devices
    given = jnp.where(mine, (first + rank[None, :]) * devices + peer[None, :], -2)
    return want[:, None, :], starts, lengths, given[:, None, :]


def body(tokens, cotangent, seq_lengths, w_qkv, w_out, w_in, w_down, attn_gain, mlp_gain):
    group_size = lax.axis_size("grp")
    devices = lax.axis_size("rep") * group_size
    device = lax.axis_index("rep") * group_size + lax.axis_index("grp")
    micros = min(MICRO, max(1, CHUNK_ROWS * devices // CAP))
    both = ("rep", "grp")

    def swap(rows):
        return lax.all_to_all(rows, both, split_axis=0, concat_axis=0, tiled=True)

    def gather(rows):
        return lax.all_gather(rows, "grp", axis=0, tiled=True)

    want, starts, lengths, given = plan(seq_lengths, device, devices, micros)
    token_rows = swap(pack_rows(tokens[:, :, 0], want, devices, micros))
    top_rows = swap(pack_rows(cotangent[:, :, 0], want, devices, micros))
    gains = lax.all_gather(jnp.stack([attn_gain, mlp_gain]), "grp", axis=1, tiled=True)
    gain_one = gains[:1].astype(F32)
    gain_two = gains[1:].astype(F32)
    full_qkv = gather(w_qkv)
    full_out = gather(w_out)
    gap = jnp.zeros((w_in.shape[0], FF_PAD - FF), BF16)
    full_in = gather(jnp.concatenate([w_in[:, :FF], gap, w_in[:, FF:], gap], axis=1))
    full_down = gather(w_down)

    cosine, sine = rotary_tables(QKV_TILE)
    hidden, act_a = unpack_rows(
        token_rows, starts, lengths, given, gain_one, devices, micros, True
    )
    (top,) = unpack_rows(
        top_rows, starts, lengths, given, gain_one, devices, micros, False
    )
    qkv = qkv_rows(act_a, full_qkv, cosine, sine)
    attn_o, prob = attend(qkv, lengths)
    middle, act_b = middle_rows(attn_o, hidden, full_out, gain_two)
    layer_rows, grad_b, grad_gelu_w, grad_line_w, grad_down_w = ffn(
        act_b, top, middle, full_in, full_down
    )
    layer_back = swap(repack_rows(layer_rows, starts, lengths, given, devices, micros))

    def owned(part):
        return lax.psum_scatter(part, "grp", scatter_dimension=0, tiled=True)

    def summed(part):
        return lax.psum(part, "rep")

    grad_down = summed(owned(grad_down_w))
    grad_gelu = summed(owned(grad_gelu_w))
    grad_line = summed(owned(grad_line_w))
    grad_mid, grad_o, grad_out_w, grad_gain_two = branch_back(
        grad_b, middle, top, attn_o, full_out, gain_two
    )
    grad_out = summed(owned(grad_out_w))
    grad_qkv_rows = attend_back(qkv, grad_o, prob, cosine[:, :LANES], sine[:, :LANES])
    grad_qkv_w = qkv_grad(act_a, grad_qkv_rows)
    grad_qkv = summed(owned(grad_qkv_w))
    grad_rows, grad_gain_one = input_back(
        grad_qkv_rows, full_qkv, hidden, grad_mid, gain_one
    )
    grad_back = swap(repack_rows(grad_rows, starts, lengths, given, devices, micros))
    gain_parts = jnp.concatenate([grad_gain_one, grad_gain_two], axis=0)
    gain_parts = gain_parts.reshape(2, 1, group_size, -1)
    gain_parts = jnp.broadcast_to(
        gain_parts, (2, devices // group_size, *gain_parts.shape[2:])
    ).reshape(2, devices, -1)
    gain_sums = jnp.sum(
        lax.all_to_all(gain_parts, both, split_axis=1, concat_axis=1, tiled=True), axis=1
    )
    layer_out = spread_rows(layer_back, want, devices, micros)[:, :, None, :]
    grad_tokens = spread_rows(grad_back, want, devices, micros)[:, :, None, :]
    return (
        layer_out,
        grad_tokens,
        gain_sums[0],
        gain_sums[1],
        grad_qkv.astype(F32),
        grad_out.astype(F32),
        jnp.concatenate([grad_gelu[:, :FF], grad_line[:, :FF]], axis=1).astype(F32),
        grad_down.astype(F32),
    )


def solution(mesh):
    return jax.shard_map(
        body,
        mesh=mesh,
        in_specs=(
            P(None, None, ("rep", "grp"), None),
            P(None, None, ("rep", "grp"), None),
            P(),
            P("grp", None),
            P("grp", None),
            P("grp", None),
            P("grp", None),
            P("grp"),
            P("grp"),
        ),
        out_specs=(
            P(None, None, ("rep", "grp"), None),
            P(None, None, ("rep", "grp"), None),
            P("grp"),
            P("grp"),
            P("grp", None),
            P("grp", None),
            P("grp", None),
            P("grp", None),
        ),
        check_vma=False,
    )
```

time: 1420 us -> 790 us (0.56); the launches traced: 1390 us -> 789 us
  matrix products: 565 us -> 0 us
  local copies, waits for them, and re-layouts: 511 us -> 45.4 us
  waiting for transfers between devices: 54.4 us -> 489 us
  Pallas kernels: 0 us -> 194 us
  other arithmetic: 146 us -> 8.19 us
  blocking collectives: 53 us -> 16 us
  starting transfers between devices: 43.8 us -> 22.4 us
    dot_general x272 -> x0, matrix products: 565 us -> none  [the longest x16 111 us: contract_rows(): lax.dot_general(left, right, (((0,), (0,)), ((), ())), preferred_element_...]
    scatter x24 -> x0, local copies, waits for them, and re-layouts: 330 us -> none  [the longest x4 110 us: body(): back_rows.at[0, drop_source, safe_rank].set(layer_rows, mode='drop')]
    pallas_call x0 -> x16, Pallas kernels: none -> 194 us  [the longest x1 83.9 us: ffn(): pl.pallas_call(ffn_kernel, grid=(FF_STEPS,), in_specs=[whole, whole, whol...]
    reduce_scatter x2 -> x5, waiting for transfers between devices: 0.03 us -> 187 us  [owned(): return lax.psum_scatter(part, 'grp', scatter_dimension=0, tiled=True)]
    psum x1, waiting for transfers between devices: 18.8 us -> 118 us  [summed(): return lax.psum(part, 'rep')]
    all_to_all x8 -> x5, waiting for transfers between devices: 32.5 us -> 121 us  [the longest x4 118 us: swap(): return lax.all_to_all(rows, both, split_axis=0, concat_axis=0, tiled=True)]
    gather x29 -> x0, local copies, waits for them, and re-layouts: 75.2 us -> none  [the longest x4 18.7 us: body(): layer_parts.append(returned[0, target, send_rank])]
    convert_element_type x49 -> x5, other arithmetic: 70.8 us -> 7.43 us  [the longest x1 2.54 us: body(): grad_qkv.astype(F32)]
  transfers between devices with their start and end apart: 15 -> 15, of which waited for: 3 -> 9; matrix products, arithmetic and copies ran while one was open for 56% -> 1% of each run, Pallas kernels for 0% -> 12%
where the time goes in v1:
time: 790 us; the launch traced here: 789 us
  waiting for transfers between devices  489 us (62%)
  Pallas kernels  194 us (25%)
  local copies, waits for them, and re-layouts  45.4 us (6%)
  starting transfers between devices  22.4 us (3%)
  blocking collectives  16 us (2%)
  between operations  14.7 us (2%)
  other arithmetic  8.19 us (1%)
    reduce_scatter x5, waiting for transfers between devices, owned(): return lax.psum_scatter(part, 'grp', scatter_dimension=0, tiled=True)  187 us
    psum x1, waiting for transfers between devices, summed(): return lax.psum(part, 'rep')  118 us
    all_to_all x4, waiting for transfers between devices, swap(): return lax.all_to_all(rows, both, split_axis=0, concat_axis=0, tiled=True)  118 us
    pallas_call x1, Pallas kernels, ffn(): pl.pallas_call(ffn_kernel, grid=(FF_STEPS,), in_specs=[whole, whole, whol...  83.9 us
    all_gather x4, waiting for transfers between devices, gather(): return lax.all_gather(rows, 'grp', axis=0, tiled=True)  59.3 us
    unnamed x68, local copies, waits for them, and re-layouts  41.6 us
    pallas_call x1, Pallas kernels, attend_back(): pl.pallas_call(attend_back_kernel, grid=(BLOCKS,), in_specs=[pl.BlockSpec...  24.9 us
    all_to_all x4, starting transfers between devices, swap(): return lax.all_to_all(rows, both, split_axis=0, concat_axis=0, tiled=True)  18 us
  transfers between devices with their start and end apart: 15, of which 9 were waited for; matrix products, arithmetic and copies ran while one was open for 1% of the time, Pallas kernels for 12%

profile of v1, /device:TPU:0, one launch (start us, length us, event | category | flops | bytes accessed | tf_op | source)
XLA Modules:
  0.0 789.4 jit_solution(2400970337205292457)
XLA Ops:
  14.7 7.3 all-to-all-start.1
  25.9 45.1 %all-to-all-done.1.arrived_ref = bf16[32,2,16,1024]{3,2,1,0:T(8,128)(2,1)S(1)} async-done(((bf16[32,2,16,1024]{3,2,1,0:T(8,128)(2,1)}), bf16[32,2,16,1024]{3,2,1,0:T(8,128)(2,1)S(1)}, u32[]{:S(2)}, u32[]{:S(2)}) %all-to-all-start.1) | async-done | bytes 2097184 | tf_op jit(solution)/shard_map/all_to_all | solution.py:644
  71.0 4.1 all-to-all-start
  75.9 16.0 %all_gather.15 = bf16[2,1024]{1,0:T(2,128)(2,1)S(1)} all-gather(bf16[2,128]{1,0:T(2,128)(2,1)S(1)} %pad_maximum_fusion.2), channel_id=1, replica_groups=mesh['rep'=4,'grp'=8] {'grp'}, dimensions={1}, use_global_device_ids=true | all-gather | bytes 4608 | tf_op jit(solution)/shard_map/all_gather | solution.py:652
  95.4 28.6 %all-to-all-done.arrived_ref = bf16[32,2,16,1024]{3,2,1,0:T(8,128)(2,1)} async-done(((bf16[32,2,16,1024]{3,2,1,0:T(8,128)(2,1)}), bf16[32,2,16,1024]{3,2,1,0:T(8,128)(2,1)}, u32[]{:S(2)}, u32[]{:S(2)}) %all-to-all-start) | async-done | bytes 2097184 | tf_op jit(solution)/shard_map/all_to_all | solution.py:644
  124.0 3.6 shard_map.153
  129.0 15.9 %shard_map.154.q_ref.k_ref.v_ref = bf16[1024,3072]{1,0:T(8,128)(2,1)S(1)} custom-call(bf16[1024,1024]{1,0:T(8,128)(2,1)S(1)} %get-tuple-element.25.act_ref, bf16[1024,3072]{1,0:T(8,128)(2,1)} %all-gather.5.cloned.1.call-done.weight_ref, f32[128,512]{1,0:T(8,128)S(1)} %copy.34.cos_ref, f32[128,512]{1,0:T(8,128)S(1)} %copy.35.sin_ref), custom_call_target="tpu_custom_call" | custom-call | flops 6442450944 | bytes 14680064 | tf_op jit(solution)/shard_map/pallas_call | solution.py:239
  146.3 10.4 %shard_map.155 = (bf16[1024,1024]{1,0:T(8,128)(2,1)S(1)}, bf16[8,8,128,256]{3,2,1,0:T(8,128)(2,1)S(1)}) custom-call(s32[4,2]{1,0:T(4,128)S(1)} %copy.40.length_ref, bf16[1024,3072]{1,0:T(8,128)(2,1)S(1)} %shard_map.154.q_ref.k_ref.v_ref, bf16[1024,3072]{1,0:T(8,128)(2,1)S(1)} %shard_map.154.q_ref.k_ref.v_ref, bf16[1024,3072]{1,0:T(8,128)(2,1)S(1)} %shard_map.154.q_ref.k_ref.v_ref), custom_call_target="tpu_custom_call" | custom-call | flops 1073741824 | bytes 12582912 | tf_op jit(solution)/shard_map/pallas_call | solution.py:284
  165.1 3.9 shard_map.156
  172.5 59.3 %all-gather.9.cloned.1.call-done.gelu_w_ref.line_w_ref = bf16[1024,5376]{1,0:T(8,128)(2,1)} async-done(((bf16[128,5376]{1,0:T(8,128)(2,1)}), bf16[1024,5376]{1,0:T(8,128)(2,1)}) %all-gather.9.cloned.1.call-update) | async-done | bytes 11010064 | tf_op jit(solution)/shard_map/all_gather | solution.py:647
  231.8 83.9 %shard_map.159 = (bf16[1024,1024]{1,0:T(8,128)(2,1)}, f32[1024,1024]{1,0:T(8,128)}, bf16[1024,2688]{1,0:T(8,128)(2,1)}, bf16[1024,2688]{1,0:T(8,128)(2,1)}, bf16[2624,1024]{1,0:T(8,128)(2,1)}) custom-call(bf16[1024,1024]{1,0:T(8,128)(2,1)} %copy-done.24, bf16[1024,1024]{1,0:T(8,128)(2,1)} %copy-done.9, f32[1024,1024]{1,0:T(8,128)} %copy-done.20, ...), custom_call_target="tpu_custom_call" | custom-call | flops 49526341632 | bytes 32243712 | tf_op jit(solution)/shard_map/pallas_call | solution.py:453
  318.9 11.4 %shard_map.162 = (f32[1024,1024]{1,0:T(8,128)}, bf16[1024,1024]{1,0:T(8,128)(2,1)S(1)}, bf16[1024,1024]{1,0:T(8,128)(2,1)}, f32[1,1024]{1,0:T(1,128)S(1)}) custom-call(f32[1024,1024]{1,0:T(8,128)} %get-tuple-element.31.grad_b_ref, f32[1024,1024]{1,0:T(8,128)} %copy-done.20, bf16[1024,1024]{1,0:T(8,128)(2,1)S(1)} %copy-done.10, ...), custom_call_target="tpu_custom_call" | custom-call | flops 4294967296 | bytes 23068672 | tf_op jit(solution)/shard_map/pallas_call | solution.py:525
  340.0 24.9 %shard_map.163.grad_qkv_ref.grad_ref = bf16[1024,3072]{1,0:T(8,128)(2,1)S(1)} custom-call(bf16[1024,3072]{1,0:T(8,128)(2,1)S(1)} %copy-done.1, bf16[1024,3072]{1,0:T(8,128)(2,1)S(1)} %copy-done.1, bf16[1024,3072]{1,0:T(8,128)(2,1)S(1)} %copy-done.1, bf16[1024,1024]{1,0:T(8,128)(2,1)S(1)} %copy-done.12, bf16[8,8,128,256]{3,2,1,0:T(8,128)(2,1)S(1)} %copy-done.7, ...), custom_call_target="tpu_custom_call" | custom-call | flops 2684354560 | bytes 18874368 | tf_op jit(solution)/shard_map/pallas_call | solution.py:342
  364.9 9.0 %shard_map.167 = bf16[1024,3072]{1,0:T(8,128)(2,1)S(1)} custom-call(bf16[1024,1024]{1,0:T(8,128)(2,1)S(1)} %copy-done.26, bf16[1024,3072]{1,0:T(8,128)(2,1)S(1)} %shard_map.163.grad_qkv_ref.grad_ref), custom_call_target="tpu_custom_call" | custom-call | flops 6442450944 | bytes 14680064 | tf_op jit(solution)/shard_map/pallas_call | solution.py:589
  383.3 13.4 %shard_map.164 = (bf16[1024,1024]{1,0:T(8,128)(2,1)S(1)}, f32[1,1024]{1,0:T(1,128)S(1)}) custom-call(bf16[1024,3072]{1,0:T(8,128)(2,1)} %copy-done.5, bf16[1024,3072]{1,0:T(8,128)(2,1)} %all-gather.5.cloned.1.call-done.weight_ref, bf16[1024,1024]{1,0:T(8,128)(2,1)S(1)} %copy-done.23, f32[1024,1024]{1,0:T(8,128)S(1)} %copy-done.19, ...), custom_call_target="tpu_custom_call" | custom-call | flops 6442450944 | bytes 20971520 | tf_op jit(solution)/shard_map/pallas_call | solution.py:560
  397.4 4.0 all-to-all-start.4
  405.0 3.6 all-to-all-done.4
  416.5 43.9 %all-to-all-done.3.back_ref = bf16[32,2,16,1024]{3,2,1,0:T(8,128)(2,1)S(1)} async-done(((bf16[32,2,16,1024]{3,2,1,0:T(8,128)(2,1)}), bf16[32,2,16,1024]{3,2,1,0:T(8,128)(2,1)S(1)}, u32[]{:S(2)}, u32[]{:S(2)}) %all-to-all-start.3) | async-done | bytes 2097184 | tf_op jit(solution)/shard_map/all_to_all | solution.py:644
  460.4 3.9 all-to-all-start.2
  464.4 60.1 %reduce-scatter.10.cloned.1.call-done = bf16[128,2688]{1,0:T(8,128)(2,1)} async-done(((bf16[1024,2688]{1,0:T(8,128)(2,1)}), bf16[128,2688]{1,0:T(8,128)(2,1)}) %reduce-scatter.10.cloned.1.call-update) | async-done | bytes 688144 | tf_op jit(solution)/shard_map/reduce_scatter | solution.py:677
  524.5 61.3 %reduce-scatter.12.cloned.1.call-done = bf16[128,2688]{1,0:T(8,128)(2,1)} async-done(((bf16[1024,2688]{1,0:T(8,128)(2,1)}), bf16[128,2688]{1,0:T(8,128)(2,1)}) %reduce-scatter.12.cloned.1.call-update) | async-done | bytes 688144 | tf_op jit(solution)/shard_map/reduce_scatter | solution.py:677
  585.8 65.5 %reduce-scatter.6.cloned.1.call-done = bf16[128,3072]{1,0:T(8,128)(2,1)} async-done(((bf16[1024,3072]{1,0:T(8,128)(2,1)}), bf16[128,3072]{1,0:T(8,128)(2,1)}) %reduce-scatter.6.cloned.1.call-update) | async-done | bytes 786448 | tf_op jit(solution)/shard_map/reduce_scatter | solution.py:677
  654.1 3.3 shard_map.161
  657.5 117.6 %all-reduce.3.cloned.1.call-done = (bf16[128,3072]{1,0:T(8,128)(2,1)}, bf16[128,1024]{1,0:T(8,128)(2,1)}, bf16[128,2688]{1,0:T(8,128)(2,1)}, bf16[128,2688]{1,0:T(8,128)(2,1)}, bf16[328,1024]{1,0:T(8,128)(2,1)}) async-done(((bf16[128,3072]{1,0:T(8,128)(2,1)}, bf16[128,1024]{1,0:T(8,128)(2,1)}, bf16[128,2688]{1,0:T(8,128)(2,1)}, bf16[128,2688]{1,0:T(8,128)(2,1)}, bf16[328,1024]{1,0:T(8,128)(2,1)}), ...) | async-done | bytes 3096592 | tf_op jit(solution)/shard_map/psum | solution.py:680
  (137 shorter events, 74.6 us)
Async XLA Ops:
  7.2 121.8 %all-gather.5.cloned.1.call-start = ((), (), s32[]{:S(2)}) async-start(), calls=%async_computation.10 | async-start | bytes 7077888 | tf_op jit(solution)/shard_map/all_gather | solution.py:647
  7.9 153.3 %all-gather.7.cloned.1.call-start = ((), (), s32[]{:S(2)}) async-start(), calls=%async_computation.11 | async-start | bytes 2359296 | tf_op jit(solution)/shard_map/all_gather | solution.py:647
  8.7 163.8 %all-gather.11.cloned.1.call-start = ((), (), s32[]{:S(2)}) async-start(), calls=%async_computation.13 | async-start | bytes 6045696 | tf_op jit(solution)/shard_map/all_gather | solution.py:647
  9.4 222.4 %all-gather.9.cloned.1.call-start = ((), (), s32[]{:S(2)}) async-start(), calls=%async_computation.12 | async-start | bytes 12386304 | tf_op jit(solution)/shard_map/all_gather | solution.py:647
  14.7 56.3 %all-to-all-start.1 = ((bf16[32,2,16,1024]{3,2,1,0:T(8,128)(2,1)}), bf16[32,2,16,1024]{3,2,1,0:T(8,128)(2,1)S(1)}, u32[]{:S(2)}, u32[]{:S(2)}) async-start(bf16[32,2,16,1024]{3,2,1,0:T(8,128)(2,1)} %shard_map.157), calls=%async_computation.1 | async-start | bytes 4194304 | tf_op jit(solution)/shard_map/all_to_all | solution.py:644
  25.9 49.9 %copy-start.32 = (bf16[128]{0:T(256)(128)(2,1)S(1)}, bf16[128]{0:T(256)(128)(2,1)}, u32[]{:S(2)}) copy-start(bf16[128]{0:T(256)(128)(2,1)} %param.17) | copy-start | bytes 772
  25.9 49.9 %copy-start.33 = (bf16[128]{0:T(256)(128)(2,1)S(1)}, bf16[128]{0:T(256)(128)(2,1)}, u32[]{:S(2)}) copy-start(bf16[128]{0:T(256)(128)(2,1)} %param.16) | copy-start | bytes 772
  71.0 53.0 %all-to-all-start = ((bf16[32,2,16,1024]{3,2,1,0:T(8,128)(2,1)}), bf16[32,2,16,1024]{3,2,1,0:T(8,128)(2,1)}, u32[]{:S(2)}, u32[]{:S(2)}) async-start(bf16[32,2,16,1024]{3,2,1,0:T(8,128)(2,1)} %shard_map.152), calls=%async_computation | async-start | bytes 4194304 | tf_op jit(solution)/shard_map/all_to_all | solution.py:644
  75.1 389.2 %reduce-scatter.8.cloned.1.call-start = ((), (), s32[]{:S(2)}) async-start(), calls=%async_computation.15 | async-start | bytes 2359296 | tf_op jit(solution)/shard_map/reduce_scatter | solution.py:677
  161.2 7.9 copy-start.17
  231.8 83.9 %copy-start.10 = (bf16[1024,1024]{1,0:T(8,128)(2,1)S(1)}, bf16[1024,1024]{1,0:T(8,128)(2,1)}, u32[]{:S(2)}) copy-start(bf16[1024,1024]{1,0:T(8,128)(2,1)} %copy-done.9) | copy-start | bytes 6291460
  331.7 132.7 %reduce-scatter.14.cloned.1.call-start = ((), (), s32[]{:S(2)}) async-start(), calls=%async_computation.18 | async-start | bytes 6045696 | tf_op jit(solution)/shard_map/reduce_scatter | solution.py:677
  332.3 192.2 %reduce-scatter.10.cloned.1.call-start = ((), (), s32[]{:S(2)}) async-start(), calls=%async_computation.16 | async-start | bytes 6193152 | tf_op jit(solution)/shard_map/reduce_scatter | solution.py:677
  333.0 252.8 %reduce-scatter.12.cloned.1.call-start = ((), (), s32[]{:S(2)}) async-start(), calls=%async_computation.17 | async-start | bytes 6193152 | tf_op jit(solution)/shard_map/reduce_scatter | solution.py:677
  333.8 317.6 %reduce-scatter.6.cloned.1.call-start = ((), (), s32[]{:S(2)}) async-start(), calls=%async_computation.14 | async-start | bytes 7077888 | tf_op jit(solution)/shard_map/reduce_scatter | solution.py:677
  334.6 2.9 copy-start.1
  340.0 24.9 %copy-start.26 = (bf16[1024,1024]{1,0:T(8,128)(2,1)S(1)}, bf16[1024,1024]{1,0:T(8,128)(2,1)}, u32[]{:S(2)}) copy-start(bf16[1024,1024]{1,0:T(8,128)(2,1)} %copy-done.25) | copy-start | bytes 6291460
  397.4 11.3 %all-to-all-start.4 = ((f32[2,32,128]{2,0,1:T(2,128)}), f32[2,32,128]{2,0,1:T(2,128)S(1)}, u32[]{:S(2)}, u32[]{:S(2)}) async-start(f32[2,32,128]{2,0,1:T(2,128)} %bitcast.12), calls=%async_computation.4 | async-start | bytes 65536 | tf_op jit(solution)/shard_map/all_to_all | solution.py:702
  408.6 51.8 %all-to-all-start.3 = ((bf16[32,2,16,1024]{3,2,1,0:T(8,128)(2,1)}), bf16[32,2,16,1024]{3,2,1,0:T(8,128)(2,1)S(1)}, u32[]{:S(2)}, u32[]{:S(2)}) async-start(bf16[32,2,16,1024]{3,2,1,0:T(8,128)(2,1)} %copy-done.3), calls=%async_computation.3 | async-start | bytes 4194304 | tf_op jit(solution)/shard_map/all_to_all | solution.py:644
  460.4 193.7 %all-to-all-start.2 = ((bf16[32,2,16,1024]{3,2,1,0:T(8,128)(2,1)}), bf16[32,2,16,1024]{3,2,1,0:T(8,128)(2,1)}, u32[]{:S(2)}, u32[]{:S(2)}) async-start(bf16[32,2,16,1024]{3,2,1,0:T(8,128)(2,1)} %copy-done.2), calls=%async_computation.2 | async-start | bytes 4194304 | tf_op jit(solution)/shard_map/all_to_all | solution.py:644
  464.3 310.8 %all-reduce.3.cloned.1.call-start = ((), (), s32[]{:S(2)}) async-start(), calls=%async_computation.19 | async-start | bytes 6193152 | tf_op jit(solution)/shard_map/psum | solution.py:680
  775.1 4.4 copy-start.30
  777.0 3.8 copy-start.28
  777.0 3.8 copy-start.29
  (25 other events, 46.3 us)
Sparse Core Ops, SparseCore 0:
  9.9 70.1 all-gather.4
  82.0 38.1 all-gather.6
  122.1 41.8 all-gather.10
  166.3 65.4 all-gather.8
  331.8 41.2 reduce-scatter.7
  376.8 73.3 reduce-scatter.13
  454.0 70.4 reduce-scatter.9
  527.9 57.8 reduce-scatter.11
  589.5 61.7 reduce-scatter.5
  653.9 121.0 all-reduce.2

commit v2 on v1

--- a/solution.py
+++ b/solution.py
@@ -35,6 +35,8 @@
 FF_PAD = FF_STEPS * FF_TILE
 ROW_CHUNK = 256
 CHUNK_ROWS = 16
+SHARDS = 8
+REPLICAS = 4
 
 F32 = jnp.float32
 BF16 = jnp.bfloat16
@@ -389,20 +391,17 @@
     act_ref,
     top_ref,
     mid_ref,
-    gelu_w_ref,
-    line_w_ref,
+    in_ref,
     down_ref,
     layer_ref,
     grad_b_ref,
-    grad_gelu_ref,
-    grad_line_ref,
+    grad_in_ref,
     grad_down_ref,
     total,
     act_t,
     down_clean,
     kept_c,
-    kept_gelu,
-    kept_line,
+    kept_gu,
 ):
     step = pl.program_id(0)
 
@@ -418,27 +417,22 @@
     def rows_step(index, carry):
         rows = pl.ds(pl.multiple_of(index * ROW_CHUNK, ROW_CHUNK), ROW_CHUNK)
         act, top = act_ref[rows, :], top_ref[rows, :]
-        gelu_in = dot(act, gelu_w_ref[...])
-        linear = dot(act, line_w_ref[...])
+        gate_up = dot(act, in_ref[...])
+        gelu_in, linear = gate_up[:, :FF_TILE], gate_up[:, FF_TILE:]
         grad_c = dot(top, down_clean[...], 1, 1)
         phi = 0.5 * (1.0 + lax.erf(gelu_in * ROOT_HALF))
         gelu_out = gelu_in * phi
         slope = phi + gelu_in * (jnp.exp(-0.5 * gelu_in * gelu_in) * INV_ROOT_TWO_PI)
         act_c = (gelu_out * linear).astype(BF16)
-        grad_gelu = (grad_c * linear * slope).astype(BF16)
-        grad_line = (grad_c * gelu_out).astype(BF16)
         kept_c[rows, :] = act_c
-        kept_gelu[rows, :] = grad_gelu
-        kept_line[rows, :] = grad_line
+        kept_gu[rows, :FF_TILE] = (grad_c * linear * slope).astype(BF16)
+        kept_gu[rows, FF_TILE:] = (grad_c * gelu_out).astype(BF16)
         total[rows, :] += dot(act_c, down_clean[...])
-        grad_b_ref[rows, :] += dot(grad_gelu, gelu_w_ref[...], 1, 1) + dot(
-            grad_line, line_w_ref[...], 1, 1
-        )
+        grad_b_ref[rows, :] += dot(kept_gu[rows, :], in_ref[...], 1, 1)
         return carry
 
     lax.fori_loop(0, ROWS // ROW_CHUNK, rows_step, 0)
-    grad_gelu_ref[...] = dot(act_t[...], kept_gelu[...]).astype(BF16)
-    grad_line_ref[...] = dot(act_t[...], kept_line[...]).astype(BF16)
+    grad_in_ref[...] = dot(act_t[...], kept_gu[...]).astype(BF16)
     grad_down_ref[...] = dot(kept_c[...], top_ref[...], 0, 0).astype(BF16)
 
     @pl.when(step == FF_STEPS - 1)
@@ -448,7 +442,7 @@
 
 def ffn(act, top, middle, full_in, full_down):
     whole = pl.BlockSpec((ROWS, D), lambda j: (0, 0))
-    tall = pl.BlockSpec((D, FF_TILE), lambda j: (0, j))
+    tall = pl.BlockSpec((D, 2 * FF_TILE), lambda j: (0, j))
     wide = pl.BlockSpec((FF_TILE, D), lambda j: (j, 0))
     return pl.pallas_call(
         ffn_kernel,
@@ -458,15 +452,13 @@
             whole,
             whole,
             tall,
-            pl.BlockSpec((D, FF_TILE), lambda j: (0, j + FF_STEPS)),
             wide,
         ],
-        out_specs=[whole, whole, tall, tall, wide],
+        out_specs=[whole, whole, tall, wide],
         out_shape=[
             jax.ShapeDtypeStruct((ROWS, D), BF16),
             jax.ShapeDtypeStruct((ROWS, D), F32),
-            jax.ShapeDtypeStruct((D, FF_PAD), BF16),
-            jax.ShapeDtypeStruct((D, FF_PAD), BF16),
+            jax.ShapeDtypeStruct((D, 2 * FF_PAD), BF16),
             jax.ShapeDtypeStruct((FF, D), BF16),
         ],
         scratch_shapes=[
@@ -474,12 +466,11 @@
             pltpu.VMEM((D, ROWS), BF16),
             pltpu.VMEM((FF_TILE, D), BF16),
             pltpu.VMEM((ROWS, FF_TILE), BF16),
-            pltpu.VMEM((ROWS, FF_TILE), BF16),
-            pltpu.VMEM((ROWS, FF_TILE), BF16),
+            pltpu.VMEM((ROWS, 2 * FF_TILE), BF16),
         ],
         compiler_params=params(60),
         cost_estimate=cost(18 * ROWS * D * FF, 12 * D * FF, 2 * ROWS * FF),
-    )(act, top, middle, full_in, full_in, full_down)
+    )(act, top, middle, full_in, full_down)
 
 
 def branch_kernel(
@@ -525,7 +516,11 @@
     return pl.pallas_call(
         branch_kernel,
         grid=(ROWS // ROW_CHUNK,),
-        in_specs=[tile, tile, tile, tile, square, line],
+        in_specs=[
+            *[tile] * 4,
+            square,
+            line,
+        ],
         out_specs=[tile, tile, square, line],
         out_shape=[
             jax.ShapeDtypeStruct((ROWS, D), F32),
@@ -599,6 +594,239 @@
         compiler_params=params(32),
         cost_estimate=cost(6 * ROWS * D * D, 2 * (7 * D * D)),
     )(act, grad_qkv)
+
+
+MESH = pl.DeviceIdType.MESH
+REDUCE_CHUNKS = (
+    (0, 0, 512),
+    (0, 512, 512),
+    (1, 0, 1792),
+    (1, 1792, 1792),
+    (1, 3584, 1792),
+    (2, 0, 1024),
+    (3, 0, 1536),
+    (3, 1536, 1536),
+)
+HOP_CORE, HOP_X, HOP_Y, HOP_XY, HOP_YX, HOP_IN, HOP_MID, HOP_OUT = range(8)
+
+
+def place():
+    rep, grp = lax.axis_index("rep"), lax.axis_index("grp")
+    core, x, y = grp % 2, grp // 2 % 2, grp // 4
+    return rep, grp, core, x, y, grp + 1 - 2 * core, grp + 2 - 4 * x, grp + 4 - 8 * y
+
+
+def reduce_kernel(*refs):
+    tensors, refs = refs[:4], refs[4:]
+    outs, refs = refs[:4], refs[4:]
+    chunks = len(REDUCE_CHUNKS)
+    sums, from_core, from_near, from_cross, from_far = (
+        refs[i * chunks : (i + 1) * chunks] for i in range(5)
+    )
+    load_sem, send_sem, recv_sem, store_sem = refs[5 * chunks :]
+    rep, grp, core, x, y, by_core, by_x, by_y = place()
+    is_middle = (rep == 1) | (rep == 2)
+    inward, outward, across = 1 + rep // 2, 3 * (rep // 2), 3 - rep
+
+    barrier = pltpu.get_barrier_semaphore()
+    for near in (by_core, by_x, by_y):
+        pl.semaphore_signal(barrier, device_id=(rep, near), device_id_type=MESH)
+
+    @pl.when(is_middle)
+    def _():
+        pl.semaphore_signal(barrier, device_id=(across, grp), device_id_type=MESH)
+        pl.semaphore_signal(barrier, device_id=(outward, grp), device_id_type=MESH)
+        pl.semaphore_wait(barrier, 5)
+
+    @pl.when(jnp.logical_not(is_middle))
+    def _():
+        pl.semaphore_signal(barrier, device_id=(inward, grp), device_id_type=MESH)
+        pl.semaphore_wait(barrier, 4)
+
+    def hop(chunk, which):
+        tensor, start, width = REDUCE_CHUNKS[chunk]
+        half = width // 2
+        left, right, columns = pl.ds(0, half), pl.ds(half, half), pl.ds(start, width)
+        total, far = sums[chunk], from_far[chunk]
+        near, cross = from_near[chunk], from_cross[chunk]
+        if which == HOP_CORE:
+            source, target = tensors[tensor].at[:, :, 1 - core, :, columns], from_core[chunk]
+        elif which == HOP_X:
+            source, target = total.at[:, 1 - x, :, left], near.at[0]
+        elif which == HOP_Y:
+            source, target = total.at[1 - y, :, :, right], near.at[1]
+        elif which == HOP_XY:
+            source, target = total.at[1 - y, x, :, left], cross.at[0]
+        elif which == HOP_YX:
+            source, target = total.at[y, 1 - x, :, right], cross.at[1]
+        elif which == HOP_IN:
+            source, target = total.at[y, x], far.at[0]
+        elif which == HOP_MID:
+            source, target = total.at[y, x], far.at[1]
+        else:
+            source, target = far.at[0], outs[tensor].at[:, columns]
+        to_rep = (rep, rep, rep, rep, rep, inward, across, outward)[which]
+        to_grp = (by_core, by_x, by_y, by_y, by_x, grp, grp, grp)[which]
+        return pltpu.make_async_remote_copy(
+            src_ref=source,
+            dst_ref=target,
+            send_sem=send_sem.at[chunk, which],
+            recv_sem=recv_sem.at[chunk, which],
+            device_id=(to_rep, to_grp),
+            device_id_type=MESH,
+        )
+
+    def load(chunk):
+        tensor, start, width = REDUCE_CHUNKS[chunk]
+        return pltpu.make_async_copy(
+            tensors[tensor].at[:, :, core, :, pl.ds(start, width)],
+            sums[chunk],
+            load_sem.at[chunk],
+        )
+
+    def store(chunk):
+        tensor, start, width = REDUCE_CHUNKS[chunk]
+        return pltpu.make_async_copy(
+            from_far[chunk].at[0],
+            outs[tensor].at[:, pl.ds(start, width)],
+            store_sem.at[chunk],
+        )
+
+    def add(one, other):
+        return (one.astype(F32) + other.astype(F32)).astype(BF16)
+
+    def after_core(chunk):
+        load(chunk).wait()
+        hop(chunk, HOP_CORE).wait_recv()
+        total = sums[chunk]
+
+        def plane(index, carry):
+            row, column = index // 2, index % 2
+            total[row, column] = add(total[row, column], from_core[chunk][row, column])
+            return carry
+
+        lax.fori_loop(0, 4, plane, 0)
+        hop(chunk, HOP_X).start()
+        hop(chunk, HOP_Y).start()
+
+    def after_near(chunk):
+        half = REDUCE_CHUNKS[chunk][2] // 2
+        hop(chunk, HOP_X).wait_recv()
+        hop(chunk, HOP_Y).wait_recv()
+        total, near = sums[chunk], from_near[chunk]
+
+        def plane(index, carry):
+            total[index, x, :, :half] = add(total[index, x, :, :half], near[0, index])
+            total[y, index, :, half:] = add(total[y, index, :, half:], near[1, index])
+            return carry
+
+        lax.fori_loop(0, 2, plane, 0)
+        hop(chunk, HOP_XY).start()
+        hop(chunk, HOP_YX).start()
+
+    def after_cross(chunk):
+        half = REDUCE_CHUNKS[chunk][2] // 2
+        hop(chunk, HOP_XY).wait_recv()
+        hop(chunk, HOP_YX).wait_recv()
+        total, cross = sums[chunk], from_cross[chunk]
+        total[y, x, :, :half] = add(total[y, x, :, :half], cross[0])
+        total[y, x, :, half:] = add(total[y, x, :, half:], cross[1])
+
+        @pl.when(jnp.logical_not(is_middle))
+        def _():
+            hop(chunk, HOP_IN).start()
+
+    def after_in(chunk):
+        @pl.when(is_middle)
+        def _():
+            hop(chunk, HOP_IN).wait_recv()
+            total = sums[chunk]
+            total[y, x] = add(total[y, x], from_far[chunk][0])
+            hop(chunk, HOP_MID).start()
+
+    def after_middle(chunk):
+        @pl.when(is_middle)
+        def _():
+            hop(chunk, HOP_MID).wait_recv()
+            far = from_far[chunk]
+            far[0] = add(sums[chunk][y, x], far[1])
+            hop(chunk, HOP_OUT).start()
+            store(chunk).start()
+
+    for chunk in range(chunks):
+        load(chunk).start()
+        hop(chunk, HOP_CORE).start()
+    stages = (after_core, after_near, after_cross, after_in, after_middle)
+    for step in range(chunks + len(stages) - 1):
+        for late, stage in enumerate(stages):
+            if 0 <= step - late < chunks:
+                stage(step - late)
+    for chunk in range(chunks):
+        for which in (HOP_CORE, HOP_X, HOP_Y, HOP_XY, HOP_YX):
+            hop(chunk, which).wait_send()
+
+    @pl.when(is_middle)
+    def _():
+        for chunk in range(chunks):
+            hop(chunk, HOP_MID).wait_send()
+            hop(chunk, HOP_OUT).wait_send()
+            store(chunk).wait()
+
+    @pl.when(jnp.logical_not(is_middle))
+    def _():
+        for chunk in range(chunks):
+            hop(chunk, HOP_IN).wait_send()
+            hop(chunk, HOP_OUT).wait_recv()
+
+
+def reduce_all(parts):
+    split = [part.reshape(2, 2, 2, -1, part.shape[1]) for part in parts]
+    shapes = [(v.shape[3], width) for v, width in ((split[t], w) for t, _, w in REDUCE_CHUNKS)]
+    anywhere = pl.BlockSpec(memory_space=pl.ANY)
+    chunks = len(REDUCE_CHUNKS)
+    moved = sum(v.size for v in split)
+    return pl.pallas_call(
+        reduce_kernel,
+        in_specs=[anywhere] * 4,
+        out_specs=[anywhere] * 4,
+        out_shape=[jax.ShapeDtypeStruct(v.shape[3:], BF16) for v in split],
+        scratch_shapes=[
+            *[pltpu.VMEM((2, 2, r, w), BF16) for r, w in shapes],
+            *[pltpu.VMEM((2, 2, r, w), BF16) for r, w in shapes],
+            *[pltpu.VMEM((2, 2, r, w // 2), BF16) for r, w in shapes],
+            *[pltpu.VMEM((2, r, w // 2), BF16) for r, w in shapes],
+            *[pltpu.VMEM((2, r, w), BF16) for r, w in shapes],
+            pltpu.SemaphoreType.DMA((chunks,)),
+            pltpu.SemaphoreType.DMA((chunks, 8)),
+            pltpu.SemaphoreType.DMA((chunks, 8)),
+            pltpu.SemaphoreType.DMA((chunks,)),
+        ],
+        compiler_params=pltpu.CompilerParams(
+            vmem_limit_bytes=60 * MIB, collective_id=1, has_side_effects=True
+        ),
+        cost_estimate=cost(2 * moved, 40 * moved),
+    )(*split)
+
+
+def weave(weight):
+    rows = weight.shape[0]
+    gap = jnp.zeros((rows, FF_PAD - FF), weight.dtype)
+    parts = [jnp.concatenate([weight[:, i * FF : (i + 1) * FF], gap], 1) for i in range(2)]
+    tiles = [
+        parts[half][:, step * FF_TILE : (step + 1) * FF_TILE]
+        for step in range(FF_STEPS)
+        for half in range(2)
+    ]
+    return jnp.concatenate(tiles, axis=1)
+
+
+def unweave(woven):
+    tiles = [
+        woven[:, (2 * step + half) * FF_TILE :][:, : min(FF_TILE, FF - step * FF_TILE)]
+        for half in range(2)
+        for step in range(FF_STEPS)
+    ]
+    return jnp.concatenate(tiles, axis=1)
 
 
 def plan(seq_lengths, device, devices, micros):
@@ -646,6 +874,7 @@
     def gather(rows):
         return lax.all_gather(rows, "grp", axis=0, tiled=True)
 
+    near = group_size == SHARDS and devices == REPLICAS * SHARDS
     want, starts, lengths, given = plan(seq_lengths, device, devices, micros)
     token_rows = swap(pack_rows(tokens[:, :, 0], want, devices, micros))
     top_rows = swap(pack_rows(cotangent[:, :, 0], want, devices, micros))
@@ -654,8 +883,7 @@
     gain_two = gains[1:].astype(F32)
     full_qkv = gather(w_qkv)
     full_out = gather(w_out)
-    gap = jnp.zeros((w_in.shape[0], FF_PAD - FF), BF16)
-    full_in = gather(jnp.concatenate([w_in[:, :FF], gap, w_in[:, FF:], gap], axis=1))
+    full_in = gather(weave(w_in))
     full_down = gather(w_down)
 
     cosine, sine = rotary_tables(QKV_TILE)
@@ -668,31 +896,30 @@
     qkv = qkv_rows(act_a, full_qkv, cosine, sine)
     attn_o, prob = attend(qkv, lengths)
     middle, act_b = middle_rows(attn_o, hidden, full_out, gain_two)
-    layer_rows, grad_b, grad_gelu_w, grad_line_w, grad_down_w = ffn(
+    layer_rows, grad_b, grad_in_w, grad_down_w = ffn(
         act_b, top, middle, full_in, full_down
     )
     layer_back = swap(repack_rows(layer_rows, starts, lengths, given, devices, micros))
 
-    def owned(part):
-        return lax.psum_scatter(part, "grp", scatter_dimension=0, tiled=True)
-
-    def summed(part):
-        return lax.psum(part, "rep")
-
-    grad_down = summed(owned(grad_down_w))
-    grad_gelu = summed(owned(grad_gelu_w))
-    grad_line = summed(owned(grad_line_w))
+
     grad_mid, grad_o, grad_out_w, grad_gain_two = branch_back(
         grad_b, middle, top, attn_o, full_out, gain_two
     )
-    grad_out = summed(owned(grad_out_w))
     grad_qkv_rows = attend_back(qkv, grad_o, prob, cosine[:, :LANES], sine[:, :LANES])
     grad_qkv_w = qkv_grad(act_a, grad_qkv_rows)
-    grad_qkv = summed(owned(grad_qkv_w))
     grad_rows, grad_gain_one = input_back(
         grad_qkv_rows, full_qkv, hidden, grad_mid, gain_one
     )
     grad_back = swap(repack_rows(grad_rows, starts, lengths, given, devices, micros))
+    parts = (grad_down_w, grad_in_w, grad_out_w, grad_qkv_w)
+    if near:
+        owned = reduce_all(parts)
+    else:
+        owned = [
+            lax.psum(lax.psum_scatter(v, "grp", scatter_dimension=0, tiled=True), "rep")
+            for v in parts
+        ]
+    grad_down, grad_in, grad_out, grad_qkv = (v.astype(F32) for v in owned)
     gain_parts = jnp.concatenate([grad_gain_one, grad_gain_two], axis=0)
     gain_parts = gain_parts.reshape(2, 1, group_size, -1)
     gain_parts = jnp.broadcast_to(
@@ -708,10 +935,10 @@
         grad_tokens,
         gain_sums[0],
         gain_sums[1],
-        grad_qkv.astype(F32),
-        grad_out.astype(F32),
-        jnp.concatenate([grad_gelu[:, :FF], grad_line[:, :FF]], axis=1).astype(F32),
-        grad_down.astype(F32),
+        grad_qkv,
+        grad_out,
+        unweave(grad_in),
+        grad_down,
     )
 
 

time: 790 us -> 623 us (0.79)
  waiting for transfers between devices: 489 us -> 169 us
  Pallas kernels: 194 us -> 332 us
  local copies, waits for them, and re-layouts: 45.4 us -> 54 us
    reduce_scatter x5 -> x0, waiting for transfers between devices: 187 us -> none  [owned(): return lax.psum_scatter(part, 'grp', scatter_dimension=0, tiled=True)]
    pallas_call x1 -> x2, Pallas kernels: 11.4 us -> 162 us  [the longest x1 151 us: reduce_all(): pl.pallas_call(reduce_kernel, in_specs=[anywhere] * 4, out_specs=[anywher...]
    psum x1 -> x0, waiting for transfers between devices: 118 us -> none  [summed(): return lax.psum(part, 'rep')]
    pallas_call x1, Pallas kernels: 83.9 us -> 73 us  [ffn(): pl.pallas_call(ffn_kernel, grid=(FF_STEPS,), in_specs=[whole, whole, whol...]
    unnamed x68 -> x80, local copies, waits for them, and re-layouts: 41.6 us -> 45.2 us
  transfers between devices with their start and end apart: 15 -> 9, of which waited for: 9 -> 5; matrix products, arithmetic and copies ran while one was open for 1% -> 4% of each run, Pallas kernels for 12% -> 33%
where the time goes in v2:
time: 623 us; the launch traced here: 622 us
  Pallas kernels  332 us (53%)
  waiting for transfers between devices  169 us (27%)
  local copies, waits for them, and re-layouts  54 us (9%)
  starting transfers between devices  22.8 us (4%)
  blocking collectives  22.3 us (4%)
  between operations  14.3 us (2%)
  other arithmetic  6.94 us (1%)
    pallas_call x1, Pallas kernels, reduce_all(): pl.pallas_call(reduce_kernel, in_specs=[anywhere] * 4, out_specs=[anywher...  151 us
    all_to_all x4, waiting for transfers between devices, swap(): return lax.all_to_all(rows, both, split_axis=0, concat_axis=0, tiled=True)  111 us
    pallas_call x1, Pallas kernels, ffn(): pl.pallas_call(ffn_kernel, grid=(FF_STEPS,), in_specs=[whole, whole, whol...  73 us
    all_gather x4, waiting for transfers between devices, gather(): return lax.all_gather(rows, 'grp', axis=0, tiled=True)  52.5 us
    unnamed x80, local copies, waits for them, and re-layouts  45.2 us
    pallas_call x1, Pallas kernels, attend_back(): pl.pallas_call(attend_back_kernel, grid=(BLOCKS,), in_specs=[pl.BlockSpec...  25 us
    all_gather x1, blocking collectives, body(): lax.all_gather(jnp.stack([attn_gain, mlp_gain]), 'grp', axis=1, tiled=True)  22.3 us
    all_to_all x4, starting transfers between devices, swap(): return lax.all_to_all(rows, both, split_axis=0, concat_axis=0, tiled=True)  18.1 us
  transfers between devices with their start and end apart: 9, of which 5 were waited for; matrix products, arithmetic and copies ran while one was open for 4% of the time, Pallas kernels for 33%

profile of v2, /device:TPU:0, one launch (start us, length us, event | category | flops | bytes accessed | tf_op | source)
XLA Modules:
  0.0 622.0 jit_solution(3653971883817883929)
XLA Ops:
  23.3 7.3 %all-to-all-start.1 = ((bf16[32,2,16,1024]{3,2,1,0:T(8,128)(2,1)}), bf16[32,2,16,1024]{3,2,1,0:T(8,128)(2,1)S(1)}, u32[]{:S(2)}, u32[]{:S(2)}) async-start(bf16[32,2,16,1024]{3,2,1,0:T(8,128)(2,1)} %shard_map.157), calls=%async_computation.1 | async-start | bytes 4194304 | tf_op jit(solution)/shard_map/all_to_all | solution.py:872
  34.5 45.1 %all-to-all-done.1.arrived_ref = bf16[32,2,16,1024]{3,2,1,0:T(8,128)(2,1)S(1)} async-done(((bf16[32,2,16,1024]{3,2,1,0:T(8,128)(2,1)}), bf16[32,2,16,1024]{3,2,1,0:T(8,128)(2,1)S(1)}, u32[]{:S(2)}, u32[]{:S(2)}) %all-to-all-start.1) | async-done | bytes 2097184 | tf_op jit(solution)/shard_map/all_to_all | solution.py:872
  79.7 4.0 all-to-all-start
  84.5 22.3 %all_gather.15 = bf16[2,1024]{1,0:T(2,128)(2,1)S(1)} all-gather(bf16[2,128]{1,0:T(2,128)(2,1)S(1)} %pad_maximum_fusion.2), channel_id=1, replica_groups=mesh['rep'=4,'grp'=8] {'grp'}, dimensions={1}, use_global_device_ids=true | all-gather | bytes 4608 | tf_op jit(solution)/shard_map/all_gather | solution.py:881
  110.3 22.4 %all-to-all-done.arrived_ref = bf16[32,2,16,1024]{3,2,1,0:T(8,128)(2,1)} async-done(((bf16[32,2,16,1024]{3,2,1,0:T(8,128)(2,1)}), bf16[32,2,16,1024]{3,2,1,0:T(8,128)(2,1)}, u32[]{:S(2)}, u32[]{:S(2)}) %all-to-all-start) | async-done | bytes 2097184 | tf_op jit(solution)/shard_map/all_to_all | solution.py:872
  132.7 3.6 shard_map.153
  137.7 15.8 %shard_map.154.q_ref.k_ref.v_ref = bf16[1024,3072]{1,0:T(8,128)(2,1)S(1)} custom-call(bf16[1024,1024]{1,0:T(8,128)(2,1)S(1)} %get-tuple-element.28.act_ref, bf16[1024,3072]{1,0:T(8,128)(2,1)} %all-gather.5.cloned.1.call-done.weight_ref, f32[128,512]{1,0:T(8,128)S(1)} %copy.34.cos_ref, f32[128,512]{1,0:T(8,128)S(1)} %copy.35.sin_ref), custom_call_target="tpu_custom_call" | custom-call | flops 6442450944 | bytes 14680064 | tf_op jit(solution)/shard_map/pallas_call | solution.py:241
  154.8 10.4 %shard_map.155 = (bf16[1024,1024]{1,0:T(8,128)(2,1)S(1)}, bf16[8,8,128,256]{3,2,1,0:T(8,128)(2,1)S(1)}) custom-call(s32[4,2]{1,0:T(4,128)S(1)} %copy.40.length_ref, bf16[1024,3072]{1,0:T(8,128)(2,1)S(1)} %shard_map.154.q_ref.k_ref.v_ref, bf16[1024,3072]{1,0:T(8,128)(2,1)S(1)} %shard_map.154.q_ref.k_ref.v_ref, bf16[1024,3072]{1,0:T(8,128)(2,1)S(1)} %shard_map.154.q_ref.k_ref.v_ref), custom_call_target="tpu_custom_call" | custom-call | flops 1073741824 | bytes 12582912 | tf_op jit(solution)/shard_map/pallas_call | solution.py:286
  173.7 3.9 shard_map.156
  181.1 52.5 %all-gather.9.cloned.1.call-done.in_ref = bf16[1024,5376]{1,0:T(8,128)(2,1)} async-done(((bf16[128,5376]{1,0:T(8,128)(2,1)}), bf16[1024,5376]{1,0:T(8,128)(2,1)}) %all-gather.9.cloned.1.call-update) | async-done | bytes 11010064 | tf_op jit(solution)/shard_map/all_gather | solution.py:875
  233.5 73.0 %shard_map.159 = (bf16[1024,1024]{1,0:T(8,128)(2,1)}, f32[1024,1024]{1,0:T(8,128)}, bf16[1024,5376]{1,0:T(8,128)(2,1)}, bf16[2624,1024]{1,0:T(8,128)(2,1)}) custom-call(bf16[1024,1024]{1,0:T(8,128)(2,1)} %copy-done.23, bf16[1024,1024]{1,0:T(8,128)(2,1)} %copy-done.10, f32[1024,1024]{1,0:T(8,128)} %copy-done.18, ...), custom_call_target="tpu_custom_call" | custom-call | flops 49526341632 | bytes 32243712 | tf_op jit(solution)/shard_map/pallas_call | solution.py:447
  310.0 11.0 %shard_map.162 = (f32[1024,1024]{1,0:T(8,128)}, bf16[1024,1024]{1,0:T(8,128)(2,1)S(1)}, bf16[1024,1024]{1,0:T(8,128)(2,1)S(1)}, f32[1,1024]{1,0:T(1,128)S(1)}) custom-call(f32[1024,1024]{1,0:T(8,128)} %get-tuple-element.34.grad_b_ref, f32[1024,1024]{1,0:T(8,128)} %copy-done.18, bf16[1024,1024]{1,0:T(8,128)(2,1)S(1)} %copy-done.11, ...), custom_call_target="tpu_custom_call" | custom-call | flops 4294967296 | bytes 23068672 | tf_op jit(solution)/shard_map/pallas_call | solution.py:516
  321.0 25.0 %shard_map.163.grad_qkv_ref.grad_ref = bf16[1024,3072]{1,0:T(8,128)(2,1)S(1)} custom-call(bf16[1024,3072]{1,0:T(8,128)(2,1)S(1)} %bitcast.26, bf16[1024,3072]{1,0:T(8,128)(2,1)S(1)} %bitcast.26, bf16[1024,3072]{1,0:T(8,128)(2,1)S(1)} %bitcast.26, bf16[1024,1024]{1,0:T(8,128)(2,1)S(1)} %get-tuple-element.35.grad_ref, bf16[8,8,128,256]{3,2,1,0:T(8,128)(2,1)S(1)} %copy-done.7, ...), custom_call_target="tpu_custom_call" | custom-call | flops 2684354560 | bytes 18874368 | tf_op jit(solution)/shard_map/pallas_call | solution.py:344
  350.3 12.5 %shard_map.164 = (bf16[1024,1024]{1,0:T(8,128)(2,1)S(1)}, f32[1,1024]{1,0:T(1,128)S(1)}) custom-call(bf16[1024,3072]{1,0:T(8,128)(2,1)} %copy-done.4, bf16[1024,3072]{1,0:T(8,128)(2,1)} %all-gather.5.cloned.1.call-done.weight_ref, bf16[1024,1024]{1,0:T(8,128)(2,1)S(1)} %copy-done.22, f32[1024,1024]{1,0:T(8,128)S(1)} %copy-done.19, ...), custom_call_target="tpu_custom_call" | custom-call | flops 6442450944 | bytes 20971520 | tf_op jit(solution)/shard_map/pallas_call | solution.py:555
  363.4 4.6 all-to-all-start.4
  371.6 3.7 all-to-all-done.4
  375.3 2.7 all-to-all-start.3
  383.2 43.7 %all-to-all-done.3.back_ref = bf16[32,2,16,1024]{3,2,1,0:T(8,128)(2,1)S(1)} async-done(((bf16[32,2,16,1024]{3,2,1,0:T(8,128)(2,1)}), bf16[32,2,16,1024]{3,2,1,0:T(8,128)(2,1)S(1)}, u32[]{:S(2)}, u32[]{:S(2)}) %all-to-all-start.3) | async-done | bytes 2097184 | tf_op jit(solution)/shard_map/all_to_all | solution.py:872
  426.9 4.0 all-to-all-start.2
  430.9 2.8 copy-done.5
  435.3 9.0 %shard_map.167 = bf16[1024,3072]{1,0:T(8,128)(2,1)S(1)} custom-call(bf16[1024,1024]{1,0:T(8,128)(2,1)S(1)} %copy-done.25, bf16[1024,3072]{1,0:T(8,128)(2,1)S(1)} %copy-done.5), custom_call_target="tpu_custom_call" | custom-call | flops 6442450944 | bytes 14680064 | tf_op jit(solution)/shard_map/pallas_call | solution.py:584
  447.0 150.8 %shard_map.168 = (bf16[328,1024]{1,0:T(8,128)(2,1)}, bf16[128,5376]{1,0:T(8,128)(2,1)}, bf16[128,1024]{1,0:T(8,128)(2,1)}, bf16[128,3072]{1,0:T(8,128)(2,1)}) custom-call(bf16[2,2,2,328,1024]{4,3,2,1,0:T(8,128)(2,1)} %bitcast.32, bf16[2,2,2,128,5376]{4,3,2,1,0:T(8,128)(2,1)} %bitcast.31, bf16[2,2,2,128,1024]{4,3,2,1,0:T(8,128)(2,1)} %bitcast.28, ...), custom_call_target="tpu_custom_call" | custom-call | flops 24772608 | bytes 495452160 | tf_op jit(solution)/shard_map/pallas_call | solution.py:788
  605.6 3.8 concatenate.27
  612.2 3.3 shard_map.161
  (138 shorter events, 70.6 us)
Async XLA Ops:
  7.2 130.5 %all-gather.5.cloned.1.call-start = ((), (), s32[]{:S(2)}) async-start(), calls=%async_computation.5 | async-start | bytes 7077888 | tf_op jit(solution)/shard_map/all_gather | solution.py:875
  7.9 161.9 %all-gather.7.cloned.1.call-start = ((), (), s32[]{:S(2)}) async-start(), calls=%async_computation.6 | async-start | bytes 2359296 | tf_op jit(solution)/shard_map/all_gather | solution.py:875
  8.7 172.4 %all-gather.11.cloned.1.call-start = ((), (), s32[]{:S(2)}) async-start(), calls=%async_computation.8 | async-start | bytes 6045696 | tf_op jit(solution)/shard_map/all_gather | solution.py:875
  9.4 224.1 %all-gather.9.cloned.1.call-start = ((), (), s32[]{:S(2)}) async-start(), calls=%async_computation.7 | async-start | bytes 12386304 | tf_op jit(solution)/shard_map/all_gather | solution.py:875
  9.7 9.1 %slice-start.2 = ((bf16[128,5248]{1,0:T(8,128)(2,1)}), bf16[128,2688]{1,0:T(8,128)(2,1)S(1)}, s32[]{:S(2)}) async-start(bf16[128,5248]{1,0:T(8,128)(2,1)} %param.14), calls=%async_computation.11 | async-start | bytes 1376256 | tf_op jit(solution)/shard_map/slice.25
  17.4 2.9 copy-start.29
  18.1 2.7 copy-start.12
  23.3 56.3 %all-to-all-start.1 = ((bf16[32,2,16,1024]{3,2,1,0:T(8,128)(2,1)}), bf16[32,2,16,1024]{3,2,1,0:T(8,128)(2,1)S(1)}, u32[]{:S(2)}, u32[]{:S(2)}) async-start(bf16[32,2,16,1024]{3,2,1,0:T(8,128)(2,1)} %shard_map.157), calls=%async_computation.1 | async-start | bytes 4194304 | tf_op jit(solution)/shard_map/all_to_all | solution.py:872
  79.7 53.0 %all-to-all-start = ((bf16[32,2,16,1024]{3,2,1,0:T(8,128)(2,1)}), bf16[32,2,16,1024]{3,2,1,0:T(8,128)(2,1)}, u32[]{:S(2)}, u32[]{:S(2)}) async-start(bf16[32,2,16,1024]{3,2,1,0:T(8,128)(2,1)} %shard_map.152), calls=%async_computation | async-start | bytes 4194304 | tf_op jit(solution)/shard_map/all_to_all | solution.py:872
  165.2 2.6 copy-start
  169.8 7.8 %copy-start.16 = (bf16[1024,1024]{1,0:T(8,128)(2,1)}, bf16[1024,1024]{1,0:T(8,128)(2,1)S(1)}, u32[]{:S(2)}) copy-start(bf16[1024,1024]{1,0:T(8,128)(2,1)S(1)} %get-tuple-element.29.attn_ref) | copy-start | bytes 6291460
  233.5 73.0 %copy-start.11 = (bf16[1024,1024]{1,0:T(8,128)(2,1)S(1)}, bf16[1024,1024]{1,0:T(8,128)(2,1)}, u32[]{:S(2)}) copy-start(bf16[1024,1024]{1,0:T(8,128)(2,1)} %copy-done.10) | copy-start | bytes 6291460
  306.5 14.5 %slice-start = ((s8[6291456]{0:T(1024)(128)(4,1)}), s8[4194304]{0:T(1024)(128)(4,1)S(1)}, s32[]{:S(2)}) async-start(s8[6291456]{0:T(1024)(128)(4,1)} %bitcast.25), calls=%async_computation.9 | async-start | bytes 8388608
  310.0 11.0 %slice-start.1 = ((s8[6291456]{0:T(1024)(128)(4,1)}), s8[2097152]{0:T(1024)(128)(4,1)S(1)}, s32[]{:S(2)}) async-start(s8[6291456]{0:T(1024)(128)(4,1)} %bitcast.25), calls=%async_computation.10 | async-start | bytes 4194304
  310.0 11.0 %copy-start.7 = (bf16[8,8,128,256]{3,2,1,0:T(8,128)(2,1)S(1)}, bf16[8,8,128,256]{3,2,1,0:T(8,128)(2,1)}, u32[]{:S(2)}) copy-start(bf16[8,8,128,256]{3,2,1,0:T(8,128)(2,1)} %copy-done.6) | copy-start | bytes 12582916
  321.0 25.0 %copy-start.8 = (bf16[1024,1024]{1,0:T(8,128)(2,1)}, bf16[1024,1024]{1,0:T(8,128)(2,1)S(1)}, u32[]{:S(2)}) copy-start(bf16[1024,1024]{1,0:T(8,128)(2,1)S(1)} %get-tuple-element.43) | copy-start | bytes 6291460
  321.0 27.6 %copy-start.19 = (f32[1024,1024]{1,0:T(8,128)S(1)}, f32[1024,1024]{1,0:T(8,128)}, u32[]{:S(2)}) copy-start(f32[1024,1024]{1,0:T(8,128)} %get-tuple-element.37.grad_mid_ref) | copy-start | bytes 12582916
  346.0 2.6 copy-start.4
  363.4 11.9 %all-to-all-start.4 = ((f32[2,32,128]{2,0,1:T(2,128)}), f32[2,32,128]{2,0,1:T(2,128)S(1)}, u32[]{:S(2)}, u32[]{:S(2)}) async-start(f32[2,32,128]{2,0,1:T(2,128)} %bitcast.12), calls=%async_computation.4 | async-start | bytes 65536 | tf_op jit(solution)/shard_map/all_to_all | solution.py:929
  375.3 51.7 %all-to-all-start.3 = ((bf16[32,2,16,1024]{3,2,1,0:T(8,128)(2,1)}), bf16[32,2,16,1024]{3,2,1,0:T(8,128)(2,1)S(1)}, u32[]{:S(2)}, u32[]{:S(2)}) async-start(bf16[32,2,16,1024]{3,2,1,0:T(8,128)(2,1)} %copy-done.2), calls=%async_computation.3 | async-start | bytes 4194304 | tf_op jit(solution)/shard_map/all_to_all | solution.py:872
  426.9 185.3 %all-to-all-start.2 = ((bf16[32,2,16,1024]{3,2,1,0:T(8,128)(2,1)}), bf16[32,2,16,1024]{3,2,1,0:T(8,128)(2,1)}, u32[]{:S(2)}, u32[]{:S(2)}) async-start(bf16[32,2,16,1024]{3,2,1,0:T(8,128)(2,1)} %copy-done.1), calls=%async_computation.2 | async-start | bytes 4194304 | tf_op jit(solution)/shard_map/all_to_all | solution.py:872
  430.9 2.8 copy-start.5
  444.3 2.6 copy-start.3
  599.6 2.5 copy-start.28
  (20 other events, 31.3 us)
Sparse Core Ops, SparseCore 0:
  9.9 62.6 all-gather.4
  74.5 45.5 all-gather.6
  121.9 43.7 all-gather.10
  168.0 65.4 all-gather.8

commit v3 on v2

--- a/solution.py
+++ b/solution.py
@@ -37,6 +37,7 @@
 CHUNK_ROWS = 16
 SHARDS = 8
 REPLICAS = 4
+GAIN_ROWS = 8
 
 F32 = jnp.float32
 BF16 = jnp.bfloat16
@@ -72,14 +73,19 @@
     return inverse * (centred - normal * jnp.mean(grad * normal, axis=-1, keepdims=True))
 
 
-def rotary_tables(width):
+def rotary_tables():
     half = HD // 2
-    frequency = THETA ** (-2.0 * jnp.arange(half, dtype=F32) / HD)
-    angles = jnp.arange(BLK, dtype=F32)[:, None] * frequency[None, :]
-    cosine, sine = jnp.cos(angles), jnp.sin(angles)
-    cosine = jnp.concatenate([cosine, cosine], axis=1)
-    sine = jnp.concatenate([-sine, sine], axis=1)
-    return (jnp.tile(cosine, (1, width // HD)), jnp.tile(sine, (1, width // HD)))
+    frequency = np.float32(THETA) ** (-2.0 * np.arange(half, dtype=np.float32) / HD)
+    angles = np.arange(BLK, dtype=np.float32)[:, None] * frequency.astype(np.float32)[None]
+    cosine, sine = np.cos(angles), np.sin(angles)
+    return (
+        np.concatenate([cosine] * 4, axis=1).astype(np.float32),
+        np.concatenate([-sine, sine] * 2, axis=1).astype(np.float32),
+    )
+
+
+def widen(table):
+    return jnp.concatenate([table] * (QKV_TILE // LANES), axis=1)
 
 
 def turned(values):
@@ -94,129 +100,181 @@
     )
 
 
-def pack_kernel(micros, rows_ref, want_ref, out_ref):
-    total = None
+def position(devices):
+    return lax.axis_index("rep") * (devices // lax.axis_size("rep")) + lax.axis_index("grp")
+
+
+def length_sums(lengths_ref, chosen):
+    return dot(
+        lengths_ref[...].astype(F32).astype(BF16), chosen.astype(F32).astype(BF16)
+    )
+
+
+def slot_grid(sequences, devices):
+    shape = (sequences, devices * CHUNK_ROWS)
+    sequence = lax.broadcasted_iota(jnp.int32, shape, 0)
+    slot = lax.broadcasted_iota(jnp.int32, shape, 1)
+    inner = slot % CHUNK_ROWS
+    pair_cap = CAP // devices
+    return sequence, slot // CHUNK_ROWS, inner % pair_cap, inner // pair_cap
+
+
+def ceil_div(value, count):
+    return jnp.floor((value + (count - 0.5)) * (1.0 / count))
+
+
+def sent_rows(lengths_ref, group, micros, devices):
+    sequence, peer, rank, part = slot_grid(lengths_ref.shape[1], devices)
+    starts = length_sums(lengths_ref, sequence < SEQ_DEV * peer)
+    device = position(devices).astype(F32)
+    wanted = ceil_div(starts - device, devices) + rank[:1].astype(F32)
+    return pick_micros(wanted, part, group, micros, -1.0)
+
+
+def pick_micros(values, part, group, micros, other):
+    micro = lax.broadcasted_iota(jnp.int32, values.shape, 0)
+    rows = []
     for step in range(micros):
-        want = want_ref[step]
-        mine = lax.broadcasted_iota(jnp.int32, (TOK_DEV, want.shape[1]), 0)
-        pick = (mine == want).astype(F32).astype(BF16)
-        term = dot(pick, rows_ref[step], 0, 0)
-        total = term if total is None else total + term
-    out_ref[...] = total.astype(BF16).reshape(out_ref.shape)
-
-
-def pack_rows(rows, want, devices, micros):
+        chosen = jnp.where(micro == group * micros + step, values, 0.0)
+        row = jnp.sum(chosen, axis=0, keepdims=True)
+        rows.append(jnp.where(part[:1] == step, row, other))
+    return rows
+
+
+def held_rows(lengths_ref, group, micros, devices):
+    sequence, peer, rank, part = slot_grid(lengths_ref.shape[1], devices)
+    device = position(devices)
+    first = length_sums(lengths_ref, sequence < SEQ_DEV * device)
+    source = peer[:1].astype(F32)
+    given = (ceil_div(first - source, devices) + rank[:1].astype(F32)) * devices + source
+    parts = [[None] * (CAP // BLK) for _ in range(micros)]
+    for block in range(CAP // BLK):
+        own = SEQ_DEV * device + block
+        start = length_sums(lengths_ref, sequence < own)
+        length = length_sums(lengths_ref, sequence == own)
+        offsets = pick_micros(given - start, part, group, micros, -1.0)
+        limits = pick_micros(length, part, group, micros, 0.0)
+        for step in range(micros):
+            place = lax.broadcasted_iota(jnp.int32, (BLK, part.shape[1]), 0).astype(F32)
+            hit = (place == offsets[step]) & (place < limits[step])
+            parts[step][block] = hit.astype(F32).astype(BF16)
+    return jnp.concatenate([v for blocks in parts for v in blocks], axis=0)
+
+
+def row_match(row):
+    mine = lax.broadcasted_iota(jnp.int32, (TOK_DEV, row.shape[1]), 0).astype(F32)
+    return (mine == row).astype(F32).astype(BF16)
+
+
+def pack_kernel(micros, devices, lengths_ref, *refs):
+    rows = sent_rows(lengths_ref, pl.program_id(0), micros, devices)
+    picks = [row_match(row) for row in rows]
+    count = len(refs) // 2
+    for rows_ref, out_ref in zip(refs[:count], refs[count:]):
+        total = None
+        for step in range(micros):
+            term = dot(picks[step], rows_ref[step], 0, 0)
+            total = term if total is None else total + term
+        out_ref[...] = total.astype(BF16).reshape(out_ref.shape)
+
+
+def pack_rows(lengths, tables, devices, micros):
     groups = MICRO // micros
-    slots = want.shape[-1]
-    return pl.pallas_call(
-        functools.partial(pack_kernel, micros),
+    slots = devices * CHUNK_ROWS
+    count = len(tables)
+    return pl.pallas_call(
+        functools.partial(pack_kernel, micros, devices),
         grid=(groups,),
         in_specs=[
-            pl.BlockSpec((micros, TOK_DEV, D), lambda g: (g, 0, 0)),
-            pl.BlockSpec((micros, 1, slots), lambda g: (g, 0, 0)),
-        ],
-        out_specs=pl.BlockSpec((devices, 1, CHUNK_ROWS, D), lambda g: (0, g, 0, 0)),
-        out_shape=jax.ShapeDtypeStruct((devices, groups, CHUNK_ROWS, D), BF16),
-        compiler_params=params(40),
-        cost_estimate=cost(2 * MICRO * TOK_DEV * slots * D, 4 * groups * slots * D),
-    )(rows, want)
-
-
-def spread_kernel(micros, back_ref, want_ref, out_ref):
+            pl.BlockSpec(lengths.shape, lambda g: (0, 0)),
+            *[pl.BlockSpec((micros, TOK_DEV, D), lambda g: (g, 0, 0))] * count,
+        ],
+        out_specs=[
+            pl.BlockSpec((devices, 1, CHUNK_ROWS, D), lambda g: (0, g, 0, 0))
+        ]
+        * count,
+        out_shape=[jax.ShapeDtypeStruct((devices, groups, CHUNK_ROWS, D), BF16)] * count,
+        compiler_params=params(48),
+        cost_estimate=cost(
+            2 * count * MICRO * TOK_DEV * slots * D, 4 * count * groups * slots * D
+        ),
+    )(lengths, *tables)
+
+
+def spread_kernel(micros, devices, lengths_ref, back_ref, out_ref):
     arrived = back_ref[...].reshape(-1, D)
+    rows = sent_rows(lengths_ref, pl.program_id(0), micros, devices)
     for step in range(micros):
-        want = want_ref[step]
-        mine = lax.broadcasted_iota(jnp.int32, (TOK_DEV, want.shape[1]), 0)
-        pick = (mine == want).astype(F32).astype(BF16)
-        out_ref[step] = dot(pick, arrived).astype(BF16)
-
-
-def spread_rows(back, want, devices, micros):
+        out_ref[step] = dot(row_match(rows[step]), arrived).astype(BF16)
+
+
+def spread_rows(lengths, back, devices, micros):
     groups = MICRO // micros
-    slots = want.shape[-1]
-    return pl.pallas_call(
-        functools.partial(spread_kernel, micros),
+    slots = devices * CHUNK_ROWS
+    return pl.pallas_call(
+        functools.partial(spread_kernel, micros, devices),
         grid=(groups,),
         in_specs=[
+            pl.BlockSpec(lengths.shape, lambda g: (0, 0)),
             pl.BlockSpec((devices, 1, CHUNK_ROWS, D), lambda g: (0, g, 0, 0)),
-            pl.BlockSpec((micros, 1, slots), lambda g: (g, 0, 0)),
         ],
         out_specs=pl.BlockSpec((micros, TOK_DEV, D), lambda g: (g, 0, 0)),
         out_shape=jax.ShapeDtypeStruct((MICRO, TOK_DEV, D), BF16),
         compiler_params=params(40),
         cost_estimate=cost(2 * MICRO * TOK_DEV * slots * D, 4 * groups * slots * D),
-    )(back, want)
-
-
-def row_pick(start_ref, length_ref, slot_ref, group, micros):
-    parts = []
-    for step in range(micros):
-        slots = slot_ref[step]
-        for block in range(CAP // BLK):
-            micro = group * micros + step
-            place = lax.broadcasted_iota(jnp.int32, (BLK, slots.shape[1]), 0)
-            given = jnp.where(
-                place < length_ref[micro, block], place + start_ref[micro, block], -1
-            )
-            parts.append((given == slots).astype(F32).astype(BF16))
-    return jnp.concatenate(parts, axis=0)
+    )(lengths, back)
 
 
 def unpack_kernel(
-    micros, with_norm, start_ref, length_ref, slot_ref, arrived_ref, gain_ref, *outs
+    micros, devices, lengths_ref, token_ref, top_ref, gain_ref, hidden_ref, act_ref, grad_ref
 ):
-    pick = row_pick(start_ref, length_ref, slot_ref, pl.program_id(0), micros)
-    rows = dot(pick, arrived_ref[...].reshape(-1, D))
-    outs[0][...] = rows.astype(BF16)
-    if with_norm:
-        outs[1][...] = (normed(rows)[0] * gain_ref[...]).astype(BF16)
-
-
-def unpack_rows(arrived, starts, lengths, slots, gain, devices, micros, with_norm):
+    pick = held_rows(lengths_ref, pl.program_id(0), micros, devices)
+    rows = dot(pick, token_ref[...].reshape(-1, D))
+    hidden_ref[...] = rows.astype(BF16)
+    act_ref[...] = (normed(rows)[0] * gain_ref[...]).astype(BF16)
+    grad_ref[...] = dot(pick, top_ref[...].reshape(-1, D)).astype(BF16)
+
+
+def unpack_rows(lengths, tokens, top, gain, devices, micros):
     groups = MICRO // micros
-    width = slots.shape[-1]
-    out_spec = pl.BlockSpec((micros * CAP, D), lambda g: (g, 0))
-    out_type = jax.ShapeDtypeStruct((ROWS, D), BF16)
-    count = 2 if with_norm else 1
-    return pl.pallas_call(
-        functools.partial(unpack_kernel, micros, with_norm),
+    slots = devices * CHUNK_ROWS
+    chunk = pl.BlockSpec((devices, 1, CHUNK_ROWS, D), lambda g: (0, g, 0, 0))
+    return pl.pallas_call(
+        functools.partial(unpack_kernel, micros, devices),
         grid=(groups,),
         in_specs=[
-            pl.BlockSpec(memory_space=pltpu.SMEM),
-            pl.BlockSpec(memory_space=pltpu.SMEM),
-            pl.BlockSpec((micros, 1, width), lambda g: (g, 0, 0)),
-            pl.BlockSpec((devices, 1, CHUNK_ROWS, D), lambda g: (0, g, 0, 0)),
+            pl.BlockSpec(lengths.shape, lambda g: (0, 0)),
+            chunk,
+            chunk,
             pl.BlockSpec((1, D), lambda g: (0, 0)),
         ],
-        out_specs=[out_spec] * count,
-        out_shape=[out_type] * count,
-        compiler_params=params(40),
-        cost_estimate=cost(2 * ROWS * width * D, 4 * groups * width * D),
-    )(starts, lengths, slots, arrived, gain)
-
-
-def repack_kernel(micros, start_ref, length_ref, slot_ref, rows_ref, out_ref):
-    pick = row_pick(start_ref, length_ref, slot_ref, pl.program_id(0), micros)
+        out_specs=[pl.BlockSpec((micros * CAP, D), lambda g: (g, 0))] * 3,
+        out_shape=[jax.ShapeDtypeStruct((ROWS, D), BF16)] * 3,
+        compiler_params=params(48),
+        cost_estimate=cost(4 * ROWS * slots * D, 8 * groups * slots * D),
+    )(lengths, tokens, top, gain)
+
+
+def repack_kernel(micros, devices, lengths_ref, rows_ref, out_ref):
+    pick = held_rows(lengths_ref, pl.program_id(0), micros, devices)
     out_ref[...] = dot(pick, rows_ref[...], 0, 0).astype(BF16).reshape(out_ref.shape)
 
 
-def repack_rows(rows, starts, lengths, slots, devices, micros):
+def repack_rows(lengths, rows, devices, micros):
     groups = MICRO // micros
-    width = slots.shape[-1]
-    return pl.pallas_call(
-        functools.partial(repack_kernel, micros),
+    slots = devices * CHUNK_ROWS
+    return pl.pallas_call(
+        functools.partial(repack_kernel, micros, devices),
         grid=(groups,),
         in_specs=[
-            pl.BlockSpec(memory_space=pltpu.SMEM),
-            pl.BlockSpec(memory_space=pltpu.SMEM),
-            pl.BlockSpec((micros, 1, width), lambda g: (g, 0, 0)),
+            pl.BlockSpec(lengths.shape, lambda g: (0, 0)),
             pl.BlockSpec((micros * CAP, D), lambda g: (g, 0)),
         ],
         out_specs=pl.BlockSpec((devices, 1, CHUNK_ROWS, D), lambda g: (0, g, 0, 0)),
         out_shape=jax.ShapeDtypeStruct((devices, groups, CHUNK_ROWS, D), BF16),
         compiler_params=params(40),
-        cost_estimate=cost(2 * ROWS * width * D, 4 * groups * width * D),
-    )(starts, lengths, slots, rows)
+        cost_estimate=cost(2 * ROWS * slots * D, 4 * groups * slots * D),
+    )(lengths, rows)
 
 
 QKV_TILE = 512
@@ -233,7 +291,7 @@
     @pl.when(jnp.logical_not(is_value))
     def _():
         split = packed.reshape(BLOCKS, BLK, QKV_TILE)
-        spun = split * cos_ref[...][None] + turned(split) * sin_ref[...][None]
+        spun = split * widen(cos_ref[...])[None] + turned(split) * widen(sin_ref[...])[None]
         out_ref[...] = spun.reshape(ROWS, QKV_TILE).astype(BF16)
 
 
@@ -244,8 +302,8 @@
         in_specs=[
             pl.BlockSpec((ROWS, D), lambda j: (0, 0)),
             pl.BlockSpec((D, QKV_TILE), lambda j: (0, j)),
-            pl.BlockSpec((BLK, QKV_TILE), lambda j: (0, 0)),
-            pl.BlockSpec((BLK, QKV_TILE), lambda j: (0, 0)),
+            pl.BlockSpec((BLK, LANES), lambda j: (0, 0)),
+            pl.BlockSpec((BLK, LANES), lambda j: (0, 0)),
         ],
         out_specs=pl.BlockSpec((ROWS, QKV_TILE), lambda j: (0, j)),
         out_shape=jax.ShapeDtypeStruct((ROWS, 3 * D), BF16),
@@ -261,11 +319,17 @@
     return low, high
 
 
-def attend_kernel(length_ref, q_ref, k_ref, v_ref, out_ref, prob_ref):
+def attend_kernel(devices, length_ref, q_ref, k_ref, v_ref, out_ref, prob_ref):
     block = pl.program_id(0)
-    length = length_ref[block // 2, block % 2]
     low, high = head_masks(BF16)
-    valid = lax.broadcasted_iota(jnp.int32, (BLK, BLK), 1) < length
+    shape = (length_ref.shape[1], BLK)
+    own = lax.broadcasted_iota(jnp.int32, shape, 0) == (
+        SEQ_DEV * position(devices) + block % SEQ_DEV
+    )
+    lengths = length_sums(length_ref, own)
+    micro = lax.broadcasted_iota(jnp.int32, lengths.shape, 0) == block // SEQ_DEV
+    length = jnp.sum(jnp.where(micro, lengths, 0.0), axis=0, keepdims=True)
+    valid = lax.broadcasted_iota(jnp.int32, (BLK, BLK), 1).astype(F32) < length
     for pair in range(PAIRS):
         lanes = slice(pair * LANES, (pair + 1) * LANES)
         query, key, value = q_ref[:, lanes], k_ref[:, lanes], v_ref[:, lanes]
@@ -282,12 +346,12 @@
         out_ref[:, lanes] = dot(prob, both).astype(BF16)
 
 
-def attend(qkv, lengths):
-    return pl.pallas_call(
-        attend_kernel,
+def attend(qkv, lengths, devices):
+    return pl.pallas_call(
+        functools.partial(attend_kernel, devices),
         grid=(BLOCKS,),
         in_specs=[
-            pl.BlockSpec(memory_space=pltpu.SMEM),
+            pl.BlockSpec(lengths.shape, lambda b: (0, 0)),
             pl.BlockSpec((BLK, D), lambda b: (b, 0)),
             pl.BlockSpec((BLK, D), lambda b: (b, 1)),
             pl.BlockSpec((BLK, D), lambda b: (b, 2)),
@@ -474,6 +538,7 @@
 
 
 def branch_kernel(
+    order_ref,
     grad_b_ref,
     mid_ref,
     top_ref,
@@ -509,7 +574,7 @@
         grad_w_ref[...] = total[...].astype(BF16)
 
 
-def branch_back(grad_b, middle, top, attn_o, weight, gain):
+def branch_back(order, grad_b, middle, top, attn_o, weight, gain):
     tile = pl.BlockSpec((ROW_CHUNK, D), lambda i: (i, 0))
     square = pl.BlockSpec((D, D), lambda i: (0, 0))
     line = pl.BlockSpec((1, D), lambda i: (0, 0))
@@ -517,6 +582,7 @@
         branch_kernel,
         grid=(ROWS // ROW_CHUNK,),
         in_specs=[
+            pl.BlockSpec(memory_space=pl.ANY),
             *[tile] * 4,
             square,
             line,
@@ -531,25 +597,43 @@
         scratch_shapes=[pltpu.VMEM((D, D), F32)],
         compiler_params=params(40),
         cost_estimate=cost(4 * ROWS * D * D, 4 * D * D + 18 * ROWS * D),
-    )(grad_b, middle, top, attn_o, weight, gain)
+    )(order, grad_b, middle, top, attn_o, weight, gain)
 
 
 def input_kernel(
-    grad_qkv_ref, weight_ref, hidden_ref, grad_mid_ref, gain_ref, out_ref, grad_gain_ref
+    grad_qkv_ref,
+    weight_ref,
+    hidden_ref,
+    grad_mid_ref,
+    gain_ref,
+    other_ref,
+    out_ref,
+    gains_ref,
+    grad_gain,
 ):
     @pl.when(pl.program_id(0) == 0)
     def _():
-        grad_gain_ref[...] = jnp.zeros_like(grad_gain_ref)
+        grad_gain[...] = jnp.zeros_like(grad_gain)
 
     grad_a = dot(grad_qkv_ref[...], weight_ref[...], 1, 1)
     normal, inverse = normed(hidden_ref[...].astype(F32))
-    grad_gain_ref[...] += jnp.sum(grad_a * normal, axis=0, keepdims=True)
+    grad_gain[...] += jnp.sum(grad_a * normal, axis=0, keepdims=True)
     out_ref[...] = (
         grad_mid_ref[...] + norm_back(grad_a * gain_ref[...], normal, inverse)
     ).astype(BF16)
 
-
-def input_back(grad_qkv, weight, hidden, grad_mid, gain):
+    @pl.when(pl.program_id(0) == ROWS // ROW_CHUNK - 1)
+    def _():
+        width = D // SHARDS
+        for shard in range(SHARDS):
+            lanes = slice(shard * width, (shard + 1) * width)
+            for part, values in enumerate((grad_gain, other_ref)):
+                gains_ref[shard, :, part * width : (part + 1) * width] = jnp.broadcast_to(
+                    values[:, lanes], (GAIN_ROWS, width)
+                )
+
+
+def input_back(grad_qkv, weight, hidden, grad_mid, gain, other):
     tile = pl.BlockSpec((ROW_CHUNK, D), lambda i: (i, 0))
     line = pl.BlockSpec((1, D), lambda i: (0, 0))
     return pl.pallas_call(
@@ -561,15 +645,20 @@
             tile,
             tile,
             line,
-        ],
-        out_specs=[tile, line],
+            line,
+        ],
+        out_specs=[
+            tile,
+            pl.BlockSpec((SHARDS, GAIN_ROWS, 2 * D // SHARDS), lambda i: (0, 0, 0)),
+        ],
         out_shape=[
             jax.ShapeDtypeStruct((ROWS, D), BF16),
-            jax.ShapeDtypeStruct((1, D), F32),
-        ],
+            jax.ShapeDtypeStruct((SHARDS, GAIN_ROWS, 2 * D // SHARDS), F32),
+        ],
+        scratch_shapes=[pltpu.VMEM((1, D), F32)],
         compiler_params=params(40),
         cost_estimate=cost(6 * ROWS * D * D, 6 * D * D + 14 * ROWS * D),
-    )(grad_qkv, weight, hidden, grad_mid, gain)
+    )(grad_qkv, weight, hidden, grad_mid, gain, other)
 
 
 def qkv_grad_kernel(act_ref, grad_ref, out_ref, act_t):
@@ -606,6 +695,7 @@
     (2, 0, 1024),
     (3, 0, 1536),
     (3, 1536, 1536),
+    (4, 0, 256),
 )
 HOP_CORE, HOP_X, HOP_Y, HOP_XY, HOP_YX, HOP_IN, HOP_MID, HOP_OUT = range(8)
 
@@ -617,8 +707,8 @@
 
 
 def reduce_kernel(*refs):
-    tensors, refs = refs[:4], refs[4:]
-    outs, refs = refs[:4], refs[4:]
+    tensors, refs = refs[:5], refs[5:]
+    outs, refs = refs[:5], refs[5:]
     chunks = len(REDUCE_CHUNKS)
     sums, from_core, from_near, from_cross, from_far = (
         refs[i * chunks : (i + 1) * chunks] for i in range(5)
@@ -693,7 +783,7 @@
         )
 
     def add(one, other):
-        return (one.astype(F32) + other.astype(F32)).astype(BF16)
+        return (one.astype(F32) + other.astype(F32)).astype(one.dtype)
 
     def after_core(chunk):
         load(chunk).wait()
@@ -780,22 +870,22 @@
 
 
 def reduce_all(parts):
-    split = [part.reshape(2, 2, 2, -1, part.shape[1]) for part in parts]
-    shapes = [(v.shape[3], width) for v, width in ((split[t], w) for t, _, w in REDUCE_CHUNKS)]
+    split = [part.reshape(2, 2, 2, -1, part.shape[-1]) for part in parts]
+    kinds = [(split[t].dtype, split[t].shape[3], width) for t, _, width in REDUCE_CHUNKS]
     anywhere = pl.BlockSpec(memory_space=pl.ANY)
     chunks = len(REDUCE_CHUNKS)
     moved = sum(v.size for v in split)
     return pl.pallas_call(
         reduce_kernel,
-        in_specs=[anywhere] * 4,
-        out_specs=[anywhere] * 4,
-        out_shape=[jax.ShapeDtypeStruct(v.shape[3:], BF16) for v in split],
+        in_specs=[anywhere] * len(parts),
+        out_specs=[anywhere] * len(parts),
+        out_shape=[jax.ShapeDtypeStruct(v.shape[3:], v.dtype) for v in split],
         scratch_shapes=[
-            *[pltpu.VMEM((2, 2, r, w), BF16) for r, w in shapes],
-            *[pltpu.VMEM((2, 2, r, w), BF16) for r, w in shapes],
-            *[pltpu.VMEM((2, 2, r, w // 2), BF16) for r, w in shapes],
-            *[pltpu.VMEM((2, r, w // 2), BF16) for r, w in shapes],
-            *[pltpu.VMEM((2, r, w), BF16) for r, w in shapes],
+            *[pltpu.VMEM((2, 2, r, w), t) for t, r, w in kinds],
+            *[pltpu.VMEM((2, 2, r, w), t) for t, r, w in kinds],
+            *[pltpu.VMEM((2, 2, r, w // 2), t) for t, r, w in kinds],
+            *[pltpu.VMEM((2, r, w // 2), t) for t, r, w in kinds],
+            *[pltpu.VMEM((2, r, w), t) for t, r, w in kinds],
             pltpu.SemaphoreType.DMA((chunks,)),
             pltpu.SemaphoreType.DMA((chunks, 8)),
             pltpu.SemaphoreType.DMA((chunks, 8)),
@@ -806,6 +896,192 @@
         ),
         cost_estimate=cost(2 * moved, 40 * moved),
     )(*split)
+
+
+WAY_X, WAY_Y, WAY_CORE, WAY_CORE_X, WAY_CORE_Y = range(5)
+WAY_XY, WAY_YX, WAY_CORE_XY, WAY_CORE_YX = range(5, 9)
+
+
+def gather_kernel(devices, *refs):
+    shards, refs = refs[:4], refs[4:]
+    gain, sends, refs = refs[0], refs[1:3], refs[3:]
+    fulls, refs = refs[:4], refs[4:]
+    gains, lands, refs = refs[0], refs[1:3], refs[3:]
+    local_sem, way_send, way_recv, gain_send, gain_recv, row_send, row_recv = refs
+    rep, grp, core, x, y, by_core, by_x, by_y = place()
+    by_xy = by_x + by_y - grp
+    other = by_core - grp
+    device = rep * SHARDS + grp
+
+    def peer(step):
+        return lax.rem(device + step, devices)
+
+    def mesh_id(index):
+        return (index // SHARDS, lax.rem(index, SHARDS))
+
+    barrier = pltpu.get_barrier_semaphore()
+
+    def greet(step, carry):
+        pl.semaphore_signal(barrier, device_id=mesh_id(peer(step)), device_id_type=MESH)
+        return carry
+
+    lax.fori_loop(1, devices, greet, 0)
+    pl.semaphore_wait(barrier, devices - 1)
+
+    def way(which, tensor):
+        full, width = fulls[tensor], shards[tensor].shape[1]
+        left, right = pl.ds(0, width // 2), pl.ds(width // 2, width // 2)
+        own = shards[tensor]
+        source, slot, landing, part, to = {
+            WAY_X: (own, grp, by_x, None, by_x),
+            WAY_Y: (own, grp, by_y, None, by_y),
+            WAY_CORE: (own, grp, by_core, None, by_core),
+            WAY_CORE_X: (None, by_x, by_x + other, None, by_core),
+            WAY_CORE_Y: (None, by_y, by_y + other, None, by_core),
+            WAY_XY: (None, by_x, by_xy, left, by_y),
+            WAY_YX: (None, by_y, by_xy, right, by_x),
+            WAY_CORE_XY: (None, by_xy, by_xy + other, left, by_core),
+            WAY_CORE_YX: (None, by_xy, by_xy + other, right, by_core),
+        }[which]
+
+        def view(index):
+            return full.at[index] if part is None else full.at[index, :, part]
+
+        def copy(source, target):
+            return pltpu.make_async_remote_copy(
+                src_ref=source,
+                dst_ref=target,
+                send_sem=way_send.at[tensor, which],
+                recv_sem=way_recv.at[tensor, which],
+                device_id=(rep, to),
+                device_id_type=MESH,
+            )
+
+        def start():
+            copy(view(slot) if source is None else source, view(slot)).start()
+
+        def arrive():
+            copy(view(landing), view(landing)).wait_recv()
+
+        def sent():
+            copy(view(slot) if source is None else source, view(slot)).wait_send()
+
+        return start, arrive, sent
+
+    def start(tensor, *ways):
+        for which in ways:
+            way(which, tensor)[0]()
+
+    def arrive(tensor, *ways):
+        for which in ways:
+            way(which, tensor)[1]()
+
+    def gain_copy(step, slot):
+        to = lax.rem(grp + step, SHARDS)
+        return pltpu.make_async_remote_copy(
+            src_ref=gain,
+            dst_ref=gains.at[slot],
+            send_sem=gain_send.at[step],
+            recv_sem=gain_recv.at[step],
+            device_id=(rep, to),
+            device_id_type=MESH,
+        )
+
+    def row_copy(which, step, source, slot, to):
+        return pltpu.make_async_remote_copy(
+            src_ref=sends[which].at[source],
+            dst_ref=lands[which].at[slot],
+            send_sem=row_send.at[which, step],
+            recv_sem=row_recv.at[which, step],
+            device_id=mesh_id(to),
+            device_id_type=MESH,
+        )
+
+    def send_rows(which):
+        def one(step, carry):
+            row_copy(which, step, peer(step), device, peer(step)).start()
+            return carry
+
+        lax.fori_loop(1, devices, one, 0)
+
+    def land_rows(which):
+        def one(step, carry):
+            source = lax.rem(device + devices - step, devices)
+            row_copy(which, step, peer(step), source, peer(step)).wait_recv()
+            row_copy(which, step, peer(step), device, peer(step)).wait_send()
+            return carry
+
+        lax.fori_loop(1, devices, one, 0)
+
+    def local(index, source, target):
+        return pltpu.make_async_copy(source, target, local_sem.at[index])
+
+    keeps = [local(i, shards[i], fulls[i].at[grp]) for i in range(4)]
+    keeps.append(local(4, gain, gains.at[grp]))
+    keeps += [local(5 + i, sends[i].at[device], lands[i].at[device]) for i in range(2)]
+
+    for step in range(1, SHARDS):
+        gain_copy(step, grp).start()
+    start(3, WAY_X, WAY_Y, WAY_CORE)
+    send_rows(0)
+    for tensor in (2, 1, 0):
+        start(tensor, WAY_X, WAY_Y, WAY_CORE)
+    send_rows(1)
+    for keep in keeps:
+        keep.start()
+    order = (3, 2, 1, 0)
+    for late in range(len(order) + 1):
+        if late < len(order):
+            tensor = order[late]
+            arrive(tensor, WAY_X)
+            start(tensor, WAY_XY, WAY_CORE_X)
+            arrive(tensor, WAY_Y)
+            start(tensor, WAY_YX, WAY_CORE_Y)
+        if late:
+            tensor = order[late - 1]
+            arrive(tensor, WAY_XY)
+            start(tensor, WAY_CORE_XY)
+            arrive(tensor, WAY_YX)
+            start(tensor, WAY_CORE_YX)
+    for tensor in order:
+        arrive(tensor, WAY_CORE, WAY_CORE_X, WAY_CORE_Y, WAY_CORE_XY, WAY_CORE_YX)
+    for step in range(1, SHARDS):
+        gain_copy(step, lax.rem(grp + SHARDS - step, SHARDS)).wait_recv()
+        gain_copy(step, grp).wait_send()
+    for which in range(2):
+        land_rows(which)
+    for tensor in order:
+        for which in range(9):
+            way(which, tensor)[2]()
+    for keep in keeps:
+        keep.wait()
+
+
+def gather_all(shards, gain, sends, devices):
+    anywhere = pl.BlockSpec(memory_space=pl.ANY)
+    moved = SHARDS * sum(v.size for v in shards) + sum(v.size for v in sends)
+    dma = pltpu.SemaphoreType.DMA
+    out = [
+        *[jax.ShapeDtypeStruct((SHARDS, *v.shape), v.dtype) for v in (*shards, gain)],
+        *[jax.ShapeDtypeStruct(v.shape, v.dtype) for v in sends],
+    ]
+    return pl.pallas_call(
+        functools.partial(gather_kernel, devices),
+        in_specs=[anywhere] * 7,
+        out_specs=[anywhere] * 7,
+        out_shape=out,
+        scratch_shapes=[
+            dma((7,)),
+            dma((4, 9)),
+            dma((4, 9)),
+            dma((SHARDS,)),
+            dma((SHARDS,)),
+            dma((2, devices)),
+            dma((2, devices)),
+        ],
+        compiler_params=pltpu.CompilerParams(collective_id=0, has_side_effects=True),
+        cost_estimate=cost(0, 16 * moved),
+    )(*shards, gain, *sends)
 
 
 def weave(weight):
@@ -829,38 +1105,6 @@
     return jnp.concatenate(tiles, axis=1)
 
 
-def plan(seq_lengths, device, devices, micros):
-    pair_cap = CAP // devices
-    slots = devices * CHUNK_ROWS
-    slot = jnp.arange(slots, dtype=jnp.int32)
-    peer, inner = slot // CHUNK_ROWS, slot % CHUNK_ROWS
-    rank, part = inner % pair_cap, inner // pair_cap
-    micro = jnp.arange(MICRO, dtype=jnp.int32)
-    mine = (micro % micros)[:, None] == part[None, :]
-    seq = jnp.arange(seq_lengths.shape[1], dtype=jnp.int32)
-    ahead = seq[None, :] < SEQ_DEV * peer[:, None]
-    peer_start = jnp.sum(
-        jnp.where(ahead[None], seq_lengths[:, None, :], 0), axis=2, dtype=jnp.int32
-    )
-    want = jnp.where(
-        mine, (peer_start - device + devices - 1) // devices + rank[None, :], -1
-    )
-    own_seq = device * SEQ_DEV + jnp.arange(SEQ_DEV, dtype=jnp.int32)
-    starts = jnp.sum(
-        jnp.where(seq[None, None, :] < own_seq[None, :, None], seq_lengths[:, None, :], 0),
-        axis=2,
-        dtype=jnp.int32,
-    )
-    lengths = jnp.sum(
-        jnp.where(seq[None, None, :] == own_seq[None, :, None], seq_lengths[:, None, :], 0),
-        axis=2,
-        dtype=jnp.int32,
-    )
-    first = (starts[:, :1] - peer[None, :] + devices - 1) // devices
-    given = jnp.where(mine, (first + rank[None, :]) * devices + peer[None, :], -2)
-    return want[:, None, :], starts, lengths, given[:, None, :]
-
-
 def body(tokens, cotangent, seq_lengths, w_qkv, w_out, w_in, w_down, attn_gain, mlp_gain):
     group_size = lax.axis_size("grp")
     devices = lax.axis_size("rep") * group_size
@@ -871,65 +1115,60 @@
     def swap(rows):
         return lax.all_to_all(rows, both, split_axis=0, concat_axis=0, tiled=True)
 
-    def gather(rows):
-        return lax.all_gather(rows, "grp", axis=0, tiled=True)
-
     near = group_size == SHARDS and devices == REPLICAS * SHARDS
-    want, starts, lengths, given = plan(seq_lengths, device, devices, micros)
-    token_rows = swap(pack_rows(tokens[:, :, 0], want, devices, micros))
-    top_rows = swap(pack_rows(cotangent[:, :, 0], want, devices, micros))
-    gains = lax.all_gather(jnp.stack([attn_gain, mlp_gain]), "grp", axis=1, tiled=True)
+    sends = pack_rows(
+        seq_lengths, (tokens[:, :, 0], cotangent[:, :, 0]), devices, micros
+    )
+    gains = jnp.stack([attn_gain, mlp_gain])
+    shards = (w_down, weave(w_in), w_out, w_qkv)
+    if near:
+        gain = jnp.pad(gains, ((0, CHUNK_ROWS - 2), (0, 0)))
+        *full, gains, token_rows, top_rows = gather_all(shards, gain, sends, devices)
+        full = [v.reshape(-1, v.shape[-1]) for v in full]
+        gains = jnp.swapaxes(gains[:, :2], 0, 1).reshape(2, D)
+    else:
+        token_rows, top_rows = (swap(v) for v in sends)
+        full = [lax.all_gather(v, "grp", axis=0, tiled=True) for v in shards]
+        gains = lax.all_gather(gains, "grp", axis=1, tiled=True)
+    full_down, full_in, full_out, full_qkv = full
     gain_one = gains[:1].astype(F32)
     gain_two = gains[1:].astype(F32)
-    full_qkv = gather(w_qkv)
-    full_out = gather(w_out)
-    full_in = gather(weave(w_in))
-    full_down = gather(w_down)
-
-    cosine, sine = rotary_tables(QKV_TILE)
-    hidden, act_a = unpack_rows(
-        token_rows, starts, lengths, given, gain_one, devices, micros, True
-    )
-    (top,) = unpack_rows(
-        top_rows, starts, lengths, given, gain_one, devices, micros, False
+
+    cosine, sine = rotary_tables()
+    hidden, act_a, top = unpack_rows(
+        seq_lengths, token_rows, top_rows, gain_one, devices, micros
     )
     qkv = qkv_rows(act_a, full_qkv, cosine, sine)
-    attn_o, prob = attend(qkv, lengths)
+    attn_o, prob = attend(qkv, seq_lengths, devices)
     middle, act_b = middle_rows(attn_o, hidden, full_out, gain_two)
-    layer_rows, grad_b, grad_in_w, grad_down_w = ffn(
-        act_b, top, middle, full_in, full_down
-    )
-    layer_back = swap(repack_rows(layer_rows, starts, lengths, given, devices, micros))
-
-
+    layer_rows, grad_b, grad_in_w, grad_down_w = ffn(act_b, top, middle, full_in, full_down)
+    layer_send = repack_rows(seq_lengths, layer_rows, devices, micros)
+    layer_back = swap(layer_send)
     grad_mid, grad_o, grad_out_w, grad_gain_two = branch_back(
-        grad_b, middle, top, attn_o, full_out, gain_two
-    )
-    grad_qkv_rows = attend_back(qkv, grad_o, prob, cosine[:, :LANES], sine[:, :LANES])
+        layer_send, grad_b, middle, top, attn_o, full_out, gain_two
+    )
+    grad_qkv_rows = attend_back(qkv, grad_o, prob, cosine, sine)
     grad_qkv_w = qkv_grad(act_a, grad_qkv_rows)
-    grad_rows, grad_gain_one = input_back(
-        grad_qkv_rows, full_qkv, hidden, grad_mid, gain_one
-    )
-    grad_back = swap(repack_rows(grad_rows, starts, lengths, given, devices, micros))
+    grad_rows, gain_parts = input_back(
+        grad_qkv_rows, full_qkv, hidden, grad_mid, gain_one, grad_gain_two
+    )
+    grad_back = swap(repack_rows(seq_lengths, grad_rows, devices, micros))
     parts = (grad_down_w, grad_in_w, grad_out_w, grad_qkv_w)
     if near:
-        owned = reduce_all(parts)
+        *owned, gain_sums = reduce_all((*parts, gain_parts))
+        gain_sums = gain_sums[0].reshape(2, -1)
     else:
         owned = [
             lax.psum(lax.psum_scatter(v, "grp", scatter_dimension=0, tiled=True), "rep")
             for v in parts
         ]
+        gain_parts = gain_parts[:, 0].reshape(SHARDS, 2, -1).swapaxes(0, 1).reshape(2, D)
+        gain_sums = lax.psum(
+            lax.psum_scatter(gain_parts, "grp", scatter_dimension=1, tiled=True), "rep"
+        )
     grad_down, grad_in, grad_out, grad_qkv = (v.astype(F32) for v in owned)
-    gain_parts = jnp.concatenate([grad_gain_one, grad_gain_two], axis=0)
-    gain_parts = gain_parts.reshape(2, 1, group_size, -1)
-    gain_parts = jnp.broadcast_to(
-        gain_parts, (2, devices // group_size, *gain_parts.shape[2:])
-    ).reshape(2, devices, -1)
-    gain_sums = jnp.sum(
-        lax.all_to_all(gain_parts, both, split_axis=1, concat_axis=1, tiled=True), axis=1
-    )
-    layer_out = spread_rows(layer_back, want, devices, micros)[:, :, None, :]
-    grad_tokens = spread_rows(grad_back, want, devices, micros)[:, :, None, :]
+    layer_out = spread_rows(seq_lengths, layer_back, devices, micros)[:, :, None, :]
+    grad_tokens = spread_rows(seq_lengths, grad_back, devices, micros)[:, :, None, :]
     return (
         layer_out,
         grad_tokens,

time: 623 us -> 591 us (0.949)
  waiting for transfers between devices: 169 us -> 0.01 us
  Pallas kernels: 332 us -> 491 us
  blocking collectives: 22.3 us -> 51.3 us
  starting transfers between devices: 22.8 us -> 3.67 us
  local copies, waits for them, and re-layouts: 54 us -> 37.5 us
  between operations: 14.3 us -> 1.05 us
    pallas_call x11 -> x10, Pallas kernels: 193 us -> 351 us  [the longest x1 159 us: gather_all(): pl.pallas_call(functools.partial(gather_kernel, devices), in_specs=[anywh...]
    all_to_all x4 -> x1, waiting for transfers between devices: 111 us -> 0.01 us  [swap(): return lax.all_to_all(rows, both, split_axis=0, concat_axis=0, tiled=True)]
    all_gather x4 -> x0, waiting for transfers between devices: 52.5 us -> none  [gather(): return lax.all_gather(rows, 'grp', axis=0, tiled=True)]
    all_to_all x0 -> x1, blocking collectives: none -> 51.3 us  [swap(): return lax.all_to_all(rows, both, split_axis=0, concat_axis=0, tiled=True)]
    all_gather x1 -> x0, blocking collectives: 22.3 us -> none  [body(): lax.all_gather(jnp.stack([attn_gain, mlp_gain]), 'grp', axis=1, tiled=True)]
    unnamed x80 -> x84, local copies, waits for them, and re-layouts: 45.2 us -> 27.8 us
    all_to_all x4 -> x1, starting transfers between devices: 18.1 us -> 3.67 us  [swap(): return lax.all_to_all(rows, both, split_axis=0, concat_axis=0, tiled=True)]
  transfers between devices with their start and end apart: 9 -> 1, of which waited for: 5 -> 0; matrix products, arithmetic and copies ran while one was open for 4% -> 2% of each run, Pallas kernels for 33% -> 28%
where the time goes in v3:
time: 591 us; the launch traced here: 590 us
  Pallas kernels  491 us (83%)
  blocking collectives  51.3 us (9%)
  local copies, waits for them, and re-layouts  37.5 us (6%)
  other arithmetic  6.11 us (1%)
    pallas_call x1, Pallas kernels, gather_all(): pl.pallas_call(functools.partial(gather_kernel, devices), in_specs=[anywh...  159 us
    pallas_call x1, Pallas kernels, reduce_all(): pl.pallas_call(reduce_kernel, in_specs=[anywhere] * len(parts), out_specs...  151 us
    pallas_call x1, Pallas kernels, ffn(): pl.pallas_call(ffn_kernel, grid=(FF_STEPS,), in_specs=[whole, whole, whol...  72.9 us
    all_to_all x1, blocking collectives, swap(): return lax.all_to_all(rows, both, split_axis=0, concat_axis=0, tiled=True)  51.3 us
    unnamed x84, local copies, waits for them, and re-layouts  27.8 us
    pallas_call x1, Pallas kernels, attend_back(): pl.pallas_call(attend_back_kernel, grid=(BLOCKS,), in_specs=[pl.BlockSpec...  25.1 us
    pallas_call x1, Pallas kernels, qkv_rows(): pl.pallas_call(qkv_kernel, grid=(3 * D // QKV_TILE,), in_specs=[pl.BlockS...  16.5 us
    pallas_call x1, Pallas kernels, input_back(): pl.pallas_call(input_kernel, grid=(ROWS // ROW_CHUNK,), in_specs=[pl.Bloc...  12.5 us
  transfers between devices with their start and end apart: 1, of which 0 were waited for; matrix products, arithmetic and copies ran while one was open for 2% of the time, Pallas kernels for 28%

profile of v3, /device:TPU:0, one launch (start us, length us, event | category | flops | bytes accessed | tf_op | source)
XLA Modules:
  0.0 590.2 jit_solution(11843493404290986748)
XLA Ops:
  4.9 4.0 shard_map.170
  10.2 159.0 %shard_map.171 = (bf16[8,328,1024]{2,1,0:T(8,128)(2,1)}, bf16[8,128,5376]{2,1,0:T(8,128)(2,1)}, bf16[8,128,1024]{2,1,0:T(8,128)(2,1)}, bf16[8,128,3072]{2,1,0:T(...) custom-call(bf16[328,1024]{1,0:T(8,128)(2,1)} %refs_0_.1, ...), custom_call_target="tpu_custom_call" | custom-call | bytes 231735296 | tf_op jit(solution)/shard_map/pallas_call | solution.py:1068
  169.9 6.2 %shard_map.172 = (bf16[1024,1024]{1,0:T(8,128)(2,1)S(1)}, bf16[1024,1024]{1,0:T(8,128)(2,1)S(1)}, bf16[1024,1024]{1,0:T(8,128)(2,1)}) custom-call(s32[4,64]{1,0:T(4,128)S(1)} %copy-done.19, bf16[32,2,16,1024]{3,2,1,0:T(8,128)(2,1)} %get-tuple-element.41.token_ref, bf16[32,2,16,1024]{3,2,1,0:T(8,128)(2,1)} %get-tuple-element.42.top_ref, ...), custom_call_target="tpu_custom_call" | custom-call | flops 2147483648 | bytes 8388608 | tf_op jit(solution)/shard_map/pallas_call | solution.py:242
  176.1 16.5 %shard_map.173.q_ref.k_ref.v_ref = bf16[1024,3072]{1,0:T(8,128)(2,1)S(1)} custom-call(bf16[1024,1024]{1,0:T(8,128)(2,1)S(1)} %get-tuple-element.44.act_ref, bf16[1024,3072]{1,0:T(8,128)(2,1)} %bitcast.51, f32[128,128]{1,0:T(8,128)S(1)} %copy-done.17, f32[128,128]{1,0:T(8,128)S(1)} %copy-done.16), custom_call_target="tpu_custom_call" | custom-call | flops 6442450944 | bytes 14680064 | tf_op jit(solution)/shard_map/pallas_call | solution.py:299
  194.0 9.8 %shard_map.174 = (bf16[1024,1024]{1,0:T(8,128)(2,1)S(1)}, bf16[8,8,128,256]{3,2,1,0:T(8,128)(2,1)S(1)}) custom-call(s32[4,64]{1,0:T(4,128)S(1)} %copy-done.19, bf16[1024,3072]{1,0:T(8,128)(2,1)S(1)} %shard_map.173.q_ref.k_ref.v_ref, bf16[1024,3072]{1,0:T(8,128)(2,1)S(1)} %shard_map.173.q_ref.k_ref.v_ref, bf16[1024,3072]{1,0:T(8,128)(2,1)S(1)} %shard_map.173.q_ref.k_ref.v_ref), custom_call_target="tpu_custom_call" | custom-call | flops 1073741824 | bytes 12582912 | tf_op jit(solution)/shard_map/pallas_call | solution.py:350
  205.7 4.0 shard_map.175
  209.8 2.0 copy-done.7
  213.1 72.9 %shard_map.176 = (bf16[1024,1024]{1,0:T(8,128)(2,1)}, f32[1024,1024]{1,0:T(8,128)}, bf16[1024,5376]{1,0:T(8,128)(2,1)}, bf16[2624,1024]{1,0:T(8,128)(2,1)}) custom-call(bf16[1024,1024]{1,0:T(8,128)(2,1)} %copy-done.25, bf16[1024,1024]{1,0:T(8,128)(2,1)} %get-tuple-element.50.top_ref, f32[1024,1024]{1,0:T(8,128)} %copy-done.7, bf16[1024,5376]{1,0:T(8,128)(2,1)} %bitcast.50, ...), custom_call_target="tpu_custom_call" | custom-call | flops 49526341632 | bytes 32243712 | tf_op jit(solution)/shard_map/pallas_call | solution.py:511
  287.6 2.9 shard_map.177.order_ref
  295.6 10.9 %shard_map.179 = (f32[1024,1024]{1,0:T(8,128)}, bf16[1024,1024]{1,0:T(8,128)(2,1)S(1)}, bf16[1024,1024]{1,0:T(8,128)(2,1)S(1)}, f32[1,1024]{1,0:T(1,128)S(1)}) custom-call(bf16[32,2,16,1024]{3,2,1,0:T(8,128)(2,1)} %shard_map.177.order_ref, f32[1024,1024]{1,0:T(8,128)} %get-tuple-element.55.grad_b_ref, f32[1024,1024]{1,0:T(8,128)} %copy-done.7, ...), custom_call_target="tpu_custom_call" | custom-call | flops 4294967296 | bytes 23068672 | tf_op jit(solution)/shard_map/pallas_call | solution.py:581
  306.5 25.1 %shard_map.180.grad_qkv_ref.grad_ref = bf16[1024,3072]{1,0:T(8,128)(2,1)S(1)} custom-call(bf16[1024,3072]{1,0:T(8,128)(2,1)S(1)} %bitcast.36, bf16[1024,3072]{1,0:T(8,128)(2,1)S(1)} %bitcast.36, bf16[1024,3072]{1,0:T(8,128)(2,1)S(1)} %bitcast.36, bf16[1024,1024]{1,0:T(8,128)(2,1)S(1)} %get-tuple-element.56.grad_ref, bf16[8,8,128,256]{3,2,1,0:T(8,128)(2,1)S(1)} %copy-done.6, ...), custom_call_target="tpu_custom_call" | custom-call | flops 2684354560 | bytes 18874368 | tf_op jit(solution)/shard_map/pallas_call | solution.py:408
  331.6 2.7 copy-done.3
  334.3 12.5 %shard_map.181 = (bf16[1024,1024]{1,0:T(8,128)(2,1)S(1)}, f32[8,8,256]{2,1,0:T(8,128)S(1)}) custom-call(bf16[1024,3072]{1,0:T(8,128)(2,1)} %copy-done.3, bf16[1024,3072]{1,0:T(8,128)(2,1)} %bitcast.52, bf16[1024,1024]{1,0:T(8,128)(2,1)S(1)} %copy-done.24, f32[1024,1024]{1,0:T(8,128)S(1)} %copy-done.20, f32[1,1024]{1,0:T(1,128)S(1)} %get-tuple-element.95.gain_ref, ...), custom_call_target="tpu_custom_call" | custom-call | flops 6442450944 | bytes 20971520 | tf_op jit(solution)/shard_map/pallas_call | solution.py:639
  346.8 2.0 shard_map.182
  348.8 51.3 %all_to_all.10.back_ref = bf16[32,2,16,1024]{3,2,1,0:T(8,128)(2,1)} all-to-all(bf16[32,2,16,1024]{3,2,1,0:T(8,128)(2,1)S(1)} %shard_map.182), channel_id=1, replica_groups=mesh['rep'=4,'grp'=8] {'rep','grp'}, dimensions={0} | all-to-all | bytes 4194304 | tf_op jit(solution)/shard_map/all_to_all | solution.py:1116
  400.1 3.7 all-to-all-start
  403.8 2.8 copy-done.4
  408.1 9.0 %shard_map.184 = bf16[1024,3072]{1,0:T(8,128)(2,1)S(1)} custom-call(bf16[1024,1024]{1,0:T(8,128)(2,1)S(1)} %copy-done.27, bf16[1024,3072]{1,0:T(8,128)(2,1)S(1)} %copy-done.4), custom_call_target="tpu_custom_call" | custom-call | flops 6442450944 | bytes 14680064 | tf_op jit(solution)/shard_map/pallas_call | solution.py:673
  417.1 2.7 copy-done.2
  419.8 151.1 %shard_map.185 = (bf16[328,1024]{1,0:T(8,128)(2,1)}, bf16[128,5376]{1,0:T(8,128)(2,1)}, bf16[128,1024]{1,0:T(8,128)(2,1)}, bf16[128,3072]{1,0:T(8,128)(2,1)}, f32[8,256]{1,0:T(8,128)}) custom-call(bf16[2,2,2,328,1024]{4,3,2,1,0:T(8,128)(2,1)} %bitcast.45, bf16[2,2,2,128,5376]{4,3,2,1,0:T(8,128)(2,1)} %bitcast.44, bf16[2,2,2,128,1024]{4,3,2,1,0:T(8,128)(2,1)} %bitcast.38, ...), custom_call_target="tpu_custom_call" | custom-call | flops 24805376 | bytes 496107520 | tf_op jit(solution)/shard_map/pallas_call | solution.py:878
  572.8 2.3 convert_element_type.31
  578.8 3.8 concatenate.15
  585.4 2.4 shard_map.183
  587.8 2.4 shard_map.178
  (96 shorter events, 27.4 us)
Async XLA Ops:
  2.1 2.3 slice-start.2
  3.1 1.8 copy-start.21
  4.4 4.4 copy-start.30
  169.9 6.2 %copy-start.16 = (f32[128,128]{1,0:T(8,128)S(1)}, f32[128,128]{1,0:T(8,128)}, u32[]{:S(2)}) copy-start(f32[128,128]{1,0:T(8,128)} %constant.11.clone.sin_ref) | copy-start | bytes 196612
  169.9 6.2 %copy-start.17 = (f32[128,128]{1,0:T(8,128)S(1)}, f32[128,128]{1,0:T(8,128)}, u32[]{:S(2)}) copy-start(f32[128,128]{1,0:T(8,128)} %constant.10.clone.cos_ref) | copy-start | bytes 196612
  176.1 29.6 %copy-start.23 = (bf16[1024,1024]{1,0:T(8,128)(2,1)}, bf16[1024,1024]{1,0:T(8,128)(2,1)S(1)}, u32[]{:S(2)}) copy-start(bf16[1024,1024]{1,0:T(8,128)(2,1)S(1)} %get-tuple-element.47.hidden_ref) | copy-start | bytes 6291460
  194.0 9.8 %copy-start = (bf16[1024,3072]{1,0:T(8,128)(2,1)}, bf16[1024,3072]{1,0:T(8,128)(2,1)S(1)}, u32[]{:S(2)}) copy-start(bf16[1024,3072]{1,0:T(8,128)(2,1)S(1)} %shard_map.173.q_ref.k_ref.v_ref) | copy-start | bytes 18874372
  194.0 11.7 %copy-start.9 = (bf16[8,128,1024]{2,1,0:T(8,128)(2,1)S(1)}, bf16[8,128,1024]{2,1,0:T(8,128)(2,1)}, u32[]{:S(2)}) copy-start(bf16[8,128,1024]{2,1,0:T(8,128)(2,1)} %get-tuple-element.48) | copy-start | bytes 6291460
  203.8 1.9 copy-start.5
  205.7 4.0 copy-start.12
  209.8 2.0 copy-start.7
  290.5 16.0 %slice-start = ((s8[6291456]{0:T(1024)(128)(4,1)}), s8[4194304]{0:T(1024)(128)(4,1)S(1)}, s32[]{:S(2)}) async-start(s8[6291456]{0:T(1024)(128)(4,1)} %bitcast.35), calls=%async_computation.2 | async-start | bytes 8388608
  295.6 10.9 %slice-start.1 = ((s8[6291456]{0:T(1024)(128)(4,1)}), s8[2097152]{0:T(1024)(128)(4,1)S(1)}, s32[]{:S(2)}) async-start(s8[6291456]{0:T(1024)(128)(4,1)} %bitcast.35), calls=%async_computation.3 | async-start | bytes 4194304
  295.6 10.9 %copy-start.6 = (bf16[8,8,128,256]{3,2,1,0:T(8,128)(2,1)S(1)}, bf16[8,8,128,256]{3,2,1,0:T(8,128)(2,1)}, u32[]{:S(2)}) copy-start(bf16[8,8,128,256]{3,2,1,0:T(8,128)(2,1)} %copy-done.5) | copy-start | bytes 12582916
  306.5 25.1 %copy-start.8 = (bf16[1024,1024]{1,0:T(8,128)(2,1)}, bf16[1024,1024]{1,0:T(8,128)(2,1)S(1)}, u32[]{:S(2)}) copy-start(bf16[1024,1024]{1,0:T(8,128)(2,1)S(1)} %get-tuple-element.63) | copy-start | bytes 6291460
  306.5 27.8 %copy-start.20 = (f32[1024,1024]{1,0:T(8,128)S(1)}, f32[1024,1024]{1,0:T(8,128)}, u32[]{:S(2)}) copy-start(f32[1024,1024]{1,0:T(8,128)} %get-tuple-element.58.grad_mid_ref) | copy-start | bytes 12582916
  306.5 27.8 %copy-start.24 = (bf16[1024,1024]{1,0:T(8,128)(2,1)S(1)}, bf16[1024,1024]{1,0:T(8,128)(2,1)}, u32[]{:S(2)}) copy-start(bf16[1024,1024]{1,0:T(8,128)(2,1)} %copy-done.23) | copy-start | bytes 6291460
  331.6 2.7 copy-start.3
  346.8 2.0 copy-start.18
  400.1 187.7 %all-to-all-start = ((bf16[32,2,16,1024]{3,2,1,0:T(8,128)(2,1)}), bf16[32,2,16,1024]{3,2,1,0:T(8,128)(2,1)S(1)}, u32[]{:S(2)}, u32[]{:S(2)}) async-start(bf16[32,2,16,1024]{3,2,1,0:T(8,128)(2,1)} %shard_map.177.order_ref), calls=%async_computation | async-start | bytes 4194304 | tf_op jit(solution)/shard_map/all_to_all | solution.py:1116
  403.7 2.8 copy-start.4
  417.1 2.7 copy-start.2
  570.9 4.2 copy-start.31
  575.1 1.9 copy-start.28
  (14 other events, 21.4 us)

commit v4 on v3

--- a/solution.py
+++ b/solution.py
@@ -372,36 +372,20 @@
 def attend_back_kernel(
     q_ref, k_ref, v_ref, grad_ref, prob_ref, cos_ref, sin_ref, out_ref
 ):
-    low, high = head_masks(BF16)
-    lane = lax.broadcasted_iota(jnp.int32, (BLK, LANES), 1)
-    is_low = lane < HD
-    cosine, sine = cos_ref[...], sin_ref[...]
     for pair in range(PAIRS):
-        lanes = slice(pair * LANES, (pair + 1) * LANES)
-        query, key, value = q_ref[:, lanes], k_ref[:, lanes], v_ref[:, lanes]
-        grad, prob = grad_ref[:, lanes], prob_ref[0, pair]
-        grad_v = dot(prob, grad, 0, 0)
-        grad_v = jnp.where(is_low, grad_v[:BLK], grad_v[BLK:])
-        grad_p = dot(grad, jnp.concatenate([value * low, value * high], axis=0), 1, 1)
-        parts = []
-        for head in range(2):
-            keys = slice(head * BLK, (head + 1) * BLK)
-            weight, slope = prob[:, keys].astype(F32), grad_p[:, keys]
-            inner = jnp.sum(weight * slope, axis=-1, keepdims=True)
-            parts.append(weight * (slope - inner))
-        grad_s = jnp.concatenate(parts, axis=1).astype(BF16)
-        both = jnp.concatenate([key * low, key * high], axis=0)
-        grad_q = dot(grad_s, both) * SCALE
-        grad_k = dot(grad_s, query, 0, 0)
-        grad_k = jnp.where(is_low, grad_k[:BLK], grad_k[BLK:]) * SCALE
         start = pair * LANES
-        out_ref[:, start : start + LANES] = (
-            grad_q * cosine - turned(grad_q) * sine
-        ).astype(BF16)
-        out_ref[:, D + start : D + start + LANES] = (
-            grad_k * cosine - turned(grad_k) * sine
-        ).astype(BF16)
-        out_ref[:, 2 * D + start : 2 * D + start + LANES] = grad_v.astype(BF16)
+        lanes = slice(start, start + LANES)
+        results = attend_back_pair(
+            q_ref[:, lanes],
+            k_ref[:, lanes],
+            v_ref[:, lanes],
+            grad_ref[:, lanes],
+            prob_ref[0, pair],
+            cos_ref[...],
+            sin_ref[...],
+        )
+        for part, result in enumerate(results):
+            out_ref[:, part * D + start : part * D + start + LANES] = result
 
 
 def attend_back(qkv, grad_o, prob, cosine, sine):
@@ -686,17 +670,21 @@
 
 
 MESH = pl.DeviceIdType.MESH
-REDUCE_CHUNKS = (
+EARLY_CHUNKS = (
     (0, 0, 512),
     (0, 512, 512),
-    (1, 0, 1792),
-    (1, 1792, 1792),
-    (1, 3584, 1792),
+    *[(1, i * 768, 768) for i in range(7)],
     (2, 0, 1024),
-    (3, 0, 1536),
-    (3, 1536, 1536),
+)
+LATE_CHUNKS = (
+    (3, 0, 768),
+    (3, 768, 768),
+    (3, 1536, 768),
+    (3, 2304, 512),
     (4, 0, 256),
+    (3, 2816, 256),
 )
+REDUCE_CHUNKS = EARLY_CHUNKS + LATE_CHUNKS
 HOP_CORE, HOP_X, HOP_Y, HOP_XY, HOP_YX, HOP_IN, HOP_MID, HOP_OUT = range(8)
 
 
@@ -706,10 +694,62 @@
     return rep, grp, core, x, y, grp + 1 - 2 * core, grp + 2 - 4 * x, grp + 4 - 8 * y
 
 
-def reduce_kernel(*refs):
-    tensors, refs = refs[:5], refs[5:]
-    outs, refs = refs[:5], refs[5:]
-    chunks = len(REDUCE_CHUNKS)
+def mesh_id(index):
+    return (index // SHARDS, lax.rem(index, SHARDS))
+
+
+def greet_all(devices):
+    device = position(devices)
+    barrier = pltpu.get_barrier_semaphore()
+
+    def greet(step, carry):
+        to = mesh_id(lax.rem(device + step, devices))
+        pl.semaphore_signal(barrier, device_id=to, device_id_type=MESH)
+        return carry
+
+    lax.fori_loop(1, devices, greet, 0)
+    pl.semaphore_wait(barrier, devices - 1)
+
+
+def row_exchange(send, land, local_sem, send_sem, recv_sem, devices):
+    device = position(devices)
+
+    def copy(step, slot):
+        to = lax.rem(device + step, devices)
+        return pltpu.make_async_remote_copy(
+            src_ref=send(to),
+            dst_ref=land(slot),
+            send_sem=send_sem.at[step],
+            recv_sem=recv_sem.at[step],
+            device_id=mesh_id(to),
+            device_id_type=MESH,
+        )
+
+    def keep():
+        return pltpu.make_async_copy(send(device), land(device), local_sem)
+
+    def start():
+        def one(step, carry):
+            copy(step, device).start()
+            return carry
+
+        keep().start()
+        lax.fori_loop(1, devices, one, 0)
+
+    def finish():
+        def one(step, carry):
+            copy(step, lax.rem(device + devices - step, devices)).wait_recv()
+            copy(step, device).wait_send()
+            return carry
+
+        lax.fori_loop(1, devices, one, 0)
+        keep().wait()
+
+    return start, finish
+
+
+def reduction(table, tensors, outs, refs):
+    chunks = len(table)
     sums, from_core, from_near, from_cross, from_far = (
         refs[i * chunks : (i + 1) * chunks] for i in range(5)
     )
@@ -718,23 +758,8 @@
     is_middle = (rep == 1) | (rep == 2)
     inward, outward, across = 1 + rep // 2, 3 * (rep // 2), 3 - rep
 
-    barrier = pltpu.get_barrier_semaphore()
-    for near in (by_core, by_x, by_y):
-        pl.semaphore_signal(barrier, device_id=(rep, near), device_id_type=MESH)
-
-    @pl.when(is_middle)
-    def _():
-        pl.semaphore_signal(barrier, device_id=(across, grp), device_id_type=MESH)
-        pl.semaphore_signal(barrier, device_id=(outward, grp), device_id_type=MESH)
-        pl.semaphore_wait(barrier, 5)
-
-    @pl.when(jnp.logical_not(is_middle))
-    def _():
-        pl.semaphore_signal(barrier, device_id=(inward, grp), device_id_type=MESH)
-        pl.semaphore_wait(barrier, 4)
-
     def hop(chunk, which):
-        tensor, start, width = REDUCE_CHUNKS[chunk]
+        tensor, start, width = table[chunk]
         half = width // 2
         left, right, columns = pl.ds(0, half), pl.ds(half, half), pl.ds(start, width)
         total, far = sums[chunk], from_far[chunk]
@@ -767,7 +792,7 @@
         )
 
     def load(chunk):
-        tensor, start, width = REDUCE_CHUNKS[chunk]
+        tensor, start, width = table[chunk]
         return pltpu.make_async_copy(
             tensors[tensor].at[:, :, core, :, pl.ds(start, width)],
             sums[chunk],
@@ -775,7 +800,7 @@
         )
 
     def store(chunk):
-        tensor, start, width = REDUCE_CHUNKS[chunk]
+        tensor, start, width = table[chunk]
         return pltpu.make_async_copy(
             from_far[chunk].at[0],
             outs[tensor].at[:, pl.ds(start, width)],
@@ -800,7 +825,7 @@
         hop(chunk, HOP_Y).start()
 
     def after_near(chunk):
-        half = REDUCE_CHUNKS[chunk][2] // 2
+        half = table[chunk][2] // 2
         hop(chunk, HOP_X).wait_recv()
         hop(chunk, HOP_Y).wait_recv()
         total, near = sums[chunk], from_near[chunk]
@@ -815,7 +840,7 @@
         hop(chunk, HOP_YX).start()
 
     def after_cross(chunk):
-        half = REDUCE_CHUNKS[chunk][2] // 2
+        half = table[chunk][2] // 2
         hop(chunk, HOP_XY).wait_recv()
         hop(chunk, HOP_YX).wait_recv()
         total, cross = sums[chunk], from_cross[chunk]
@@ -843,59 +868,359 @@
             hop(chunk, HOP_OUT).start()
             store(chunk).start()
 
-    for chunk in range(chunks):
-        load(chunk).start()
-        hop(chunk, HOP_CORE).start()
+    def start(some):
+        for chunk in some:
+            load(chunk).start()
+            hop(chunk, HOP_CORE).start()
+
     stages = (after_core, after_near, after_cross, after_in, after_middle)
-    for step in range(chunks + len(stages) - 1):
+
+    def one_step(step):
         for late, stage in enumerate(stages):
             if 0 <= step - late < chunks:
                 stage(step - late)
-    for chunk in range(chunks):
-        for which in (HOP_CORE, HOP_X, HOP_Y, HOP_XY, HOP_YX):
-            hop(chunk, which).wait_send()
-
-    @pl.when(is_middle)
-    def _():
+
+    steps = [functools.partial(one_step, i) for i in range(chunks + len(stages) - 1)]
+
+    def finish():
         for chunk in range(chunks):
-            hop(chunk, HOP_MID).wait_send()
-            hop(chunk, HOP_OUT).wait_send()
-            store(chunk).wait()
-
-    @pl.when(jnp.logical_not(is_middle))
-    def _():
-        for chunk in range(chunks):
-            hop(chunk, HOP_IN).wait_send()
-            hop(chunk, HOP_OUT).wait_recv()
-
-
-def reduce_all(parts):
-    split = [part.reshape(2, 2, 2, -1, part.shape[-1]) for part in parts]
-    kinds = [(split[t].dtype, split[t].shape[3], width) for t, _, width in REDUCE_CHUNKS]
+            for which in (HOP_CORE, HOP_X, HOP_Y, HOP_XY, HOP_YX):
+                hop(chunk, which).wait_send()
+
+        @pl.when(is_middle)
+        def _():
+            for chunk in range(chunks):
+                hop(chunk, HOP_MID).wait_send()
+                hop(chunk, HOP_OUT).wait_send()
+                store(chunk).wait()
+
+        @pl.when(jnp.logical_not(is_middle))
+        def _():
+            for chunk in range(chunks):
+                hop(chunk, HOP_IN).wait_send()
+                hop(chunk, HOP_OUT).wait_recv()
+
+    return start, steps, finish
+
+
+def reduction_scratch(table, split):
+    kinds = [(split[t].dtype, split[t].shape[3], width) for t, _, width in table]
+    dma = pltpu.SemaphoreType.DMA
+    return [
+        *[pltpu.VMEM((2, 2, r, w), t) for t, r, w in kinds],
+        *[pltpu.VMEM((2, 2, r, w), t) for t, r, w in kinds],
+        *[pltpu.VMEM((2, 2, r, w // 2), t) for t, r, w in kinds],
+        *[pltpu.VMEM((2, r, w // 2), t) for t, r, w in kinds],
+        *[pltpu.VMEM((2, r, w), t) for t, r, w in kinds],
+        dma((len(table),)),
+        dma((len(table), 8)),
+        dma((len(table), 8)),
+        dma((len(table),)),
+    ]
+
+
+def split_shards(parts):
+    return [part.reshape(2, 2, 2, -1, part.shape[-1]) for part in parts]
+
+
+def attend_back_pair(query, key, value, grad, prob, cosine, sine):
+    low, high = head_masks(BF16)
+    is_low = lax.broadcasted_iota(jnp.int32, (BLK, LANES), 1) < HD
+    grad_v = dot(prob, grad, 0, 0)
+    grad_v = jnp.where(is_low, grad_v[:BLK], grad_v[BLK:])
+    grad_p = dot(grad, jnp.concatenate([value * low, value * high], axis=0), 1, 1)
+    parts = []
+    for head in range(2):
+        keys = slice(head * BLK, (head + 1) * BLK)
+        weight, slope = prob[:, keys].astype(F32), grad_p[:, keys]
+        inner = jnp.sum(weight * slope, axis=-1, keepdims=True)
+        parts.append(weight * (slope - inner))
+    grad_s = jnp.concatenate(parts, axis=1).astype(BF16)
+    both = jnp.concatenate([key * low, key * high], axis=0)
+    grad_q = dot(grad_s, both) * SCALE
+    grad_k = dot(grad_s, query, 0, 0)
+    grad_k = jnp.where(is_low, grad_k[:BLK], grad_k[BLK:]) * SCALE
+    return (
+        (grad_q * cosine - turned(grad_q) * sine).astype(BF16),
+        (grad_k * cosine - turned(grad_k) * sine).astype(BF16),
+        grad_v.astype(BF16),
+    )
+
+
+FEATURES = D // SHARDS
+SOME_ROWS = 128
+
+
+def interleave(steps, pieces, ahead):
+    for piece in pieces[:ahead]:
+        piece()
+    pieces = pieces[ahead:]
+    done = 0
+    for index, step in enumerate(steps):
+        step()
+        upto = -(-len(pieces) * (index + 1) // len(steps))
+        for piece in pieces[done:upto]:
+            piece()
+        done = upto
+
+
+def return_kernel(devices, micros, *refs):
+    groups = MICRO // micros
+    early = refs[:3]
+    send, lengths_ref, qkv_ref, prob_ref, grad_o_ref, act_ref, hidden_ref = refs[3:10]
+    mid_ref, weight_ref, gain_ref, other_ref, cos_ref, sin_ref = refs[10:16]
+    outs, layer_land, grad_land, grad_w_ref, gains_ref = refs[16:21], *refs[21:25]
+    wide, grads, block_prob, block_grad, act_part, w_part = refs[25:31]
+    row_hidden, row_mid, kept, packed, grad_gain, gain_parts = refs[31:37]
+    wide_sem, block_sem, act_sem, w_sem, row_sem, gain_sem = refs[37:43]
+    layer_sems, grad_sems, refs = refs[43:46], refs[46:49], refs[49:]
+    tensors = (*early, grad_w_ref, gains_ref)
+    start, steps, finish = reduction(REDUCE_CHUNKS, tensors, outs, refs)
+    start_layer, finish_layer = row_exchange(
+        lambda to: send.at[to], lambda slot: layer_land.at[slot], *layer_sems, devices
+    )
+    exchanges = [
+        row_exchange(
+            lambda to, group=group: packed.at[group, to],
+            lambda slot, group=group: grad_land.at[slot, group],
+            *[sem.at[group] for sem in grad_sems],
+            devices,
+        )
+        for group in range(groups)
+    ]
+    copy = pltpu.make_async_copy
+
+    def block_loads(block):
+        slot = block % 2
+        rows = pl.ds(block * BLK, BLK)
+        return (
+            copy(prob_ref.at[block], block_prob.at[slot], block_sem.at[slot, 0]),
+            copy(grad_o_ref.at[rows], block_grad.at[slot], block_sem.at[slot, 1]),
+        )
+
+    def act_load(part):
+        columns = pl.ds(part * FEATURES, FEATURES)
+        return copy(act_ref.at[:, columns], act_part.at[part % 2], act_sem.at[part % 2])
+
+    def w_store(part):
+        target = grad_w_ref.at[part // 4, part // 2 % 2, part % 2]
+        return copy(w_part.at[part % 2], target, w_sem.at[part % 2])
+
+    def row_loads(part):
+        slot = part % 2
+        rows = pl.ds(part * SOME_ROWS, SOME_ROWS)
+        return (
+            copy(hidden_ref.at[rows], row_hidden.at[slot], row_sem.at[slot, 0]),
+            copy(mid_ref.at[rows], row_mid.at[slot], row_sem.at[slot, 1]),
+        )
+
+    load_qkv = copy(qkv_ref, wide, wide_sem.at[0])
+    load_weight = copy(weight_ref, wide, wide_sem.at[1])
+
+    def attend_piece(block):
+        if block == 0:
+            load_qkv.wait()
+        for load in block_loads(block):
+            load.wait()
+        if block + 1 < BLOCKS:
+            for load in block_loads(block + 1):
+                load.start()
+        slot = block % 2
+        rows = slice(block * BLK, (block + 1) * BLK)
+
+        def two(index, carry):
+            for inner in range(2):
+                pair = index * 2 + inner
+                base = pl.multiple_of(pair * LANES, LANES)
+                columns = [
+                    pl.ds(pl.multiple_of(part * D + base, LANES), LANES) for part in range(3)
+                ]
+                results = attend_back_pair(
+                    *[wide[rows, c] for c in columns],
+                    block_grad[slot, :, pl.ds(base, LANES)],
+                    block_prob[slot, pair],
+                    cos_ref[...],
+                    sin_ref[...],
+                )
+                for c, result in zip(columns, results):
+                    grads[rows, c] = result
+            return carry
+
+        lax.fori_loop(0, PAIRS // 2, two, 0)
+        if block == BLOCKS - 1:
+            load_weight.start()
+            act_load(0).start()
+
+    def weight_piece(part):
+        act_load(part).wait()
+        if part + 1 < SHARDS:
+            act_load(part + 1).start()
+        if part >= 2:
+            w_store(part - 2).wait()
+        act_t = act_part[part % 2].T
+        for third in range(3):
+            columns = slice(third * D, (third + 1) * D)
+            w_part[part % 2, :, columns] = dot(act_t, grads[:, columns]).astype(BF16)
+        w_store(part).start()
+        if part == SHARDS - 1:
+            w_store(part - 1).wait()
+            w_store(part).wait()
+            start([i for i, c in enumerate(REDUCE_CHUNKS) if c[0] == 3])
+            for load in row_loads(0):
+                load.start()
+
+    def row_piece(part):
+        if part == 0:
+            load_weight.wait()
+            grad_gain[...] = jnp.zeros_like(grad_gain)
+        for load in row_loads(part):
+            load.wait()
+        if part + 1 < BLOCKS:
+            for load in row_loads(part + 1):
+                load.start()
+        slot = part % 2
+        rows = slice(part * SOME_ROWS, (part + 1) * SOME_ROWS)
+        grad_a = dot(grads[rows, :], wide[...], 1, 1)
+        normal, inverse = normed(row_hidden[slot].astype(F32))
+        grad_gain[...] += jnp.sum(grad_a * normal, axis=0, keepdims=True)
+        each = BLOCKS // groups
+        inner = slice(part % each * SOME_ROWS, (part % each + 1) * SOME_ROWS)
+        kept[inner] = (
+            row_mid[slot] + norm_back(grad_a * gain_ref[...], normal, inverse)
+        ).astype(BF16)
+        if part % each == each - 1:
+            group = part // each
+            pick = held_rows(lengths_ref, group, micros, devices)
+            packed[group] = (
+                dot(pick, kept[...], 0, 0).astype(BF16).reshape(packed.shape[1:])
+            )
+            exchanges[group][0]()
+
+    def gain_piece():
+        width = D // SHARDS
+        for shard in range(SHARDS):
+            columns = slice(shard * width, (shard + 1) * width)
+            for part, values in enumerate((grad_gain, other_ref)):
+                gain_parts[shard // 4, shard // 2 % 2, shard % 2, :, part * width : (part + 1) * width] = (
+                    jnp.broadcast_to(values[:, columns], (GAIN_ROWS, width))
+                )
+        keep = copy(gain_parts, gains_ref, gain_sem)
+        keep.start()
+        keep.wait()
+        start([i for i, c in enumerate(REDUCE_CHUNKS) if c[0] == 4])
+
+    greet_all(devices)
+    load_qkv.start()
+    for load in block_loads(0):
+        load.start()
+    start(range(len(EARLY_CHUNKS)))
+    start_layer()
+    pieces = [
+        *[functools.partial(attend_piece, i) for i in range(BLOCKS)],
+        *[functools.partial(weight_piece, i) for i in range(SHARDS)],
+        *[functools.partial(row_piece, i) for i in range(BLOCKS)],
+        gain_piece,
+    ]
+    count = len(EARLY_CHUNKS)
+    interleave(steps[:count], pieces, 2)
+    for step in steps[count:]:
+        step()
+    finish()
+    finish_layer()
+    for exchange in exchanges:
+        exchange[1]()
+
+
+def return_all(
+    parts,
+    send,
+    lengths,
+    qkv,
+    prob,
+    grad_o,
+    act,
+    hidden,
+    grad_mid,
+    weight,
+    gain,
+    other,
+    tables,
+    devices,
+    micros,
+):
+    early = split_shards(parts)
+    groups = MICRO // micros
+    rows = D // SHARDS
+    split = [
+        *early,
+        jax.ShapeDtypeStruct((2, 2, 2, rows, 3 * D), BF16),
+        jax.ShapeDtypeStruct((2, 2, 2, GAIN_ROWS, 2 * rows), F32),
+    ]
     anywhere = pl.BlockSpec(memory_space=pl.ANY)
-    chunks = len(REDUCE_CHUNKS)
-    moved = sum(v.size for v in split)
-    return pl.pallas_call(
-        reduce_kernel,
-        in_specs=[anywhere] * len(parts),
-        out_specs=[anywhere] * len(parts),
-        out_shape=[jax.ShapeDtypeStruct(v.shape[3:], v.dtype) for v in split],
+    inside = pl.BlockSpec(memory_space=pltpu.VMEM)
+    dma = pltpu.SemaphoreType.DMA
+    *owned, layer_back, grad_back, _, _ = pl.pallas_call(
+        functools.partial(return_kernel, devices, micros),
+        in_specs=[
+            *[anywhere] * 4,
+            inside,
+            *[anywhere] * 7,
+            *[inside] * 4,
+        ],
+        out_specs=[anywhere] * 9,
+        out_shape=[
+            *[jax.ShapeDtypeStruct(v.shape[3:], v.dtype) for v in split],
+            jax.ShapeDtypeStruct(send.shape, send.dtype),
+            jax.ShapeDtypeStruct(send.shape, send.dtype),
+            *split[3:],
+        ],
         scratch_shapes=[
-            *[pltpu.VMEM((2, 2, r, w), t) for t, r, w in kinds],
-            *[pltpu.VMEM((2, 2, r, w), t) for t, r, w in kinds],
-            *[pltpu.VMEM((2, 2, r, w // 2), t) for t, r, w in kinds],
-            *[pltpu.VMEM((2, r, w // 2), t) for t, r, w in kinds],
-            *[pltpu.VMEM((2, r, w), t) for t, r, w in kinds],
-            pltpu.SemaphoreType.DMA((chunks,)),
-            pltpu.SemaphoreType.DMA((chunks, 8)),
-            pltpu.SemaphoreType.DMA((chunks, 8)),
-            pltpu.SemaphoreType.DMA((chunks,)),
+            pltpu.VMEM((ROWS, 3 * D), BF16),
+            pltpu.VMEM((ROWS, 3 * D), BF16),
+            pltpu.VMEM((2, PAIRS, BLK, 2 * BLK), BF16),
+            pltpu.VMEM((2, BLK, D), BF16),
+            pltpu.VMEM((2, ROWS, FEATURES), BF16),
+            pltpu.VMEM((2, FEATURES, 3 * D), BF16),
+            pltpu.VMEM((2, SOME_ROWS, D), BF16),
+            pltpu.VMEM((2, SOME_ROWS, D), F32),
+            pltpu.VMEM((ROWS // groups, D), BF16),
+            pltpu.VMEM((groups, devices, CHUNK_ROWS, D), BF16),
+            pltpu.VMEM((1, D), F32),
+            pltpu.VMEM((2, 2, 2, GAIN_ROWS, 2 * rows), F32),
+            dma((2,)),
+            dma((2, 2)),
+            dma((2,)),
+            dma((2,)),
+            dma((2, 2)),
+            dma,
+            dma,
+            dma((devices,)),
+            dma((devices,)),
+            dma((groups,)),
+            dma((groups, devices)),
+            dma((groups, devices)),
+            *reduction_scratch(REDUCE_CHUNKS, split),
         ],
         compiler_params=pltpu.CompilerParams(
-            vmem_limit_bytes=60 * MIB, collective_id=1, has_side_effects=True
+            vmem_limit_bytes=63 * MIB, collective_id=1, has_side_effects=True
         ),
-        cost_estimate=cost(2 * moved, 40 * moved),
-    )(*split)
+        cost_estimate=cost(16 * ROWS * D * D, 600 * MIB),
+    )(
+        *early,
+        send,
+        lengths,
+        qkv,
+        prob,
+        grad_o,
+        act,
+        hidden,
+        grad_mid,
+        weight,
+        gain,
+        other,
+        *tables,
+    )
+    return (*owned, layer_back, grad_back)
 
 
 WAY_X, WAY_Y, WAY_CORE, WAY_CORE_X, WAY_CORE_Y = range(5)
@@ -1143,30 +1468,47 @@
     middle, act_b = middle_rows(attn_o, hidden, full_out, gain_two)
     layer_rows, grad_b, grad_in_w, grad_down_w = ffn(act_b, top, middle, full_in, full_down)
     layer_send = repack_rows(seq_lengths, layer_rows, devices, micros)
-    layer_back = swap(layer_send)
     grad_mid, grad_o, grad_out_w, grad_gain_two = branch_back(
         layer_send, grad_b, middle, top, attn_o, full_out, gain_two
     )
-    grad_qkv_rows = attend_back(qkv, grad_o, prob, cosine, sine)
-    grad_qkv_w = qkv_grad(act_a, grad_qkv_rows)
-    grad_rows, gain_parts = input_back(
-        grad_qkv_rows, full_qkv, hidden, grad_mid, gain_one, grad_gain_two
-    )
-    grad_back = swap(repack_rows(seq_lengths, grad_rows, devices, micros))
-    parts = (grad_down_w, grad_in_w, grad_out_w, grad_qkv_w)
     if near:
-        *owned, gain_sums = reduce_all((*parts, gain_parts))
+        grad_down, grad_in, grad_out, grad_qkv, gain_sums, layer_back, grad_back = return_all(
+            (grad_down_w, grad_in_w, grad_out_w),
+            layer_send,
+            seq_lengths,
+            qkv,
+            prob,
+            grad_o,
+            act_a,
+            hidden,
+            grad_mid,
+            full_qkv,
+            gain_one,
+            grad_gain_two,
+            (cosine, sine),
+            devices,
+            micros,
+        )
         gain_sums = gain_sums[0].reshape(2, -1)
     else:
-        owned = [
+        layer_back = swap(layer_send)
+        grad_qkv_rows = attend_back(qkv, grad_o, prob, cosine, sine)
+        grad_qkv_w = qkv_grad(act_a, grad_qkv_rows)
+        grad_rows, gain_parts = input_back(
+            grad_qkv_rows, full_qkv, hidden, grad_mid, gain_one, grad_gain_two
+        )
+        grad_back = swap(repack_rows(seq_lengths, grad_rows, devices, micros))
+        grad_down, grad_in, grad_out, grad_qkv = (
             lax.psum(lax.psum_scatter(v, "grp", scatter_dimension=0, tiled=True), "rep")
-            for v in parts
-        ]
+            for v in (grad_down_w, grad_in_w, grad_out_w, grad_qkv_w)
+        )
         gain_parts = gain_parts[:, 0].reshape(SHARDS, 2, -1).swapaxes(0, 1).reshape(2, D)
         gain_sums = lax.psum(
             lax.psum_scatter(gain_parts, "grp", scatter_dimension=1, tiled=True), "rep"
         )
-    grad_down, grad_in, grad_out, grad_qkv = (v.astype(F32) for v in owned)
+    grad_down, grad_in, grad_out, grad_qkv = (
+        v.astype(F32) for v in (grad_down, grad_in, grad_out, grad_qkv)
+    )
     layer_out = spread_rows(seq_lengths, layer_back, devices, micros)[:, :, None, :]
     grad_tokens = spread_rows(seq_lengths, grad_back, devices, micros)[:, :, None, :]
     return (

time: 591 us -> 514 us (0.87)
  blocking collectives: 51.3 us -> 0 us
  local copies, waits for them, and re-layouts: 37.5 us -> 22.6 us
  Pallas kernels: 491 us -> 479 us
    all_to_all x1 -> x0, blocking collectives: 51.3 us -> none  [swap(): return lax.all_to_all(rows, both, split_axis=0, concat_axis=0, tiled=True)]
    unnamed x84 -> x74, local copies, waits for them, and re-layouts: 27.8 us -> 15.2 us
    pallas_call x4 -> x1, Pallas kernels: 198 us -> 188 us  [return_all(): pl.pallas_call(functools.partial(return_kernel, devices, micros), in_spec...]
  transfers between devices with their start and end apart: 1 -> 0, of which waited for: 0 -> 0; matrix products, arithmetic and copies ran while one was open for 2% -> 0% of each run, Pallas kernels for 28% -> 0%
where the time goes in v4:
time: 514 us; the launch traced here: 508 us
  Pallas kernels  479 us (93%)
  local copies, waits for them, and re-layouts  22.6 us (4%)
    pallas_call x1, Pallas kernels, return_all(): pl.pallas_call(functools.partial(return_kernel, devices, micros), in_spec...  188 us
    pallas_call x1, Pallas kernels, gather_all(): pl.pallas_call(functools.partial(gather_kernel, devices), in_specs=[anywh...  159 us
    pallas_call x1, Pallas kernels, ffn(): pl.pallas_call(ffn_kernel, grid=(FF_STEPS,), in_specs=[whole, whole, whol...  73.3 us
    pallas_call x1, Pallas kernels, qkv_rows(): pl.pallas_call(qkv_kernel, grid=(3 * D // QKV_TILE,), in_specs=[pl.BlockS...  16.6 us
    unnamed x74, local copies, waits for them, and re-layouts  15.2 us
    pallas_call x1, Pallas kernels, branch_back(): pl.pallas_call(branch_kernel, grid=(ROWS // ROW_CHUNK,), in_specs=[pl.Blo...  11.5 us

profile of v4, /device:TPU:0, one launch (start us, length us, event | category | flops | bytes accessed | tf_op | source)
XLA Modules:
  0.0 507.7 jit_solution(6389183024614300611)
XLA Ops:
  1.3 1.3 fusion.4.refs_4_
  2.6 1.5 slice.165
  6.2 4.0 shard_map.170
  10.2 1.3 copy-done.7
  11.5 159.0 %shard_map.171 = (bf16[8,328,1024]{2,1,0:T(8,128)(2,1)}, bf16[8,128,5376]{2,1,0:T(8,128)(2,1)}, bf16[8,128,1024]{2,1,0:T(8,128)(2,1)}, bf16[8,128,3072]{2,1,0:T(...) custom-call(bf16[328,1024]{1,0:T(8,128)(2,1)} %refs_0_.1, ...), custom_call_target="tpu_custom_call" | custom-call | bytes 231735296 | tf_op jit(solution)/shard_map/pallas_call | solution.py:1393
  171.2 6.1 %shard_map.172 = (bf16[1024,1024]{1,0:T(8,128)(2,1)S(1)}, bf16[1024,1024]{1,0:T(8,128)(2,1)S(1)}, bf16[1024,1024]{1,0:T(8,128)(2,1)}) custom-call(s32[4,64]{1,0:T(4,128)S(1)} %copy-done.11, bf16[32,2,16,1024]{3,2,1,0:T(8,128)(2,1)} %get-tuple-element.41.token_ref, bf16[32,2,16,1024]{3,2,1,0:T(8,128)(2,1)} %get-tuple-element.42.top_ref, ...), custom_call_target="tpu_custom_call" | custom-call | flops 2147483648 | bytes 8388608 | tf_op jit(solution)/shard_map/pallas_call | solution.py:242
  177.4 16.6 %shard_map.173.q_ref.k_ref.v_ref.refs_5_ = bf16[1024,3072]{1,0:T(8,128)(2,1)S(1)} custom-call(bf16[1024,1024]{1,0:T(8,128)(2,1)S(1)} %get-tuple-element.44.act_ref.refs_8_, bf16[1024,3072]{1,0:T(8,128)(2,1)} %bitcast.43, f32[128,128]{1,0:T(8,128)S(1)} %copy-done.21, f32[128,128]{1,0:T(8,128)S(1)} %copy-done.20), custom_call_target="tpu_custom_call" | custom-call | flops 6442450944 | bytes 14680064 | tf_op jit(solution)/shard_map/pallas_call | solution.py:299
  194.0 9.8 %shard_map.174 = (bf16[1024,1024]{1,0:T(8,128)(2,1)S(1)}, bf16[8,8,128,256]{3,2,1,0:T(8,128)(2,1)S(1)}) custom-call(s32[4,64]{1,0:T(4,128)S(1)} %copy-done.11, bf16[1024,3072]{1,0:T(8,128)(2,1)S(1)} %shard_map.173.q_ref.k_ref.v_ref.refs_5_, bf16[1024,3072]{1,0:T(8,128)(2,1)S(1)} %shard_map.173.q_ref.k_ref.v_ref.refs_5_, ...), custom_call_target="tpu_custom_call" | custom-call | flops 1073741824 | bytes 12582912 | tf_op jit(solution)/shard_map/pallas_call | solution.py:350
  203.9 1.9 copy-done.14
  205.8 3.9 shard_map.175
  209.8 2.0 copy-done.2
  211.8 1.3 copy-done.23
  213.1 73.3 %shard_map.176 = (bf16[1024,1024]{1,0:T(8,128)(2,1)}, f32[1024,1024]{1,0:T(8,128)}, bf16[1024,5376]{1,0:T(8,128)(2,1)}, bf16[2624,1024]{1,0:T(8,128)(2,1)}) custom-call(bf16[1024,1024]{1,0:T(8,128)(2,1)} %copy-done.23, bf16[1024,1024]{1,0:T(8,128)(2,1)} %get-tuple-element.50.top_ref, f32[1024,1024]{1,0:T(8,128)} %copy-done.2, bf16[1024,5376]{1,0:T(8,128)(2,1)} %bitcast.42, ...), custom_call_target="tpu_custom_call" | custom-call | flops 49526341632 | bytes 32243712 | tf_op jit(solution)/shard_map/pallas_call | solution.py:495
  286.4 1.6 copy-done.10
  288.0 2.0 shard_map.177.order_ref.refs_3_
  290.2 11.5 %shard_map.178 = (f32[1024,1024]{1,0:T(8,128)}, bf16[1024,1024]{1,0:T(8,128)(2,1)S(1)}, bf16[1024,1024]{1,0:T(8,128)(2,1)S(1)}, f32[1,1024]{1,0:T(1,128)S(1)}) custom-call(bf16[32,2,16,1024]{3,2,1,0:T(8,128)(2,1)S(1)} %shard_map.177.order_ref.refs_3_, f32[1024,1024]{1,0:T(8,128)} %get-tuple-element.57.grad_b_ref, f32[1024,1024]{1,0:T(8,128)} %copy-done.2, ...), custom_call_target="tpu_custom_call" | custom-call | flops 4294967296 | bytes 23068672 | tf_op jit(solution)/shard_map/pallas_call | solution.py:565
  301.8 1.3 copy-done.15
  303.1 1.3 copy-done.16
  305.0 187.9 %shard_map.179 = (bf16[328,1024]{1,0:T(8,128)(2,1)}, bf16[128,5376]{1,0:T(8,128)(2,1)}, bf16[128,1024]{1,0:T(8,128)(2,1)}, bf16[128,3072]{1,0:T(8,128)(2,1)}, f3...) custom-call(bf16[2,2,2,328,1024]{4,3,2,1,0:T(8,128)(2,1)} %bitcast.4, ...), custom_call_target="tpu_custom_call" | custom-call | flops 17179869184 | bytes 629145600 | tf_op jit(solution)/shard_map/pallas_call | solution.py:1162
  493.0 1.6 copy-done.9
  494.6 2.4 shard_map.180
  497.0 2.5 shard_map.181
  501.8 2.9 concatenate.15
  506.0 1.3 convert_element_type.28
  (78 shorter events, 8.0 us)
Async XLA Ops:
  2.6 1.5 copy-start.26
  4.1 1.6 copy-start.18
  4.3 1.9 copy-start.17
  6.2 4.0 copy-start.27
  171.2 6.2 %copy-start.13 = (f32[1,1024]{1,0:T(1,128)}, f32[1,1024]{1,0:T(1,128)S(1)}, u32[]{:S(2)}) copy-start(f32[1,1024]{1,0:T(1,128)S(1)} %get-tuple-element.95.gain_ref.refs_12_) | copy-start | bytes 12292
  171.2 6.2 %copy-start.20 = (f32[128,128]{1,0:T(8,128)S(1)}, f32[128,128]{1,0:T(8,128)}, u32[]{:S(2)}) copy-start(f32[128,128]{1,0:T(8,128)} %constant.11.clone.sin_ref.refs_15_) | copy-start | bytes 196612
  171.2 6.2 %copy-start.21 = (f32[128,128]{1,0:T(8,128)S(1)}, f32[128,128]{1,0:T(8,128)}, u32[]{:S(2)}) copy-start(f32[128,128]{1,0:T(8,128)} %constant.10.clone.cos_ref.refs_14_) | copy-start | bytes 196612
  177.4 16.6 %copy-start.24 = (bf16[1024,1024]{1,0:T(8,128)(2,1)}, bf16[1024,1024]{1,0:T(8,128)(2,1)S(1)}, u32[]{:S(2)}) copy-start(bf16[1024,1024]{1,0:T(8,128)(2,1)S(1)} %get-tuple-element.44.act_ref.refs_8_) | copy-start | bytes 6291460
  177.4 28.4 %copy-start.22 = (bf16[1024,1024]{1,0:T(8,128)(2,1)}, bf16[1024,1024]{1,0:T(8,128)(2,1)S(1)}, u32[]{:S(2)}) copy-start(bf16[1024,1024]{1,0:T(8,128)(2,1)S(1)} %get-tuple-element.47.hidden_ref.refs_9_) | copy-start | bytes 6291460
  194.0 9.8 %copy-start = (bf16[1024,3072]{1,0:T(8,128)(2,1)}, bf16[1024,3072]{1,0:T(8,128)(2,1)S(1)}, u32[]{:S(2)}) copy-start(bf16[1024,3072]{1,0:T(8,128)(2,1)S(1)} %shard_map.173.q_ref.k_ref.v_ref.refs_5_) | copy-start | bytes 18874372
  194.0 11.8 %copy-start.3 = (bf16[8,128,1024]{2,1,0:T(8,128)(2,1)S(1)}, bf16[8,128,1024]{2,1,0:T(8,128)(2,1)}, u32[]{:S(2)}) copy-start(bf16[8,128,1024]{2,1,0:T(8,128)(2,1)} %get-tuple-element.48) | copy-start | bytes 6291460
  203.9 1.9 copy-start.14
  205.8 3.9 copy-start.5
  209.8 2.0 copy-start.2
  286.4 1.6 copy-start.10
  288.0 2.0 copy-start.4
  288.0 2.2 copy-start.6
  290.2 11.5 %copy-start.1 = (bf16[32,2,16,1024]{3,2,1,0:T(8,128)(2,1)}, bf16[32,2,16,1024]{3,2,1,0:T(8,128)(2,1)S(1)}, u32[]{:S(2)}) copy-start(bf16[32,2,16,1024]{3,2,1,0:T(8,128)(2,1)S(1)} %shard_map.177.order_ref.refs_3_) | copy-start | bytes 6291460
  305.0 188.0 %copy-start.12 = (s32[4,64]{1,0:T(4,128)S(1)}, s32[4,64]{1,0:T(4,128)}, u32[]{:S(2)}) copy-start(s32[4,64]{1,0:T(4,128)} %lengths_ref.9) | copy-start | bytes 3076
  493.0 1.6 copy-start.9
  494.6 2.4 copy-start.8
  497.0 3.7 copy-start.25
  497.0 3.7 copy-start.30
  501.8 2.9 copy-start.29
  (8 other events, 9.7 us)

commit v5 on v4

--- a/solution.py
+++ b/solution.py
@@ -31,8 +31,6 @@
 SCALE = HD**-0.5
 
 FF_TILE = 384
-FF_STEPS = -(-FF // FF_TILE)
-FF_PAD = FF_STEPS * FF_TILE
 ROW_CHUNK = 256
 CHUNK_ROWS = 16
 SHARDS = 8
@@ -319,31 +317,42 @@
     return low, high
 
 
+def attend_pair(query, key, value, valid):
+    low, high = head_masks(BF16)
+    scores = dot(query, jnp.concatenate([key * low, key * high], axis=0), 1, 1)
+    parts = []
+    for head in range(2):
+        score = scores[:, head * BLK : (head + 1) * BLK] * SCALE
+        score = jnp.where(valid, score, NEG)
+        expo = jnp.exp(score - jnp.max(score, axis=-1, keepdims=True))
+        parts.append(expo / jnp.sum(expo, axis=-1, keepdims=True))
+    prob = jnp.concatenate(parts, axis=1).astype(BF16)
+    both = jnp.concatenate([value * low, value * high], axis=0)
+    return dot(prob, both).astype(BF16), prob
+
+
+def block_lengths(length_ref, block, devices):
+    shape = (length_ref.shape[1], BLK)
+    own = lax.broadcasted_iota(jnp.int32, shape, 0) == (
+        SEQ_DEV * position(devices) + block
+    )
+    return length_sums(length_ref, own)
+
+
+def key_mask(length):
+    return lax.broadcasted_iota(jnp.int32, (BLK, BLK), 1).astype(F32) < length
+
+
 def attend_kernel(devices, length_ref, q_ref, k_ref, v_ref, out_ref, prob_ref):
     block = pl.program_id(0)
-    low, high = head_masks(BF16)
-    shape = (length_ref.shape[1], BLK)
-    own = lax.broadcasted_iota(jnp.int32, shape, 0) == (
-        SEQ_DEV * position(devices) + block % SEQ_DEV
-    )
-    lengths = length_sums(length_ref, own)
+    lengths = block_lengths(length_ref, block % SEQ_DEV, devices)
     micro = lax.broadcasted_iota(jnp.int32, lengths.shape, 0) == block // SEQ_DEV
-    length = jnp.sum(jnp.where(micro, lengths, 0.0), axis=0, keepdims=True)
-    valid = lax.broadcasted_iota(jnp.int32, (BLK, BLK), 1).astype(F32) < length
+    valid = key_mask(jnp.sum(jnp.where(micro, lengths, 0.0), axis=0, keepdims=True))
     for pair in range(PAIRS):
         lanes = slice(pair * LANES, (pair + 1) * LANES)
-        query, key, value = q_ref[:, lanes], k_ref[:, lanes], v_ref[:, lanes]
-        scores = dot(query, jnp.concatenate([key * low, key * high], axis=0), 1, 1)
-        parts = []
-        for head in range(2):
-            score = scores[:, head * BLK : (head + 1) * BLK] * SCALE
-            score = jnp.where(valid, score, NEG)
-            expo = jnp.exp(score - jnp.max(score, axis=-1, keepdims=True))
-            parts.append(expo / jnp.sum(expo, axis=-1, keepdims=True))
-        prob = jnp.concatenate(parts, axis=1).astype(BF16)
-        prob_ref[0, pair] = prob
-        both = jnp.concatenate([value * low, value * high], axis=0)
-        out_ref[:, lanes] = dot(prob, both).astype(BF16)
+        out_ref[:, lanes], prob_ref[0, pair] = attend_pair(
+            q_ref[:, lanes], k_ref[:, lanes], v_ref[:, lanes], valid
+        )
 
 
 def attend(qkv, lengths, devices):
@@ -447,7 +456,6 @@
     grad_down_ref,
     total,
     act_t,
-    down_clean,
     kept_c,
     kept_gu,
 ):
@@ -459,15 +467,12 @@
         grad_b_ref[...] = jnp.zeros_like(grad_b_ref)
         act_t[...] = act_ref[...].T
 
-    row = lax.broadcasted_iota(jnp.int32, (FF_TILE, D), 0) + step * FF_TILE
-    down_clean[...] = jnp.where(row < FF, down_ref[...].astype(F32), 0.0).astype(BF16)
-
     def rows_step(index, carry):
         rows = pl.ds(pl.multiple_of(index * ROW_CHUNK, ROW_CHUNK), ROW_CHUNK)
         act, top = act_ref[rows, :], top_ref[rows, :]
         gate_up = dot(act, in_ref[...])
         gelu_in, linear = gate_up[:, :FF_TILE], gate_up[:, FF_TILE:]
-        grad_c = dot(top, down_clean[...], 1, 1)
+        grad_c = dot(top, down_ref[...], 1, 1)
         phi = 0.5 * (1.0 + lax.erf(gelu_in * ROOT_HALF))
         gelu_out = gelu_in * phi
         slope = phi + gelu_in * (jnp.exp(-0.5 * gelu_in * gelu_in) * INV_ROOT_TWO_PI)
@@ -475,7 +480,7 @@
         kept_c[rows, :] = act_c
         kept_gu[rows, :FF_TILE] = (grad_c * linear * slope).astype(BF16)
         kept_gu[rows, FF_TILE:] = (grad_c * gelu_out).astype(BF16)
-        total[rows, :] += dot(act_c, down_clean[...])
+        total[rows, :] += dot(act_c, down_ref[...])
         grad_b_ref[rows, :] += dot(kept_gu[rows, :], in_ref[...], 1, 1)
         return carry
 
@@ -483,7 +488,7 @@
     grad_in_ref[...] = dot(act_t[...], kept_gu[...]).astype(BF16)
     grad_down_ref[...] = dot(kept_c[...], top_ref[...], 0, 0).astype(BF16)
 
-    @pl.when(step == FF_STEPS - 1)
+    @pl.when(step == pl.num_programs(0) - 1)
     def _():
         layer_ref[...] = total[...].astype(BF16)
 
@@ -494,7 +499,7 @@
     wide = pl.BlockSpec((FF_TILE, D), lambda j: (j, 0))
     return pl.pallas_call(
         ffn_kernel,
-        grid=(FF_STEPS,),
+        grid=(full_down.shape[0] // FF_TILE,),
         in_specs=[
             whole,
             whole,
@@ -506,13 +511,12 @@
         out_shape=[
             jax.ShapeDtypeStruct((ROWS, D), BF16),
             jax.ShapeDtypeStruct((ROWS, D), F32),
-            jax.ShapeDtypeStruct((D, 2 * FF_PAD), BF16),
-            jax.ShapeDtypeStruct((FF, D), BF16),
+            jax.ShapeDtypeStruct(full_in.shape, BF16),
+            jax.ShapeDtypeStruct(full_down.shape, BF16),
         ],
         scratch_shapes=[
             pltpu.VMEM((ROWS, D), F32),
             pltpu.VMEM((D, ROWS), BF16),
-            pltpu.VMEM((FF_TILE, D), BF16),
             pltpu.VMEM((ROWS, FF_TILE), BF16),
             pltpu.VMEM((ROWS, 2 * FF_TILE), BF16),
         ],
@@ -948,7 +952,8 @@
 
 
 FEATURES = D // SHARDS
-SOME_ROWS = 128
+SOME_ROWS = 256
+ROW_PIECES = ROWS // SOME_ROWS
 
 
 def interleave(steps, pieces, ahead):
@@ -1004,14 +1009,13 @@
 
     def w_store(part):
         target = grad_w_ref.at[part // 4, part // 2 % 2, part % 2]
-        return copy(w_part.at[part % 2], target, w_sem.at[part % 2])
+        return copy(w_part, target, w_sem)
 
     def row_loads(part):
-        slot = part % 2
         rows = pl.ds(part * SOME_ROWS, SOME_ROWS)
         return (
-            copy(hidden_ref.at[rows], row_hidden.at[slot], row_sem.at[slot, 0]),
-            copy(mid_ref.at[rows], row_mid.at[slot], row_sem.at[slot, 1]),
+            copy(hidden_ref.at[rows], row_hidden, row_sem.at[0]),
+            copy(mid_ref.at[rows], row_mid, row_sem.at[1]),
         )
 
     load_qkv = copy(qkv_ref, wide, wide_sem.at[0])
@@ -1029,8 +1033,8 @@
         rows = slice(block * BLK, (block + 1) * BLK)
 
         def two(index, carry):
-            for inner in range(2):
-                pair = index * 2 + inner
+            for inner in range(4):
+                pair = index * 4 + inner
                 base = pl.multiple_of(pair * LANES, LANES)
                 columns = [
                     pl.ds(pl.multiple_of(part * D + base, LANES), LANES) for part in range(3)
@@ -1046,7 +1050,7 @@
                     grads[rows, c] = result
             return carry
 
-        lax.fori_loop(0, PAIRS // 2, two, 0)
+        lax.fori_loop(0, PAIRS // 4, two, 0)
         if block == BLOCKS - 1:
             load_weight.start()
             act_load(0).start()
@@ -1055,15 +1059,14 @@
         act_load(part).wait()
         if part + 1 < SHARDS:
             act_load(part + 1).start()
-        if part >= 2:
-            w_store(part - 2).wait()
         act_t = act_part[part % 2].T
+        if part:
+            w_store(part - 1).wait()
         for third in range(3):
             columns = slice(third * D, (third + 1) * D)
-            w_part[part % 2, :, columns] = dot(act_t, grads[:, columns]).astype(BF16)
+            w_part[:, columns] = dot(act_t, grads[:, columns]).astype(BF16)
         w_store(part).start()
         if part == SHARDS - 1:
-            w_store(part - 1).wait()
             w_store(part).wait()
             start([i for i, c in enumerate(REDUCE_CHUNKS) if c[0] == 3])
             for load in row_loads(0):
@@ -1075,19 +1078,18 @@
             grad_gain[...] = jnp.zeros_like(grad_gain)
         for load in row_loads(part):
             load.wait()
-        if part + 1 < BLOCKS:
+        rows = slice(part * SOME_ROWS, (part + 1) * SOME_ROWS)
+        grad_a = dot(grads[rows, :], wide[...], 1, 1)
+        normal, inverse = normed(row_hidden[...].astype(F32))
+        grad_gain[...] += jnp.sum(grad_a * normal, axis=0, keepdims=True)
+        each = ROW_PIECES // groups
+        inner = slice(part % each * SOME_ROWS, (part % each + 1) * SOME_ROWS)
+        kept[inner] = (
+            row_mid[...] + norm_back(grad_a * gain_ref[...], normal, inverse)
+        ).astype(BF16)
+        if part + 1 < ROW_PIECES:
             for load in row_loads(part + 1):
                 load.start()
-        slot = part % 2
-        rows = slice(part * SOME_ROWS, (part + 1) * SOME_ROWS)
-        grad_a = dot(grads[rows, :], wide[...], 1, 1)
-        normal, inverse = normed(row_hidden[slot].astype(F32))
-        grad_gain[...] += jnp.sum(grad_a * normal, axis=0, keepdims=True)
-        each = BLOCKS // groups
-        inner = slice(part % each * SOME_ROWS, (part % each + 1) * SOME_ROWS)
-        kept[inner] = (
-            row_mid[slot] + norm_back(grad_a * gain_ref[...], normal, inverse)
-        ).astype(BF16)
         if part % each == each - 1:
             group = part // each
             pick = held_rows(lengths_ref, group, micros, devices)
@@ -1118,7 +1120,7 @@
     pieces = [
         *[functools.partial(attend_piece, i) for i in range(BLOCKS)],
         *[functools.partial(weight_piece, i) for i in range(SHARDS)],
-        *[functools.partial(row_piece, i) for i in range(BLOCKS)],
+        *[functools.partial(row_piece, i) for i in range(ROW_PIECES)],
         gain_piece,
     ]
     count = len(EARLY_CHUNKS)
@@ -1180,9 +1182,9 @@
             pltpu.VMEM((2, PAIRS, BLK, 2 * BLK), BF16),
             pltpu.VMEM((2, BLK, D), BF16),
             pltpu.VMEM((2, ROWS, FEATURES), BF16),
-            pltpu.VMEM((2, FEATURES, 3 * D), BF16),
-            pltpu.VMEM((2, SOME_ROWS, D), BF16),
-            pltpu.VMEM((2, SOME_ROWS, D), F32),
+            pltpu.VMEM((FEATURES, 3 * D), BF16),
+            pltpu.VMEM((SOME_ROWS, D), BF16),
+            pltpu.VMEM((SOME_ROWS, D), F32),
             pltpu.VMEM((ROWS // groups, D), BF16),
             pltpu.VMEM((groups, devices, CHUNK_ROWS, D), BF16),
             pltpu.VMEM((1, D), F32),
@@ -1190,8 +1192,8 @@
             dma((2,)),
             dma((2, 2)),
             dma((2,)),
+            dma,
             dma((2,)),
-            dma((2, 2)),
             dma,
             dma,
             dma((devices,)),
@@ -1227,207 +1229,514 @@
 WAY_XY, WAY_YX, WAY_CORE_XY, WAY_CORE_YX = range(5, 9)
 
 
-def gather_kernel(devices, *refs):
-    shards, refs = refs[:4], refs[4:]
-    gain, sends, refs = refs[0], refs[1:3], refs[3:]
-    fulls, refs = refs[:4], refs[4:]
-    gains, lands, refs = refs[0], refs[1:3], refs[3:]
-    local_sem, way_send, way_recv, gain_send, gain_recv, row_send, row_recv = refs
+GATHER_CHUNKS = (
+    (0, 0, 1536),
+    (0, 1536, 1536),
+    (1, 0, 1024),
+    (2, 0, 768),
+    (3, 0, 512),
+    (3, 512, 512),
+    *[(2, i * 768, 768) for i in range(1, 7)],
+)
+OUT_CHUNK = 2
+FF_CHUNKS = (3, 6, 7, 8, 9, 10, 11)
+AHEAD = 3
+
+
+def gathering(table, shards, fulls, keep_sem, send_sem, recv_sem):
     rep, grp, core, x, y, by_core, by_x, by_y = place()
     by_xy = by_x + by_y - grp
     other = by_core - grp
-    device = rep * SHARDS + grp
-
-    def peer(step):
-        return lax.rem(device + step, devices)
-
-    def mesh_id(index):
-        return (index // SHARDS, lax.rem(index, SHARDS))
-
-    barrier = pltpu.get_barrier_semaphore()
-
-    def greet(step, carry):
-        pl.semaphore_signal(barrier, device_id=mesh_id(peer(step)), device_id_type=MESH)
-        return carry
-
-    lax.fori_loop(1, devices, greet, 0)
-    pl.semaphore_wait(barrier, devices - 1)
-
-    def way(which, tensor):
-        full, width = fulls[tensor], shards[tensor].shape[1]
-        left, right = pl.ds(0, width // 2), pl.ds(width // 2, width // 2)
-        own = shards[tensor]
-        source, slot, landing, part, to = {
-            WAY_X: (own, grp, by_x, None, by_x),
-            WAY_Y: (own, grp, by_y, None, by_y),
-            WAY_CORE: (own, grp, by_core, None, by_core),
-            WAY_CORE_X: (None, by_x, by_x + other, None, by_core),
-            WAY_CORE_Y: (None, by_y, by_y + other, None, by_core),
-            WAY_XY: (None, by_x, by_xy, left, by_y),
-            WAY_YX: (None, by_y, by_xy, right, by_x),
-            WAY_CORE_XY: (None, by_xy, by_xy + other, left, by_core),
-            WAY_CORE_YX: (None, by_xy, by_xy + other, right, by_core),
+
+    def view(chunk, slot, half=None):
+        tensor, start, width = table[chunk]
+        rows = shards[tensor].shape[0]
+        if half is not None:
+            start, width = start + half * (width // 2), width // 2
+        first = pl.multiple_of(slot * rows, rows)
+        return fulls[tensor].at[pl.ds(first, rows), pl.ds(start, width)]
+
+    def own(chunk):
+        tensor, start, width = table[chunk]
+        return shards[tensor].at[:, pl.ds(start, width)]
+
+    def way(chunk, which):
+        slot, landing, half, to = {
+            WAY_X: (grp, by_x, None, by_x),
+            WAY_Y: (grp, by_y, None, by_y),
+            WAY_CORE: (grp, by_core, None, by_core),
+            WAY_CORE_X: (by_x, by_x + other, None, by_core),
+            WAY_CORE_Y: (by_y, by_y + other, None, by_core),
+            WAY_XY: (by_x, by_xy, 0, by_y),
+            WAY_YX: (by_y, by_xy, 1, by_x),
+            WAY_CORE_XY: (by_xy, by_xy + other, 0, by_core),
+            WAY_CORE_YX: (by_xy, by_xy + other, 1, by_core),
         }[which]
-
-        def view(index):
-            return full.at[index] if part is None else full.at[index, :, part]
+        from_own = which in (WAY_X, WAY_Y, WAY_CORE)
 
         def copy(source, target):
             return pltpu.make_async_remote_copy(
                 src_ref=source,
                 dst_ref=target,
-                send_sem=way_send.at[tensor, which],
-                recv_sem=way_recv.at[tensor, which],
+                send_sem=send_sem.at[chunk, which],
+                recv_sem=recv_sem.at[chunk, which],
                 device_id=(rep, to),
                 device_id_type=MESH,
             )
 
-        def start():
-            copy(view(slot) if source is None else source, view(slot)).start()
-
-        def arrive():
-            copy(view(landing), view(landing)).wait_recv()
-
-        def sent():
-            copy(view(slot) if source is None else source, view(slot)).wait_send()
-
-        return start, arrive, sent
-
-    def start(tensor, *ways):
+        source = own(chunk) if from_own else view(chunk, slot, half)
+        here = view(chunk, landing, half)
+        return (
+            lambda: copy(source, view(chunk, slot, half)).start(),
+            lambda: copy(here, here).wait_recv(),
+            lambda: copy(source, view(chunk, slot, half)).wait_send(),
+        )
+
+    def keep(chunk):
+        return pltpu.make_async_copy(own(chunk), view(chunk, grp), keep_sem.at[chunk])
+
+    def start(chunk, *ways):
         for which in ways:
-            way(which, tensor)[0]()
-
-    def arrive(tensor, *ways):
+            way(chunk, which)[0]()
+
+    def arrive(chunk, *ways):
         for which in ways:
-            way(which, tensor)[1]()
+            way(chunk, which)[1]()
+
+    def first(chunk):
+        start(chunk, WAY_X, WAY_Y, WAY_CORE)
+        keep(chunk).start()
+
+    def forward(chunk):
+        arrive(chunk, WAY_X)
+        start(chunk, WAY_XY, WAY_CORE_X)
+        arrive(chunk, WAY_Y)
+        start(chunk, WAY_YX, WAY_CORE_Y)
+
+    def last(chunk):
+        arrive(chunk, WAY_XY)
+        start(chunk, WAY_CORE_XY)
+        arrive(chunk, WAY_YX)
+        start(chunk, WAY_CORE_YX)
+
+    def complete(chunk):
+        keep(chunk).wait()
+        arrive(chunk, WAY_CORE, WAY_CORE_X, WAY_CORE_Y, WAY_CORE_XY, WAY_CORE_YX)
+
+    def sent(chunk):
+        for which in range(9):
+            way(chunk, which)[2]()
+
+    return first, forward, last, complete, sent
+
+
+def forward_kernel(devices, micros, *refs):
+    groups = MICRO // micros
+    lengths_ref, gain_shard, cos_ref, sin_ref, token_send, top_send = refs[:6]
+    w_qkv_ref, w_out_ref, w_in_ref, w_down_ref = refs[6:10]
+    gain_rows, gain_grad, hidden_out, act_out, qkv_out, prob_out = refs[10:16]
+    attn_out, mid_out, layer_out, grad_mid_out, grad_in_out, grad_down_out = refs[16:22]
+    weight_out, grad_o_out, grad_out_out, refs = *refs[22:25], refs[25:]
+    weight, full_out, full_in, full_down, token_land, top_land, gain_land = refs[:7]
+    picks, act_b, act_t, top, total, grad_b = refs[7:13]
+    s_hidden, s_act, s_qkv, s_prob, s_attn, s_mid, s_in, s_down = refs[13:21]
+    raw_in, own_in = refs[21:23]
+    store_sem, gain_sem, gain_send, gain_recv = refs[23:27]
+    row_sems, refs = refs[27:30], refs[30:]
+    shards = (w_qkv_ref, w_out_ref, own_in, w_down_ref)
+    fulls = (weight, full_out, full_in, full_down)
+    first, forward, last, complete, sent = gathering(GATHER_CHUNKS, shards, fulls, *refs)
+    rep, grp = lax.axis_index("rep"), lax.axis_index("grp")
+    chunks = len(GATHER_CHUNKS)
+    slots = devices * CHUNK_ROWS
+
+    def exchange(send, land, group, index):
+        return row_exchange(
+            lambda to: send.at[to, group],
+            lambda slot: land.at[slot, group],
+            *[sem.at[index] for sem in row_sems],
+            devices,
+        )
+
+    token_swaps = [exchange(token_send, token_land, g, g) for g in range(groups)]
+    top_swaps = [exchange(top_send, top_land, g, groups + g) for g in range(groups)]
 
     def gain_copy(step, slot):
-        to = lax.rem(grp + step, SHARDS)
         return pltpu.make_async_remote_copy(
-            src_ref=gain,
-            dst_ref=gains.at[slot],
+            src_ref=gain_shard,
+            dst_ref=gain_land.at[slot],
             send_sem=gain_send.at[step],
             recv_sem=gain_recv.at[step],
-            device_id=(rep, to),
+            device_id=(rep, lax.rem(grp + step, SHARDS)),
             device_id_type=MESH,
         )
 
-    def row_copy(which, step, source, slot, to):
-        return pltpu.make_async_remote_copy(
-            src_ref=sends[which].at[source],
-            dst_ref=lands[which].at[slot],
-            send_sem=row_send.at[which, step],
-            recv_sem=row_recv.at[which, step],
-            device_id=mesh_id(to),
-            device_id_type=MESH,
-        )
-
-    def send_rows(which):
-        def one(step, carry):
-            row_copy(which, step, peer(step), device, peer(step)).start()
+    pending = {}
+
+    def free(name):
+        if name in pending:
+            pending.pop(name).wait()
+
+    def put(name, source, target):
+        index = ("hidden", "act", "qkv", "prob", "attn", "mid", "in", "down", "late", "layer", "far", "o", "w")
+        copy = pltpu.make_async_copy(source, target, store_sem.at[index.index(name)])
+        copy.start()
+        pending[name] = copy
+
+    def tick(step):
+        if step < chunks:
+            forward(step)
+            if step + AHEAD < chunks:
+                first(step + AHEAD)
+        if 0 < step <= chunks:
+            last(step - 1)
+
+    def gain_row(part):
+        table = gain_land[...].astype(F32)
+        return jnp.concatenate([table[s, part : part + 1] for s in range(SHARDS)], axis=1)
+
+    def micro_rows(micro):
+        return slice(micro * CAP, (micro + 1) * CAP)
+
+    def qkv_piece(micro):
+        group, rows = micro // micros, micro_rows(micro)
+        for name in ("hidden", "act", "qkv"):
+            free(name)
+        values = dot(picks[rows, :], token_land[:, group].reshape(slots, D))
+        s_hidden[...] = values.astype(BF16)
+        act = (normed(values)[0] * gain_rows[0:1, :]).astype(BF16)
+        s_act[...] = act
+        for step in range(3 * D // QKV_TILE):
+            lanes = slice(step * QKV_TILE, (step + 1) * QKV_TILE)
+            packed = dot(act, weight[:, lanes])
+            if step < 2 * D // QKV_TILE:
+                split = packed.reshape(CAP // BLK, BLK, QKV_TILE)
+                split = (
+                    split * widen(cos_ref[...])[None]
+                    + turned(split) * widen(sin_ref[...])[None]
+                )
+                packed = split.reshape(CAP, QKV_TILE)
+            s_qkv[:, lanes] = packed.astype(BF16)
+        put("hidden", s_hidden, hidden_out.at[rows])
+        put("act", s_act, act_out.at[rows])
+        put("qkv", s_qkv, qkv_out.at[rows])
+
+    def attend_piece(micro):
+        free("prob")
+        free("attn")
+
+        def one(block, carry):
+            rows = pl.ds(pl.multiple_of(block * BLK, BLK), BLK)
+            lengths = block_lengths(lengths_ref, block, devices)
+            valid = key_mask(lengths[micro : micro + 1])
+            for pair in range(PAIRS):
+                columns = [
+                    slice(part * D + pair * LANES, part * D + (pair + 1) * LANES)
+                    for part in range(3)
+                ]
+                context, prob = attend_pair(*[s_qkv[rows, c] for c in columns], valid)
+                s_attn[rows, columns[0]] = context
+                s_prob[block, pair] = prob
             return carry
 
-        lax.fori_loop(1, devices, one, 0)
-
-    def land_rows(which):
-        def one(step, carry):
-            source = lax.rem(device + devices - step, devices)
-            row_copy(which, step, peer(step), source, peer(step)).wait_recv()
-            row_copy(which, step, peer(step), device, peer(step)).wait_send()
-            return carry
-
-        lax.fori_loop(1, devices, one, 0)
-
-    def local(index, source, target):
-        return pltpu.make_async_copy(source, target, local_sem.at[index])
-
-    keeps = [local(i, shards[i], fulls[i].at[grp]) for i in range(4)]
-    keeps.append(local(4, gain, gains.at[grp]))
-    keeps += [local(5 + i, sends[i].at[device], lands[i].at[device]) for i in range(2)]
-
+        lax.fori_loop(0, SEQ_DEV, one, 0)
+
+    def middle_piece(micro):
+        rows = micro_rows(micro)
+        free("mid")
+        middle = s_hidden[...].astype(F32) + dot(s_attn[...], full_out[...])
+        s_mid[...] = middle
+        total[rows, :] = middle
+        act_b[rows, :] = (normed(middle)[0] * gain_rows[1:2, :]).astype(BF16)
+        put("prob", s_prob, prob_out.at[pl.ds(micro * SEQ_DEV, SEQ_DEV)])
+        put("attn", s_attn, attn_out.at[rows])
+        put("mid", s_mid, mid_out.at[rows])
+
+    def top_piece(micro):
+        group, rows = micro // micros, micro_rows(micro)
+        values = dot(picks[rows, :], top_land[:, group].reshape(slots, D))
+        top[rows, :] = values.astype(BF16)
+
+    def ff_views(step):
+        return (
+            slice(step * 2 * FF_TILE, (step + 1) * 2 * FF_TILE),
+            slice(step * FF_TILE, (step + 1) * FF_TILE),
+            step % 2 * 3 * FF_TILE,
+        )
+
+    def ff_forward(step):
+        both, hidden, base = ff_views(step)
+        gate_up = dot(act_b[...], full_in[:, both])
+        gelu_in, linear = gate_up[:, :FF_TILE], gate_up[:, FF_TILE:]
+        phi = 0.5 * (1.0 + lax.erf(gelu_in * ROOT_HALF))
+        gelu_out = gelu_in * phi
+        slope = phi + gelu_in * (jnp.exp(-0.5 * gelu_in * gelu_in) * INV_ROOT_TWO_PI)
+        act_c = (gelu_out * linear).astype(BF16)
+        weight[:, base : base + FF_TILE] = (linear * slope).astype(BF16)
+        weight[:, base + FF_TILE : base + 2 * FF_TILE] = gelu_out.astype(BF16)
+        weight[:, base + 2 * FF_TILE : base + 3 * FF_TILE] = act_c
+        total[...] += dot(act_c, full_down[hidden, :])
+
+    def ff_backward(step):
+        both, hidden, base = ff_views(step)
+        kept = slice(6 * FF_TILE, 8 * FF_TILE)
+        grad_c = dot(top[...], full_down[hidden, :], 1, 1)
+        for part in range(2):
+            factor = weight[:, base + part * FF_TILE : base + (part + 1) * FF_TILE]
+            start = (6 + part) * FF_TILE
+            weight[:, start : start + FF_TILE] = (grad_c * factor.astype(F32)).astype(BF16)
+        grad_b[...] += dot(weight[:, kept], full_in[:, both], 1, 1)
+        s_in[...] = dot(act_t[...], weight[:, kept]).astype(BF16)
+        act_c = weight[:, base + 2 * FF_TILE : base + 3 * FF_TILE]
+        s_down[...] = dot(act_c, top[...], 0, 0).astype(BF16)
+
+    raw_load = pltpu.make_async_copy(w_in_ref, raw_in, store_sem.at[12])
+    raw_load.start()
+    greet_all(devices)
+    gain_keep = pltpu.make_async_copy(gain_shard, gain_land.at[grp], gain_sem)
+    gain_keep.start()
     for step in range(1, SHARDS):
         gain_copy(step, grp).start()
-    start(3, WAY_X, WAY_Y, WAY_CORE)
-    send_rows(0)
-    for tensor in (2, 1, 0):
-        start(tensor, WAY_X, WAY_Y, WAY_CORE)
-    send_rows(1)
-    for keep in keeps:
-        keep.start()
-    order = (3, 2, 1, 0)
-    for late in range(len(order) + 1):
-        if late < len(order):
-            tensor = order[late]
-            arrive(tensor, WAY_X)
-            start(tensor, WAY_XY, WAY_CORE_X)
-            arrive(tensor, WAY_Y)
-            start(tensor, WAY_YX, WAY_CORE_Y)
-        if late:
-            tensor = order[late - 1]
-            arrive(tensor, WAY_XY)
-            start(tensor, WAY_CORE_XY)
-            arrive(tensor, WAY_YX)
-            start(tensor, WAY_CORE_YX)
-    for tensor in order:
-        arrive(tensor, WAY_CORE, WAY_CORE_X, WAY_CORE_Y, WAY_CORE_XY, WAY_CORE_YX)
+    token_swaps[0][0]()
+    first(0)
+    first(1)
+    for swap in token_swaps[1:]:
+        swap[0]()
+    first(2)
+    raw_load.wait()
+    weave_inside(raw_in, own_in)
+    for group in range(groups):
+        rows = slice(group * micros * CAP, (group + 1) * micros * CAP)
+        picks[rows, :] = held_rows(lengths_ref, group, micros, devices)
+    grad_b[...] = jnp.zeros_like(grad_b)
+    for step in range(3):
+        tick(step)
+    gain_keep.wait()
     for step in range(1, SHARDS):
         gain_copy(step, lax.rem(grp + SHARDS - step, SHARDS)).wait_recv()
         gain_copy(step, grp).wait_send()
-    for which in range(2):
-        land_rows(which)
-    for tensor in order:
-        for which in range(9):
-            way(which, tensor)[2]()
-    for keep in keeps:
-        keep.wait()
-
-
-def gather_all(shards, gain, sends, devices):
+    for part in range(2):
+        gain_rows[part : part + 1, :] = gain_row(part)
+    for swap in token_swaps:
+        swap[1]()
+    for swap in top_swaps:
+        swap[0]()
+    complete(0)
+    complete(1)
+    put("late", weight, weight_out)
+    for micro in range(MICRO):
+        qkv_piece(micro)
+        tick(3 + micro)
+        attend_piece(micro)
+        if micro == 0:
+            complete(OUT_CHUNK)
+        middle_piece(micro)
+    act_t[...] = act_b[...].T
+    for chunk in (4, 5):
+        complete(chunk)
+    free("late")
+    for chunk in range(2):
+        sent(chunk)
+    steps = len(FF_CHUNKS)
+    for step in range(2):
+        if step:
+            tick(7)
+        complete(FF_CHUNKS[step])
+        ff_forward(step)
+    for swap in top_swaps:
+        swap[1]()
+    for micro in range(MICRO):
+        top_piece(micro)
+    for step in range(steps):
+        if step + 2 < steps:
+            tick(8 + step)
+            complete(FF_CHUNKS[step + 2])
+        free("in")
+        free("down")
+        ff_backward(step)
+        if step + 2 < steps:
+            ff_forward(step + 2)
+        both, hidden, _ = ff_views(step)
+        put("in", s_in, grad_in_out.at[:, both])
+        put("down", s_down, grad_down_out.at[hidden])
+    free("attn")
+    free("mid")
+    load_attn = pltpu.make_async_copy(attn_out, act_b, store_sem.at[13])
+    load_mid = pltpu.make_async_copy(mid_out, total, store_sem.at[14])
+    load_attn.start()
+    for group in range(groups):
+        rows = slice(group * micros * CAP, (group + 1) * micros * CAP)
+        values = dot(picks[rows, :], total[rows, :].astype(BF16), 0, 0)
+        token_land[:, group] = values.astype(BF16).reshape(devices, CHUNK_ROWS, D)
+    put("layer", token_land, layer_out)
+    load_mid.start()
+    load_mid.wait()
+    gain_grad[...] = jnp.zeros_like(gain_grad)
+
+    def branch(index, carry):
+        rows = pl.ds(pl.multiple_of(index * ROW_CHUNK, ROW_CHUNK), ROW_CHUNK)
+        normal, inverse = normed(total[rows, :])
+        grad = grad_b[rows, :]
+        gain_grad[...] += jnp.sum(grad * normal, axis=0, keepdims=True)
+        grad_mid = top[rows, :].astype(F32) + norm_back(
+            grad * gain_rows[1:2, :], normal, inverse
+        )
+        total[rows, :] = grad_mid
+        weight[rows, :D] = grad_mid.astype(BF16)
+        return carry
+
+    lax.fori_loop(0, ROWS // ROW_CHUNK, branch, 0)
+    put("far", total, grad_mid_out)
+    weight[:, D : 2 * D] = dot(weight[:, :D], full_out[...], 1, 1).astype(BF16)
+    put("o", weight.at[:, pl.ds(D, D)], grad_o_out)
+    load_attn.wait()
+    weight[:, 2 * D :] = dot(act_b[...], weight[:, :D], 0, 0).astype(BF16)
+    put("w", weight.at[:, pl.ds(2 * D, D)], grad_out_out)
+    for name in list(pending):
+        free(name)
+    for chunk in range(2, chunks):
+        sent(chunk)
+
+
+def forward_all(lengths, gain, tables, sends, shards, devices, micros):
     anywhere = pl.BlockSpec(memory_space=pl.ANY)
-    moved = SHARDS * sum(v.size for v in shards) + sum(v.size for v in sends)
+    inside = pl.BlockSpec(memory_space=pltpu.VMEM)
     dma = pltpu.SemaphoreType.DMA
-    out = [
-        *[jax.ShapeDtypeStruct((SHARDS, *v.shape), v.dtype) for v in (*shards, gain)],
-        *[jax.ShapeDtypeStruct(v.shape, v.dtype) for v in sends],
-    ]
+    groups = MICRO // micros
+    exchanged = sends[0].shape
+    chunks = len(GATHER_CHUNKS)
+    full = [(SHARDS * v.shape[0], v.shape[1]) for v in shards]
+    full[2] = (D, 2 * SHARDS * ff_shard(SHARDS))
+    rows16 = jax.ShapeDtypeStruct((ROWS, D), BF16)
+    rows32 = jax.ShapeDtypeStruct((ROWS, D), F32)
     return pl.pallas_call(
-        functools.partial(gather_kernel, devices),
-        in_specs=[anywhere] * 7,
-        out_specs=[anywhere] * 7,
-        out_shape=out,
+        functools.partial(forward_kernel, devices, micros),
+        in_specs=[inside, anywhere, inside, inside, *[anywhere] * 6],
+        out_specs=[inside, inside, *[anywhere] * 13],
+        out_shape=[
+            jax.ShapeDtypeStruct((2, D), F32),
+            jax.ShapeDtypeStruct((1, D), F32),
+            rows16,
+            rows16,
+            jax.ShapeDtypeStruct((ROWS, 3 * D), BF16),
+            jax.ShapeDtypeStruct((BLOCKS, PAIRS, BLK, 2 * BLK), BF16),
+            rows16,
+            rows32,
+            jax.ShapeDtypeStruct(exchanged, BF16),
+            rows32,
+            jax.ShapeDtypeStruct(full[2], BF16),
+            jax.ShapeDtypeStruct(full[3], BF16),
+            jax.ShapeDtypeStruct(full[0], BF16),
+            rows16,
+            jax.ShapeDtypeStruct((D, D), BF16),
+        ],
         scratch_shapes=[
-            dma((7,)),
-            dma((4, 9)),
-            dma((4, 9)),
+            *[pltpu.VMEM(v, BF16) for v in full],
+            pltpu.VMEM(exchanged, BF16),
+            pltpu.VMEM(exchanged, BF16),
+            pltpu.VMEM((SHARDS, *gain.shape), BF16),
+            pltpu.VMEM((ROWS, devices * CHUNK_ROWS), BF16),
+            pltpu.VMEM((ROWS, D), BF16),
+            pltpu.VMEM((D, ROWS), BF16),
+            pltpu.VMEM((ROWS, D), BF16),
+            pltpu.VMEM((ROWS, D), F32),
+            pltpu.VMEM((ROWS, D), F32),
+            pltpu.VMEM((CAP, D), BF16),
+            pltpu.VMEM((CAP, D), BF16),
+            pltpu.VMEM((CAP, 3 * D), BF16),
+            pltpu.VMEM((SEQ_DEV, PAIRS, BLK, 2 * BLK), BF16),
+            pltpu.VMEM((CAP, D), BF16),
+            pltpu.VMEM((CAP, D), F32),
+            pltpu.VMEM((D, 2 * FF_TILE), BF16),
+            pltpu.VMEM((FF_TILE, D), BF16),
+            pltpu.VMEM(shards[2].shape, BF16),
+            pltpu.VMEM((shards[2].shape[0], full[2][1]), BF16),
+            dma((15,)),
+            dma,
             dma((SHARDS,)),
             dma((SHARDS,)),
-            dma((2, devices)),
-            dma((2, devices)),
-        ],
-        compiler_params=pltpu.CompilerParams(collective_id=0, has_side_effects=True),
-        cost_estimate=cost(0, 16 * moved),
-    )(*shards, gain, *sends)
-
-
-def weave(weight):
-    rows = weight.shape[0]
-    gap = jnp.zeros((rows, FF_PAD - FF), weight.dtype)
-    parts = [jnp.concatenate([weight[:, i * FF : (i + 1) * FF], gap], 1) for i in range(2)]
-    tiles = [
-        parts[half][:, step * FF_TILE : (step + 1) * FF_TILE]
-        for step in range(FF_STEPS)
-        for half in range(2)
-    ]
-    return jnp.concatenate(tiles, axis=1)
-
-
-def unweave(woven):
-    tiles = [
-        woven[:, (2 * step + half) * FF_TILE :][:, : min(FF_TILE, FF - step * FF_TILE)]
-        for half in range(2)
-        for step in range(FF_STEPS)
-    ]
-    return jnp.concatenate(tiles, axis=1)
+            dma((2 * groups,)),
+            dma((2 * groups, devices)),
+            dma((2 * groups, devices)),
+            dma((chunks,)),
+            dma((chunks, 9)),
+            dma((chunks, 9)),
+        ],
+        compiler_params=pltpu.CompilerParams(
+            vmem_limit_bytes=63 * MIB, collective_id=0, has_side_effects=True
+        ),
+        cost_estimate=cost(30 * ROWS * D * FF, 600 * MIB),
+    )(lengths, gain, *tables, *sends, *shards)
+
+
+def ff_shard(group_size):
+    return -(-FF // group_size // CHUNK_ROWS) * CHUNK_ROWS
+
+
+def weave(weight, group_size):
+    each, wide = FF // group_size, ff_shard(group_size)
+    gap = jnp.zeros((weight.shape[0], wide - each), weight.dtype)
+    halves = []
+    for half in range(2):
+        parts = []
+        for shard in range(group_size):
+            first = half * FF + shard * each
+            parts += [weight[:, first : first + each], gap]
+        halves.append(jnp.concatenate(parts, axis=1))
+    steps = group_size * wide // FF_TILE
+    return jnp.concatenate(
+        [
+            halves[half][:, step * FF_TILE : (step + 1) * FF_TILE]
+            for step in range(steps)
+            for half in range(2)
+        ],
+        axis=1,
+    )
+
+
+def weave_block(block):
+    each, wide = FF // SHARDS, ff_shard(SHARDS)
+    sources = []
+    for lane in range(block * 128, (block + 1) * 128):
+        half = lane % (2 * FF_TILE) // FF_TILE
+        unit = lane // (2 * FF_TILE) * FF_TILE + lane % FF_TILE
+        if unit % wide < each:
+            sources.append(half * FF + unit // wide * each + unit % wide)
+    return min(sources) // 128 * 128, -(-(max(sources) + 1) // 128) * 128
+
+
+def weave_inside(raw, woven):
+    each, wide = FF // SHARDS, ff_shard(SHARDS)
+    for block in range(woven.shape[1] // 128):
+        start, end = weave_block(block)
+        first = block * 128
+        half = first % (2 * FF_TILE) // FF_TILE
+        base = first // (2 * FF_TILE) * FF_TILE + first % FF_TILE
+        shape = (end - start, 128)
+        unit = base + lax.broadcasted_iota(jnp.int32, shape, 1)
+        low, turn = base // wide, (base // wide + 1) * wide
+        shard = jnp.where(unit >= turn, low + 1, low)
+        inner = unit - shard * wide
+        source = half * FF + shard * each + inner
+        mine = start + lax.broadcasted_iota(jnp.int32, shape, 0)
+        pick = ((source == mine) & (inner < each)).astype(F32).astype(BF16)
+        woven[:, first : first + 128] = dot(raw[:, start:end], pick).astype(BF16)
+
+
+def unweave(woven, group_size):
+    each, wide = FF // group_size, ff_shard(group_size)
+    steps = group_size * wide // FF_TILE
+    parts = []
+    for half in range(2):
+        row = jnp.concatenate(
+            [
+                woven[:, (2 * step + half) * FF_TILE : (2 * step + half + 1) * FF_TILE]
+                for step in range(steps)
+            ],
+            axis=1,
+        )
+        parts += [row[:, i * wide : i * wide + each] for i in range(group_size)]
+    return jnp.concatenate(parts, axis=1)
 
 
 def body(tokens, cotangent, seq_lengths, w_qkv, w_out, w_in, w_down, attn_gain, mlp_gain):
@@ -1445,32 +1754,50 @@
         seq_lengths, (tokens[:, :, 0], cotangent[:, :, 0]), devices, micros
     )
     gains = jnp.stack([attn_gain, mlp_gain])
-    shards = (w_down, weave(w_in), w_out, w_qkv)
+    pad = ff_shard(group_size) - w_down.shape[0]
+    held = w_in if near else weave(w_in, group_size)
+    shards = (w_qkv, w_out, held, jnp.pad(w_down, ((0, pad), (0, 0))))
+    tables = rotary_tables()
     if near:
         gain = jnp.pad(gains, ((0, CHUNK_ROWS - 2), (0, 0)))
-        *full, gains, token_rows, top_rows = gather_all(shards, gain, sends, devices)
-        full = [v.reshape(-1, v.shape[-1]) for v in full]
-        gains = jnp.swapaxes(gains[:, :2], 0, 1).reshape(2, D)
+        (
+            gains,
+            grad_gain_two,
+            hidden,
+            act_a,
+            qkv,
+            prob,
+            _,
+            _,
+            layer_send,
+            grad_mid,
+            grad_in_w,
+            grad_down_w,
+            full_qkv,
+            grad_o,
+            grad_out_w,
+        ) = forward_all(seq_lengths, gain, tables, sends, shards, devices, micros)
+        gain_one = gains[:1]
     else:
         token_rows, top_rows = (swap(v) for v in sends)
-        full = [lax.all_gather(v, "grp", axis=0, tiled=True) for v in shards]
-        gains = lax.all_gather(gains, "grp", axis=1, tiled=True)
-    full_down, full_in, full_out, full_qkv = full
-    gain_one = gains[:1].astype(F32)
-    gain_two = gains[1:].astype(F32)
-
-    cosine, sine = rotary_tables()
-    hidden, act_a, top = unpack_rows(
-        seq_lengths, token_rows, top_rows, gain_one, devices, micros
-    )
-    qkv = qkv_rows(act_a, full_qkv, cosine, sine)
-    attn_o, prob = attend(qkv, seq_lengths, devices)
-    middle, act_b = middle_rows(attn_o, hidden, full_out, gain_two)
-    layer_rows, grad_b, grad_in_w, grad_down_w = ffn(act_b, top, middle, full_in, full_down)
-    layer_send = repack_rows(seq_lengths, layer_rows, devices, micros)
-    grad_mid, grad_o, grad_out_w, grad_gain_two = branch_back(
-        layer_send, grad_b, middle, top, attn_o, full_out, gain_two
-    )
+        full_qkv, full_out, full_in, full_down = (
+            lax.all_gather(v, "grp", axis=0, tiled=True) for v in shards
+        )
+        gains = lax.all_gather(gains, "grp", axis=1, tiled=True).astype(F32)
+        gain_one, gain_two = gains[:1], gains[1:]
+        hidden, act_a, top = unpack_rows(
+            seq_lengths, token_rows, top_rows, gain_one, devices, micros
+        )
+        qkv = qkv_rows(act_a, full_qkv, *tables)
+        attn_o, prob = attend(qkv, seq_lengths, devices)
+        middle, act_b = middle_rows(attn_o, hidden, full_out, gain_two)
+        layer_rows, grad_b, grad_in_w, grad_down_w = ffn(
+            act_b, top, middle, full_in, full_down
+        )
+        layer_send = repack_rows(seq_lengths, layer_rows, devices, micros)
+        grad_mid, grad_o, grad_out_w, grad_gain_two = branch_back(
+            layer_send, grad_b, middle, top, attn_o, full_out, gain_two
+        )
     if near:
         grad_down, grad_in, grad_out, grad_qkv, gain_sums, layer_back, grad_back = return_all(
             (grad_down_w, grad_in_w, grad_out_w),
@@ -1485,14 +1812,14 @@
             full_qkv,
             gain_one,
             grad_gain_two,
-            (cosine, sine),
+            tables,
             devices,
             micros,
         )
         gain_sums = gain_sums[0].reshape(2, -1)
     else:
         layer_back = swap(layer_send)
-        grad_qkv_rows = attend_back(qkv, grad_o, prob, cosine, sine)
+        grad_qkv_rows = attend_back(qkv, grad_o, prob, *tables)
         grad_qkv_w = qkv_grad(act_a, grad_qkv_rows)
         grad_rows, gain_parts = input_back(
             grad_qkv_rows, full_qkv, hidden, grad_mid, gain_one, grad_gain_two
@@ -1518,8 +1845,8 @@
         gain_sums[1],
         grad_qkv,
         grad_out,
-        unweave(grad_in),
-        grad_down,
+        unweave(grad_in, group_size),
+        grad_down[: w_down.shape[0]],
     )
 
 

time: 514 us -> 460 us (0.89)
  Pallas kernels: 479 us -> 432 us
  local copies, waits for them, and re-layouts: 22.6 us -> 14.1 us
    pallas_call x8 -> x1, Pallas kernels: 282 us -> 230 us  [forward_all(): pl.pallas_call(functools.partial(forward_kernel, devices, micros), in_spe...]
    unnamed x74 -> x22, local copies, waits for them, and re-layouts: 15.2 us -> 6.65 us
where the time goes in v5:
time: 460 us; the launch traced here: 452 us
  Pallas kernels  432 us (94%)
  local copies, waits for them, and re-layouts  14.1 us (3%)
  other arithmetic  5.64 us (1%)
    pallas_call x1, Pallas kernels, forward_all(): pl.pallas_call(functools.partial(forward_kernel, devices, micros), in_spe...  230 us
    pallas_call x1, Pallas kernels, return_all(): pl.pallas_call(functools.partial(return_kernel, devices, micros), in_spec...  192 us

profile of v5, /device:TPU:0, one launch (start us, length us, event | category | flops | bytes accessed | tf_op | source)
XLA Modules:
  0.0 452.2 jit_solution(1666789917895023299)
XLA Ops:
  0.6 1.3 fusion.2.refs_1_
  1.9 2.0 pad.9.refs_9_
  3.9 0.7 copy-done.2
  4.6 1.4 copy-done.4
  6.0 1.4 copy-done.5
  7.4 4.0 shard_map.170
  11.4 1.4 copy-done.6
  12.8 230.5 %shard_map.171 = (f32[2,1024]{1,0:T(2,128)}, f32[1,1024]{1,0:T(1,128)}, bf16[1024,1024]{1,0:T(8,128)(2,1)}, bf16[1024,1024]{1,0:T(8,128)(2,1)}, bf16[1024,3072]{...) custom-call(s32[4,64]{1,0:T(4,128)} %lengths_ref.5, ...), custom_call_target="tpu_custom_call" | custom-call | flops 82543902720 | bytes 629145600 | tf_op jit(solution)/shard_map/pallas_call | solution.py:1612
  243.2 1.3 slice.126.refs_12_
  244.5 192.2 %shard_map.172 = (bf16[336,1024]{1,0:T(8,128)(2,1)}, bf16[128,5376]{1,0:T(8,128)(2,1)}, bf16[128,1024]{1,0:T(8,128)(2,1)}, bf16[128,3072]{1,0:T(8,128)(2,1)}, f3...) custom-call(bf16[2,2,2,336,1024]{4,3,2,1,0:T(8,128)(2,1)} %bitcast.2, ...), custom_call_target="tpu_custom_call" | custom-call | flops 17179869184 | bytes 629145600 | tf_op jit(solution)/shard_map/pallas_call | solution.py:1164
  436.8 0.0 copy-start
  436.8 0.0 copy-done.3
  436.8 0.0 copy-start.1
  436.8 1.7 copy-done.1
  438.5 2.4 shard_map.173
  441.0 2.5 shard_map.174
  443.4 1.3 slice_bitcast_fusion
  444.7 0.8 convert_element_type.15
  445.5 1.2 slice_convert_fusion
  446.8 1.3 convert_element_type.14
  448.1 0.3 fusion.4
  448.3 0.5 pad_maximum_fusion
  448.9 0.5 pad_maximum_fusion.6
  449.3 2.6 concatenate.53
  (14 shorter events, 0.0 us)
Async XLA Ops:
  3.9 0.7 copy-start.2
  4.6 1.4 copy-start.4
  6.0 1.4 copy-start.5
  11.4 1.4 copy-start.6
  244.5 192.2 %copy-start.3 = (s32[4,64]{1,0:T(4,128)S(1)}, s32[4,64]{1,0:T(4,128)}, u32[]{:S(2)}) copy-start(s32[4,64]{1,0:T(4,128)} %lengths_ref.5) | copy-start | bytes 3076
  436.8 4.2 copy-start
  436.8 1.7 copy-start.1
  441.0 3.7 copy-start.10
  441.0 4.6 %copy-start.9 = (bf16[336,1024]{1,0:T(8,128)(2,1)S(1)}, bf16[336,1024]{1,0:T(8,128)(2,1)}, u32[]{:S(2)}) copy-start(bf16[336,1024]{1,0:T(8,128)(2,1)} %get-tuple-element.51) | copy-start | bytes 2064388
  443.4 3.3 copy-start.8
  445.5 2.5 copy-start.7

commit v6 on v5

--- a/solution.py
+++ b/solution.py
@@ -1240,7 +1240,7 @@
 )
 OUT_CHUNK = 2
 FF_CHUNKS = (3, 6, 7, 8, 9, 10, 11)
-AHEAD = 3
+EARLY_FIRSTS = 7
 
 
 def gathering(table, shards, fulls, keep_sem, send_sem, recv_sem):
@@ -1386,8 +1386,8 @@
     def tick(step):
         if step < chunks:
             forward(step)
-            if step + AHEAD < chunks:
-                first(step + AHEAD)
+            if EARLY_FIRSTS <= step + 2 < chunks:
+                first(step + 2)
         if 0 < step <= chunks:
             last(step - 1)
 
@@ -1503,14 +1503,19 @@
     for swap in token_swaps[1:]:
         swap[0]()
     first(2)
-    raw_load.wait()
-    weave_inside(raw_in, own_in)
+    first(4)
+    first(5)
     for group in range(groups):
         rows = slice(group * micros * CAP, (group + 1) * micros * CAP)
         picks[rows, :] = held_rows(lengths_ref, group, micros, devices)
     grad_b[...] = jnp.zeros_like(grad_b)
-    for step in range(3):
-        tick(step)
+    tick(0)
+    tick(1)
+    raw_load.wait()
+    weave_inside(raw_in, own_in)
+    first(3)
+    first(6)
+    tick(2)
     gain_keep.wait()
     for step in range(1, SHARDS):
         gain_copy(step, lax.rem(grp + SHARDS - step, SHARDS)).wait_recv()
@@ -1532,6 +1537,7 @@
             complete(OUT_CHUNK)
         middle_piece(micro)
     act_t[...] = act_b[...].T
+    tick(7)
     for chunk in (4, 5):
         complete(chunk)
     free("late")
@@ -1540,7 +1546,7 @@
     steps = len(FF_CHUNKS)
     for step in range(2):
         if step:
-            tick(7)
+            tick(8)
         complete(FF_CHUNKS[step])
         ff_forward(step)
     for swap in top_swaps:
@@ -1549,7 +1555,7 @@
         top_piece(micro)
     for step in range(steps):
         if step + 2 < steps:
-            tick(8 + step)
+            tick(9 + step)
             complete(FF_CHUNKS[step + 2])
         free("in")
         free("down")

time: 460 us -> 454 us (0.987)
  Pallas kernels: 432 us -> 425 us
    pallas_call x1, Pallas kernels: 230 us -> 226 us  [forward_all(): pl.pallas_call(functools.partial(forward_kernel, devices, micros), in_spe...]
where the time goes in v6:
time: 454 us; the launch traced here: 446 us
  Pallas kernels  425 us (94%)
  local copies, waits for them, and re-layouts  14.1 us (3%)
  other arithmetic  5.64 us (1%)
    pallas_call x1, Pallas kernels, forward_all(): pl.pallas_call(functools.partial(forward_kernel, devices, micros), in_spe...  226 us
    pallas_call x1, Pallas kernels, return_all(): pl.pallas_call(functools.partial(return_kernel, devices, micros), in_spec...  191 us

profile of v6, /device:TPU:0, one launch (start us, length us, event | category | flops | bytes accessed | tf_op | source)
XLA Modules:
  0.0 446.0 jit_solution(2584523238388936684)
XLA Ops:
  0.6 1.3 fusion.2.refs_1_
  1.9 2.0 pad.9.refs_9_
  3.9 0.7 copy-done.2
  4.6 1.4 copy-done.4
  6.0 1.4 copy-done.5
  7.4 4.0 shard_map.170
  11.4 1.4 copy-done.6
  12.8 225.7 %shard_map.171 = (f32[2,1024]{1,0:T(2,128)}, f32[1,1024]{1,0:T(1,128)}, bf16[1024,1024]{1,0:T(8,128)(2,1)}, bf16[1024,1024]{1,0:T(8,128)(2,1)}, bf16[1024,3072]{...) custom-call(s32[4,64]{1,0:T(4,128)} %lengths_ref.5, ...), custom_call_target="tpu_custom_call" | custom-call | flops 82543902720 | bytes 629145600 | tf_op jit(solution)/shard_map/pallas_call | solution.py:1618
  238.5 1.3 slice.126.refs_12_
  239.8 190.8 %shard_map.172 = (bf16[336,1024]{1,0:T(8,128)(2,1)}, bf16[128,5376]{1,0:T(8,128)(2,1)}, bf16[128,1024]{1,0:T(8,128)(2,1)}, bf16[128,3072]{1,0:T(8,128)(2,1)}, f3...) custom-call(bf16[2,2,2,336,1024]{4,3,2,1,0:T(8,128)(2,1)} %bitcast.2, ...), custom_call_target="tpu_custom_call" | custom-call | flops 17179869184 | bytes 629145600 | tf_op jit(solution)/shard_map/pallas_call | solution.py:1164
  430.6 0.0 copy-start
  430.6 0.0 copy-done.3
  430.6 0.0 copy-start.1
  430.6 1.7 copy-done.1
  432.3 2.4 shard_map.173
  434.8 2.5 shard_map.174
  437.2 1.3 slice_bitcast_fusion
  438.5 0.8 convert_element_type.15
  439.4 1.2 slice_convert_fusion
  440.6 1.3 convert_element_type.14
  441.9 0.3 fusion.4
  442.1 0.5 pad_maximum_fusion
  442.7 0.5 pad_maximum_fusion.6
  443.1 2.6 concatenate.53
  (14 shorter events, 0.0 us)
Async XLA Ops:
  3.9 0.7 copy-start.2
  4.6 1.4 copy-start.4
  6.0 1.4 copy-start.5
  11.4 1.4 copy-start.6
  239.8 190.8 %copy-start.3 = (s32[4,64]{1,0:T(4,128)S(1)}, s32[4,64]{1,0:T(4,128)}, u32[]{:S(2)}) copy-start(s32[4,64]{1,0:T(4,128)} %lengths_ref.5) | copy-start | bytes 3076
  430.6 4.2 copy-start
  430.6 1.7 copy-start.1
  434.8 3.7 copy-start.10
  434.8 4.6 %copy-start.9 = (bf16[336,1024]{1,0:T(8,128)(2,1)S(1)}, bf16[336,1024]{1,0:T(8,128)(2,1)}, u32[]{:S(2)}) copy-start(bf16[336,1024]{1,0:T(8,128)(2,1)} %get-tuple-element.51) | copy-start | bytes 2064388
  437.2 3.3 copy-start.8
  439.3 2.5 copy-start.7
